TPU v7x, 512 devices: a whole 4x4x16 slice. The times are simulated.
512 devices in a mesh: row: 4 (over z_lo), col: 16 (over x, z_hi), dp: 8 (over y, core).
Axes of the slice: x: 4, y: 4, z: 16 (z_hi: 4, z_lo: 4; z = z_hi * 4 + z_lo), core: 2. Of those that a mesh axis runs over, the one named last changes fastest.
Arguments:
- activations: bfloat16 [8, 2048, 12288], P('dp', 'row', 'col'), may hold values from -6 to 6
- out_grads: bfloat16 [8, 2048, 6144], P('dp', 'col', 'row'), may hold values from -0.046875 to 0.046875
Outputs:
- weight_grad: bfloat16 [12288, 6144], P(('col', 'dp'), 'row')
All inputs are finite; a program needn't handle non-finite values.
Results may differ from a plain program's by a relative error of at most 0.017.
Values may be sent and summed in bfloat16 or wider, within the bound.
No kernel may reach another device: no remote copies, remote signals or barrier semaphores. Data moves between devices by JAX's collectives and lax.ppermute only.
A program may use at most 64 MiB of HBM per device.

v0:
```python
import jax
import jax.numpy as jnp
from jax import lax
from jax.sharding import PartitionSpec as P


def contract_tokens(left, right):
    return lax.dot_general(
        left, right, (((0,), (0,)), ((), ())), preferred_element_type=jnp.float32
    )


def shards(activations, out_grads):
    inputs = activations[0]
    grads = out_grads[0]
    input_whole = lax.all_gather(inputs, "row", axis=0, tiled=True)
    partial_value = contract_tokens(input_whole, lax.all_gather(grads, "col", axis=0, tiled=True))
    summed = lax.psum_scatter(
        partial_value.astype(jnp.bfloat16).astype(jnp.float32).astype(jnp.bfloat16),
        "dp",
        scatter_dimension=0,
        tiled=True,
    )
    return summed


def solution(mesh):
    in_specs = (P("dp", "row", "col"), P("dp", "col", "row"))
    out_specs = P(("col", "dp"), "row")
    return jax.shard_map(shards, mesh=mesh, in_specs=in_specs, out_specs=out_specs, check_vma=False)
```

profile of v0, /device:TPU:1, one launch (start us, length us, event | category | flops | bytes accessed | tf_op | source)
XLA Modules:
  0.0 319.1 jit_solution(2530678798674223609)
XLA Ops:
  6.5 0.0 all-gather.5.cloned.1.call-start
  6.5 0.7 all-gather.5.cloned.1.call-update
  7.3 0.0 all-gather.7.cloned.1.call-start
  7.3 0.7 all-gather.7.cloned.1.call-update
  8.0 0.0 reduce-scatter.2.cloned.1.call-start
  8.1 78.4 %all-gather.5.cloned.1.call-done = bf16[1,2048,768]{2,1,0:T(8,128)(2,1)} async-done(((bf16[1,512,768]{2,1,0:T(8,128)(2,1)}), bf16[1,2048,768]{2,1,0:T(8,128)(2,1)}) %all-gather.5.cloned.1.call-update) | async-done | bytes 3145744 | tf_op jit(solution)/shard_map/all_gather | solution.py:16
  86.5 180.5 %all-gather.7.cloned.1.call-done = bf16[1,2048,1536]{2,1,0:T(8,128)(2,1)} async-done(((bf16[1,128,1536]{2,1,0:T(8,128)(2,1)}), bf16[1,2048,1536]{2,1,0:T(8,128)(2,1)}) %all-gather.7.cloned.1.call-update) | async-done | bytes 6291472 | tf_op jit(solution)/shard_map/all_gather | solution.py:17
  267.0 9.3 %fusion.2 = bf16[768,1536]{1,0:T(8,128)(2,1)} fusion(bf16[1,2048,1536]{2,1,0:T(8,128)(2,1)} %all-gather.7.cloned.1.call-done, bf16[1,2048,768]{2,1,0:T(8,128)(2,1)} %all-gather.5.cloned.1.call-done), kind=kOutput, calls=%fused_computation.2 | convolution fusion | flops 4833017856 | bytes 11796480 | tf_op jit(solution)/shard_map/dot_general | solution.py:8
  276.3 0.0 reduce-scatter.2.cloned.1.call-update
  276.3 36.3 %reduce-scatter.2.cloned.1.call-done = bf16[96,1536]{1,0:T(8,128)(2,1)} async-done(((bf16[768,1536]{1,0:T(8,128)(2,1)}), bf16[96,1536]{1,0:T(8,128)(2,1)}) %reduce-scatter.2.cloned.1.call-update) | async-done | bytes 294928 | tf_op jit(solution)/shard_map/reduce_scatter | solution.py:18
Async XLA Ops:
  6.5 80.0 %all-gather.5.cloned.1.call-start = ((), (), s32[]{:S(2)}) async-start(), calls=%async_computation.2 | async-start | bytes 3932160 | tf_op jit(solution)/shard_map/all_gather | solution.py:16
  7.3 259.7 %all-gather.7.cloned.1.call-start = ((), (), s32[]{:S(2)}) async-start(), calls=%async_computation.3 | async-start | bytes 6684672 | tf_op jit(solution)/shard_map/all_gather | solution.py:17
  8.0 304.6 %reduce-scatter.2.cloned.1.call-start = ((), (), s32[]{:S(2)}) async-start(), calls=%async_computation.1 | async-start | bytes 2654208 | tf_op jit(solution)/shard_map/reduce_scatter | solution.py:18
Sparse Core Ops, SparseCore 0:
  9.5 76.9 all-gather.4
  89.6 177.3 all-gather.6
  276.4 36.0 reduce-scatter.1
where the time goes:
time: 320 us; the launch traced here: 319 us
  waiting for transfers between devices  297 us (93%)
  between operations  13.1 us (4%)
  matrix products  9.28 us (3%)
    all_gather x1, waiting for transfers between devices, shards(): lax.all_gather(grads, 'col', axis=0, tiled=True)  180 us
    all_gather x1, waiting for transfers between devices, shards(): input_whole = lax.all_gather(inputs, 'row', axis=0, tiled=True)  78.4 us
    reduce_scatter x1, waiting for transfers between devices, shards(): lax.psum_scatter(partial_value.astype(jnp.bfloat16).astype(jnp.float32).a...  36.3 us
    dot_general x1, matrix products, contract_tokens(): lax.dot_general(left, right, (((0,), (0,)), ((), ())), preferred_element_...  9.28 us
  transfers between devices with their start and end apart: 3, of which 3 were waited for; matrix products, arithmetic and copies ran while one was open for 0% of the time, Pallas kernels for 0%

commit v1 on v0

v1 whole, which is shorter than its diff:
```python
import jax
import jax.numpy as jnp
from jax import lax
from jax.experimental import pallas as pl
from jax.experimental.pallas import tpu as pltpu
from jax.sharding import PartitionSpec as P

F32, BF16 = jnp.float32, jnp.bfloat16
TILE = 256


def vmem_spec():
    return pl.BlockSpec(memory_space=pltpu.VMEM)


def smem_spec():
    return pl.BlockSpec(memory_space=pltpu.SMEM)


def any_spec():
    return pl.BlockSpec(memory_space=pl.ANY)


def params(mib):
    return pltpu.CompilerParams(vmem_limit_bytes=mib << 20)


def turn_kernel(where, a_ref, out_ref):
    h = where[2]
    for q in range(4):
        start = pl.multiple_of(lax.rem(h + q, 4) * 128, 128)
        out_ref[:, q * 128 : (q + 1) * 128] = a_ref[pl.ds(start, 128), :].T


def turn(where, a):
    return pl.pallas_call(
        turn_kernel,
        out_shape=jax.ShapeDtypeStruct((a.shape[1], a.shape[0]), BF16),
        in_specs=[smem_spec(), vmem_spec()],
        out_specs=vmem_spec(),
        compiler_params=params(16),
        name="turn",
    )(where, a)


def product_kernel(where, *refs):
    inputs, grads = refs[:6], refs[6:-7]
    other_ref, own_ref, left, right, total, in_sem, grad_sem = refs[-7:]
    line, x, core = where[0], where[1], where[4]
    started = []
    for t in range(4):
        delta = lax.rem(x + t, 4) - line
        place = left.at[:, pl.ds(t * 512, 512)]
        for source, test in zip(inputs, (
            delta == 0, delta == -1, delta == 1, delta == -2, delta == 2, jnp.abs(delta) == 3,
        )):
            @pl.when(test)
            def _():
                pltpu.make_async_copy(source, place, in_sem.at[t]).start()
        started.append(pltpu.make_async_copy(inputs[0], place, in_sem.at[t]))
    at = 0
    for i, source in enumerate(grads):
        copy = pltpu.make_async_copy(source, right.at[pl.ds(at, source.shape[0])], grad_sem.at[i])
        copy.start()
        started.append(copy)
        at += source.shape[0]
    for copy in started:
        copy.wait()

    def step(i, carry):
        columns = pl.ds(pl.multiple_of(i * TILE, TILE), TILE)
        total[:, columns] = jnp.dot(left[...], right[:, columns], preferred_element_type=F32)
        return carry

    lax.fori_loop(0, total.shape[1] // TILE, step, 0)
    for y in range(4):
        mine = pl.multiple_of(y * 192 + core * 96, 32)
        other = pl.multiple_of(y * 192 + (1 - core) * 96, 32)
        other_ref[y] = total[pl.ds(other, 96), :].astype(BF16)
        own_ref[y] = total[pl.ds(mine, 96), :]


def product(where, inputs, grads):
    rows, columns = inputs[0].shape[0], grads[0].shape[1]
    tokens = sum(g.shape[0] for g in grads)
    return pl.pallas_call(
        product_kernel,
        out_shape=[
            jax.ShapeDtypeStruct((4, rows // 8, columns), BF16),
            jax.ShapeDtypeStruct((4, rows // 8, columns), F32),
        ],
        in_specs=[smem_spec()] + [any_spec()] * (len(inputs) + len(grads)),
        out_specs=[vmem_spec(), vmem_spec()],
        scratch_shapes=[
            pltpu.VMEM((rows, tokens), BF16),
            pltpu.VMEM((tokens, columns), BF16),
            pltpu.VMEM((rows, columns), F32),
            pltpu.SemaphoreType.DMA((4,)),
            pltpu.SemaphoreType.DMA((len(grads),)),
        ],
        compiler_params=params(40),
        cost_estimate=pl.CostEstimate(flops=2 * rows * columns * tokens, bytes_accessed=12 << 20, transcendentals=0),
        name="product",
    )(where, *inputs, *grads)


def add_cores_kernel(where, own_ref, got_ref, *outs):
    y = where[3]
    for k in range(4):
        at = lax.rem(y + k, 4)
        outs[k][...] = (own_ref[at] + got_ref[at].astype(F32)).astype(outs[k].dtype)


def add_cores(where, own, got):
    shape = own.shape[1:]
    return pl.pallas_call(
        add_cores_kernel,
        out_shape=[jax.ShapeDtypeStruct(shape, F32)] + [jax.ShapeDtypeStruct(shape, BF16)] * 3,
        in_specs=[smem_spec(), vmem_spec(), vmem_spec()],
        out_specs=[vmem_spec()] * 4,
        compiler_params=params(16),
        name="add_cores",
    )(where, own, got)


def add_chips_kernel(kept_ref, *refs):
    total = kept_ref[...]
    for ref in refs[:-1]:
        total += ref[...].astype(F32)
    refs[-1][...] = total.astype(BF16)


def add_chips(kept, got):
    return pl.pallas_call(
        add_chips_kernel,
        out_shape=jax.ShapeDtypeStruct(kept.shape, BF16),
        in_specs=[vmem_spec()] * (1 + len(got)),
        out_specs=vmem_spec(),
        compiler_params=params(16),
        name="add_chips",
    )(kept, *got)


def along_x(value, step):
    return lax.ppermute(value, "col", [(x * 4 + h, (x + step) % 4 * 4 + h) for x in range(4) for h in range(4)])


def along_z_hi(value, step):
    return lax.ppermute(value, "col", [(x * 4 + h, x * 4 + (h + step) % 4) for x in range(4) for h in range(4)])


def along_row(value, pairs):
    return lax.ppermute(value, "row", pairs)


def along_y(value, step):
    return lax.ppermute(value, "dp", [(y * 2 + c, (y + step) % 4 * 2 + c) for y in range(4) for c in range(2)])


def shards(activations, out_grads):
    line, col, dp = lax.axis_index("row"), lax.axis_index("col"), lax.axis_index("dp")
    where = jnp.stack([line, col // 4, col % 4, dp // 2, dp % 2]).astype(jnp.int32)
    grads = out_grads[0]
    half = grads.shape[0] // 2

    before = along_z_hi(grads, 1)
    after = along_z_hi(grads, -1)
    own = turn(where, activations[0])
    from_low = along_row(own, [(0, 1), (1, 2), (2, 3)])
    from_high = along_row(own, [(3, 2), (2, 1), (1, 0)])
    far_top = along_z_hi(before[:half], 1)
    far_bottom = along_z_hi(after[half:], -1)
    near = jnp.concatenate([after, before])
    far = jnp.concatenate([far_top, far_bottom])
    low_2 = along_row(from_low, [(1, 2), (2, 3)])
    high_2 = along_row(from_high, [(2, 1), (1, 0)])
    ends = along_row(jnp.where(line == 2, low_2, high_2), [(2, 3), (1, 0)])

    pieces = []
    for t in range(4):
        sent = [grads, near, far] if t == 0 else [along_x(v, -t) for v in (grads, near, far)]
        pieces += [sent[0], sent[1][: 2 * half], sent[2], sent[1][2 * half :]]
    other, mine = product(where, [own, from_low, from_high, low_2, high_2, ends], pieces)
    got = lax.ppermute(other, "dp", [(d, d ^ 1) for d in range(8)])
    kept, *sends = add_cores(where, mine, got)
    return add_chips(kept, [along_y(v, k + 1) for k, v in enumerate(sends)])


def solution(mesh):
    in_specs = (P("dp", "row", "col"), P("dp", "col", "row"))
    out_specs = P(("col", "dp"), "row")
    return jax.shard_map(shards, mesh=mesh, in_specs=in_specs, out_specs=out_specs, check_vma=False)
```

time: 320 us -> 212 us (0.66)
  the two profiles are of different devices: /device:TPU:1 before, /device:TPU:73 now
where the time goes in v1:
time: 212 us; the launch traced here: 211 us
  waiting for transfers between devices  111 us (52%)
  starting transfers between devices  80.7 us (38%)
  Pallas kernels  13.1 us (6%)
  local copies, waits for them, and re-layouts  5.72 us (3%)
    ppermute x4, waiting for transfers between devices, along_z_hi(): lax.ppermute(value, 'col', [(x * 4 + h, x * 4 + (h + step) % 4) for x in...  58.3 us
    ppermute x9, starting transfers between devices, along_x(): lax.ppermute(value, 'col', [(x * 4 + h, (x + step) % 4 * 4 + h) for x in...  36.6 us
    ppermute x9, waiting for transfers between devices, along_x(): lax.ppermute(value, 'col', [(x * 4 + h, (x + step) % 4 * 4 + h) for x in...  29.6 us
    ppermute x4, starting transfers between devices, along_z_hi(): lax.ppermute(value, 'col', [(x * 4 + h, x * 4 + (h + step) % 4) for x in...  19.8 us
    ppermute x3, waiting for transfers between devices, along_y(): lax.ppermute(value, 'dp', [(y * 2 + c, (y + step) % 4 * 2 + c) for y in r...  12 us
    pallas_call x1, Pallas kernels, product(): pl.pallas_call(product_kernel, out_shape=[jax.ShapeDtypeStruct((4, rows /...  10.8 us
    ppermute x5, starting transfers between devices, along_row(): return lax.ppermute(value, 'row', pairs)  10.1 us
    ppermute x3, starting transfers between devices, along_y(): lax.ppermute(value, 'dp', [(y * 2 + c, (y + step) % 4 * 2 + c) for y in r...  9.81 us
  transfers between devices with their start and end apart: 22, of which 13 were waited for; matrix products, arithmetic and copies ran while one was open for 2% of the time, Pallas kernels for 0%

profile of v1, /device:TPU:73, one launch (start us, length us, event | category | flops | bytes accessed | tf_op | source)
XLA Modules:
  0.0 211.2 jit_solution(15038164482833317974)
XLA Ops:
  0.0 10.6 %collective-permute-start.5 = (bf16[128,1536]{1,0:T(8,128)(2,1)}, bf16[128,1536]{1,0:T(8,128)(2,1)S(1)}, u32[]{:S(2)}, u32[]{:S(2)}) collective-permute-start(bf16[128,1536]{1,0:T(8,128)(2,1)} %bitcast.8), channel_id=1, source_target_pairs={{0,24},{8,0},{16,8},{24,16},{32,56},{40,32},{48,40},{56,48},{64,88... | collective-permute-start | bytes 1179656 | tf_op jit(solution)/shard_map/ppermute | solution.py:149
  10.7 1.9 collective-permute-start.6
  14.7 2.8 %collective-permute-start.1 = (bf16[768,512]{1,0:T(8,128)(2,1)S(1)}, bf16[768,512]{1,0:T(8,128)(2,1)S(1)}, u32[]{:S(2)}, u32[]{:S(2)}) collective-permute-start(bf16[768,512]{1,0:T(8,128)(2,1)S(1)} %turn.1.refs_0_), channel_id=1, source_target_pairs={{384,256},{256,128},{128,0},{385,257},{257,129},{129,1},{386,258},... | collective-permute-start | bytes 2359304 | tf_op jit(solution)/shard_map/ppermute | solution.py:153
  17.4 2.7 %collective-permute-start = (bf16[768,512]{1,0:T(8,128)(2,1)S(1)}, bf16[768,512]{1,0:T(8,128)(2,1)S(1)}, u32[]{:S(2)}, u32[]{:S(2)}) collective-permute-start(bf16[768,512]{1,0:T(8,128)(2,1)S(1)} %turn.1.refs_0_), channel_id=1, source_target_pairs={{0,128},{128,256},{256,384},{1,129},{129,257},{257,385},{2,130},{1... | collective-permute-start | bytes 2359304 | tf_op jit(solution)/shard_map/ppermute | solution.py:153
  20.1 20.6 %collective-permute-done.5.refs_7_ = bf16[128,1536]{1,0:T(8,128)(2,1)S(1)} collective-permute-done((bf16[128,1536]{1,0:T(8,128)(2,1)}, bf16[128,1536]{1,0:T(8,128)(2,1)S(1)}, u32[]{:S(2)}, u32[]{:S(2)}) %collective-permute-start.5) | collective-permute-done | bytes 393248 | tf_op jit(solution)/shard_map/ppermute | solution.py:149
  41.6 6.1 %collective-permute-done.6.refs_9_ = bf16[128,1536]{1,0:T(8,128)(2,1)S(1)} collective-permute-done((bf16[128,1536]{1,0:T(8,128)(2,1)}, bf16[128,1536]{1,0:T(8,128)(2,1)S(1)}, u32[]{:S(2)}, u32[]{:S(2)}) %collective-permute-start.6) | collective-permute-done | bytes 393248 | tf_op jit(solution)/shard_map/ppermute | solution.py:149
  48.5 3.1 %collective-permute-start.16 = (bf16[256,1536]{1,0:T(8,128)(2,1)}, bf16[256,1536]{1,0:T(8,128)(2,1)}, u32[]{:S(2)}, u32[]{:S(2)}) collective-permute-start(bf16[256,1536]{1,0:T(8,128)(2,1)} %constant_dynamic-update-slice_fusion.2), channel_id=1, source_target_pairs={{0,32},{8,40},{16,48},{24,56},{32,64},{40,72},{48,80},{56,88},{64,... | collective-permute-start | bytes 2359304 | tf_op jit(solution)/shard_map/ppermute | solution.py:145
  52.3 2.2 %collective-permute-start.7 = (bf16[64,1536]{1,0:T(8,128)(2,1)}, bf16[64,1536]{1,0:T(8,128)(2,1)}, u32[]{:S(2)}, u32[]{:S(2)}) collective-permute-start(bf16[64,1536]{1,0:T(8,128)(2,1)} %slice.32), channel_id=1, source_target_pairs={{0,8},{8,16},{16,24},{24,0},{32,40},{40,48},{48,56},{56,32},{64,72... | collective-permute-start | bytes 589832 | tf_op jit(solution)/shard_map/ppermute | solution.py:149
  54.5 3.1 %collective-permute-start.15 = (bf16[128,1536]{1,0:T(8,128)(2,1)S(1)}, bf16[128,1536]{1,0:T(8,128)(2,1)}, u32[]{:S(2)}, u32[]{:S(2)}) collective-permute-start(bf16[128,1536]{1,0:T(8,128)(2,1)S(1)} %bitcast.10), channel_id=1, source_target_pairs={{0,32},{8,40},{16,48},{24,56},{32,64},{40,72},{48,80},{56,88},{64,... | collective-permute-start | bytes 1179656 | tf_op jit(solution)/shard_map/ppermute | solution.py:145
  57.7 28.7 %collective-permute-done.7 = bf16[64,1536]{1,0:T(8,128)(2,1)} collective-permute-done((bf16[64,1536]{1,0:T(8,128)(2,1)}, bf16[64,1536]{1,0:T(8,128)(2,1)}, u32[]{:S(2)}, u32[]{:S(2)}) %collective-permute-start.7) | collective-permute-done | bytes 196640 | tf_op jit(solution)/shard_map/ppermute | solution.py:149
  86.3 5.0 %collective-permute-start.8 = (bf16[64,1536]{1,0:T(8,128)(2,1)S(1)}, bf16[64,1536]{1,0:T(8,128)(2,1)S(1)}, u32[]{:S(2)}, u32[]{:S(2)}) collective-permute-start(bf16[64,1536]{1,0:T(8,128)(2,1)S(1)} %slice.33), channel_id=1, source_target_pairs={{0,24},{8,0},{16,8},{24,16},{32,56},{40,32},{48,40},{56,48},{64,88... | collective-permute-start | bytes 589832 | tf_op jit(solution)/shard_map/ppermute | solution.py:149
  95.6 2.8 %collective-permute-done.8 = bf16[64,1536]{1,0:T(8,128)(2,1)S(1)} collective-permute-done((bf16[64,1536]{1,0:T(8,128)(2,1)S(1)}, bf16[64,1536]{1,0:T(8,128)(2,1)S(1)}, u32[]{:S(2)}, u32[]{:S(2)}) %collective-permute-start.8) | collective-permute-done | bytes 196640 | tf_op jit(solution)/shard_map/ppermute | solution.py:149
  98.4 4.6 %collective-permute-start.13 = (bf16[256,1536]{1,0:T(8,128)(2,1)}, bf16[256,1536]{1,0:T(8,128)(2,1)S(1)}, u32[]{:S(2)}, u32[]{:S(2)}) collective-permute-start(bf16[256,1536]{1,0:T(8,128)(2,1)} %constant_dynamic-update-slice_fusion.2), channel_id=1, source_target_pairs={{0,64},{8,72},{16,80},{24,88},{32,96},{40,104},{48,112},{56,120},{... | collective-permute-start | bytes 2359304 | tf_op jit(solution)/shard_map/ppermute | solution.py:145
  103.1 2.8 %collective-permute-start.10 = (bf16[256,1536]{1,0:T(8,128)(2,1)}, bf16[256,1536]{1,0:T(8,128)(2,1)S(1)}, u32[]{:S(2)}, u32[]{:S(2)}) collective-permute-start(bf16[256,1536]{1,0:T(8,128)(2,1)} %constant_dynamic-update-slice_fusion.2), channel_id=1, source_target_pairs={{0,96},{8,104},{16,112},{24,120},{32,0},{40,8},{48,16},{56,24},{64... | collective-permute-start | bytes 2359304 | tf_op jit(solution)/shard_map/ppermute | solution.py:145
  107.0 8.8 %collective-permute-done.3.refs_4_ = bf16[768,512]{1,0:T(8,128)(2,1)S(1)} collective-permute-done((bf16[768,512]{1,0:T(8,128)(2,1)S(1)}, bf16[768,512]{1,0:T(8,128)(2,1)S(1)}, u32[]{:S(2)}, u32[]{:S(2)}) %collective-permute-start.3) | collective-permute-done | bytes 786464 | tf_op jit(solution)/shard_map/ppermute | solution.py:153
  115.8 4.6 %collective-permute-start.12 = (bf16[128,1536]{1,0:T(8,128)(2,1)S(1)}, bf16[128,1536]{1,0:T(8,128)(2,1)S(1)}, u32[]{:S(2)}, u32[]{:S(2)}) collective-permute-start(bf16[128,1536]{1,0:T(8,128)(2,1)S(1)} %bitcast.11), channel_id=1, source_target_pairs={{0,64},{8,72},{16,80},{24,88},{32,96},{40,104},{48,112},{56,120},{... | collective-permute-start | bytes 1179656 | tf_op jit(solution)/shard_map/ppermute | solution.py:145
  120.5 2.8 %collective-permute-start.9 = (bf16[128,1536]{1,0:T(8,128)(2,1)S(1)}, bf16[128,1536]{1,0:T(8,128)(2,1)S(1)}, u32[]{:S(2)}, u32[]{:S(2)}) collective-permute-start(bf16[128,1536]{1,0:T(8,128)(2,1)S(1)} %bitcast.12), channel_id=1, source_target_pairs={{0,96},{8,104},{16,112},{24,120},{32,0},{40,8},{48,16},{56,24},{64... | collective-permute-start | bytes 1179656 | tf_op jit(solution)/shard_map/ppermute | solution.py:145
  124.8 2.5 %collective-permute-start.17 = (bf16[128,1536]{1,0:T(8,128)(2,1)S(1)}, bf16[128,1536]{1,0:T(8,128)(2,1)S(1)}, u32[]{:S(2)}, u32[]{:S(2)}) collective-permute-start(bf16[128,1536]{1,0:T(8,128)(2,1)S(1)} %constant_dynamic-update-slice_fusion.refs_8_), channel_id=1, source_target_pairs={{0,32},{8,40},{16,48},{24,56},{32,64},{40,72},{48,80},{56,88},{64,... | collective-permute-start | bytes 1179656 | tf_op jit(solution)/shard_map/ppermute | solution.py:145
  127.3 2.1 collective-permute-done.12.refs_14_
  129.4 4.6 %collective-permute-start.14 = (bf16[128,1536]{1,0:T(8,128)(2,1)S(1)}, bf16[128,1536]{1,0:T(8,128)(2,1)S(1)}, u32[]{:S(2)}, u32[]{:S(2)}) collective-permute-start(bf16[128,1536]{1,0:T(8,128)(2,1)S(1)} %constant_dynamic-update-slice_fusion.refs_8_), channel_id=1, source_target_pairs={{0,64},{8,72},{16,80},{24,88},{32,96},{40,104},{48,112},{56,120},{... | collective-permute-start | bytes 1179656 | tf_op jit(solution)/shard_map/ppermute | solution.py:145
  134.0 7.2 %collective-permute-done.10 = bf16[256,1536]{1,0:T(8,128)(2,1)S(1)} collective-permute-done((bf16[256,1536]{1,0:T(8,128)(2,1)}, bf16[256,1536]{1,0:T(8,128)(2,1)S(1)}, u32[]{:S(2)}, u32[]{:S(2)}) %collective-permute-start.10) | collective-permute-done | bytes 786464 | tf_op jit(solution)/shard_map/ppermute | solution.py:145
  141.2 8.4 %collective-permute-start.11 = (bf16[128,1536]{1,0:T(8,128)(2,1)S(1)}, bf16[128,1536]{1,0:T(8,128)(2,1)S(1)}, u32[]{:S(2)}, u32[]{:S(2)}) collective-permute-start(bf16[128,1536]{1,0:T(8,128)(2,1)S(1)} %constant_dynamic-update-slice_fusion.refs_8_), channel_id=1, source_target_pairs={{0,96},{8,104},{16,112},{24,120},{32,0},{40,8},{48,16},{56,24},{64... | collective-permute-start | bytes 1179656 | tf_op jit(solution)/shard_map/ppermute | solution.py:145
  149.7 8.2 %collective-permute-done.9.refs_10_ = bf16[128,1536]{1,0:T(8,128)(2,1)S(1)} collective-permute-done((bf16[128,1536]{1,0:T(8,128)(2,1)S(1)}, bf16[128,1536]{1,0:T(8,128)(2,1)S(1)}, u32[]{:S(2)}, u32[]{:S(2)}) %collective-permute-start.9) | collective-permute-done | bytes 393248 | tf_op jit(solution)/shard_map/ppermute | solution.py:145
  158.0 12.0 %collective-permute-done.11.refs_12_ = bf16[128,1536]{1,0:T(8,128)(2,1)S(1)} collective-permute-done((bf16[128,1536]{1,0:T(8,128)(2,1)S(1)}, bf16[128,1536]{1,0:T(8,128)(2,1)S(1)}, u32[]{:S(2)}, u32[]{:S(2)}) %collective-permute-start.11) | collective-permute-done | bytes 393248 | tf_op jit(solution)/shard_map/ppermute | solution.py:145
  170.0 10.8 %product.1 = (bf16[4,96,1536]{2,1,0:T(8,128)(2,1)S(1)}, f32[4,96,1536]{2,1,0:T(8,128)S(1)}) custom-call(s32[5]{0:T(128)S(1)} %stack.23.where, bf16[768,512]{1,0:T(8,128)(2,1)S(1)} %turn.1.refs_0_, bf16[768,512]{1,0:T(8,128)(2,1)S(1)} %collective-permute-done.refs_1_, bf16[768,512]{1,0:T(8,128)(2,1)S(1)} %collective-permute-done.1.refs_2_, ...), custom_call_target="tpu_custom_call" | custom-call | flops 4831838208 | bytes 12582912 | tf_op jit(solution)/shard_map/product/pallas_call | solution.py:86
  180.8 4.5 %collective-permute-start.18 = (bf16[4,96,1536]{2,1,0:T(8,128)(2,1)S(1)}, bf16[4,96,1536]{2,1,0:T(8,128)(2,1)S(1)}, u32[]{:S(2)}, u32[]{:S(2)}) collective-permute-start(bf16[4,96,1536]{2,1,0:T(8,128)(2,1)S(1)} %get-tuple-element.12), channel_id=1, source_target_pairs={{0,1},{1,0},{2,3},{3,2},{4,5},{5,4},{6,7},{7,6},{8,9},{9,8},{10,11... | collective-permute-start | bytes 3538952 | tf_op jit(solution)/shard_map/ppermute | solution.py:184
  185.3 2.5 %collective-permute-done.18.got_ref = bf16[4,96,1536]{2,1,0:T(8,128)(2,1)S(1)} collective-permute-done((bf16[4,96,1536]{2,1,0:T(8,128)(2,1)S(1)}, bf16[4,96,1536]{2,1,0:T(8,128)(2,1)S(1)}, u32[]{:S(2)}, u32[]{:S(2)}) %collective-permute-start.18) | collective-permute-done | bytes 1179680 | tf_op jit(solution)/shard_map/ppermute | solution.py:184
  188.5 3.2 %collective-permute-start.19 = (bf16[96,1536]{1,0:T(8,128)(2,1)S(1)}, bf16[96,1536]{1,0:T(8,128)(2,1)S(1)}, u32[]{:S(2)}, u32[]{:S(2)}) collective-permute-start(bf16[96,1536]{1,0:T(8,128)(2,1)S(1)} %get-tuple-element.14), channel_id=1, source_target_pairs={{0,2},{1,3},{2,4},{3,5},{4,6},{5,7},{6,0},{7,1},{8,10},{9,11},{10,... | collective-permute-start | bytes 884744 | tf_op jit(solution)/shard_map/ppermute | solution.py:157
  191.7 2.6 %collective-permute-start.20 = (bf16[96,1536]{1,0:T(8,128)(2,1)S(1)}, bf16[96,1536]{1,0:T(8,128)(2,1)S(1)}, u32[]{:S(2)}, u32[]{:S(2)}) collective-permute-start(bf16[96,1536]{1,0:T(8,128)(2,1)S(1)} %get-tuple-element.15), channel_id=1, source_target_pairs={{0,4},{1,5},{2,6},{3,7},{4,0},{5,1},{6,2},{7,3},{8,12},{9,13},{10,... | collective-permute-start | bytes 884744 | tf_op jit(solution)/shard_map/ppermute | solution.py:157
  194.3 4.0 %collective-permute-start.21 = (bf16[96,1536]{1,0:T(8,128)(2,1)S(1)}, bf16[96,1536]{1,0:T(8,128)(2,1)S(1)}, u32[]{:S(2)}, u32[]{:S(2)}) collective-permute-start(bf16[96,1536]{1,0:T(8,128)(2,1)S(1)} %get-tuple-element.16), channel_id=1, source_target_pairs={{0,6},{1,7},{2,0},{3,1},{4,2},{5,3},{6,4},{7,5},{8,14},{9,15},{10,... | collective-permute-start | bytes 884744 | tf_op jit(solution)/shard_map/ppermute | solution.py:157
  198.6 4.4 %collective-permute-done.20.refs_1_ = bf16[96,1536]{1,0:T(8,128)(2,1)S(1)} collective-permute-done((bf16[96,1536]{1,0:T(8,128)(2,1)S(1)}, bf16[96,1536]{1,0:T(8,128)(2,1)S(1)}, u32[]{:S(2)}, u32[]{:S(2)}) %collective-permute-start.20) | collective-permute-done | bytes 294944 | tf_op jit(solution)/shard_map/ppermute | solution.py:157
  203.0 7.3 %collective-permute-done.21.refs_2_ = bf16[96,1536]{1,0:T(8,128)(2,1)S(1)} collective-permute-done((bf16[96,1536]{1,0:T(8,128)(2,1)S(1)}, bf16[96,1536]{1,0:T(8,128)(2,1)S(1)}, u32[]{:S(2)}, u32[]{:S(2)}) %collective-permute-start.21) | collective-permute-done | bytes 294944 | tf_op jit(solution)/shard_map/ppermute | solution.py:157
  (31 shorter events, 13.1 us)
Async XLA Ops:
  0.0 40.8 %collective-permute-start.5 = (bf16[128,1536]{1,0:T(8,128)(2,1)}, bf16[128,1536]{1,0:T(8,128)(2,1)S(1)}, u32[]{:S(2)}, u32[]{:S(2)}) collective-permute-start(bf16[128,1536]{1,0:T(8,128)(2,1)} %bitcast.8), channel_id=1, source_target_pairs={{0,24},{8,0},{16,8},{24,16},{32,56},{40,32},{48,40},{56,48},{64,88... | collective-permute-start | bytes 1179656 | tf_op jit(solution)/shard_map/ppermute | solution.py:149
  10.7 37.1 %collective-permute-start.6 = (bf16[128,1536]{1,0:T(8,128)(2,1)}, bf16[128,1536]{1,0:T(8,128)(2,1)S(1)}, u32[]{:S(2)}, u32[]{:S(2)}) collective-permute-start(bf16[128,1536]{1,0:T(8,128)(2,1)} %bitcast.9), channel_id=1, source_target_pairs={{0,8},{8,16},{16,24},{24,0},{32,40},{40,48},{48,56},{56,32},{64,72... | collective-permute-start | bytes 1179656 | tf_op jit(solution)/shard_map/ppermute | solution.py:149
  12.7 1.1 copy-start
  14.6 39.9 %copy-start.1 = (bf16[1,128,1536]{2,1,0:T(8,128)(2,1)S(1)}, bf16[1,128,1536]{2,1,0:T(8,128)(2,1)}, u32[]{:S(2)}) copy-start(bf16[1,128,1536]{2,1,0:T(8,128)(2,1)} %param.3) | copy-start | bytes 1179652
  14.7 76.7 %collective-permute-start.1 = (bf16[768,512]{1,0:T(8,128)(2,1)S(1)}, bf16[768,512]{1,0:T(8,128)(2,1)S(1)}, u32[]{:S(2)}, u32[]{:S(2)}) collective-permute-start(bf16[768,512]{1,0:T(8,128)(2,1)S(1)} %turn.1.refs_0_), channel_id=1, source_target_pairs={{384,256},{256,128},{128,0},{385,257},{257,129},{129,1},{386,258},... | collective-permute-start | bytes 2359304 | tf_op jit(solution)/shard_map/ppermute | solution.py:153
  17.4 75.2 %collective-permute-start = (bf16[768,512]{1,0:T(8,128)(2,1)S(1)}, bf16[768,512]{1,0:T(8,128)(2,1)S(1)}, u32[]{:S(2)}, u32[]{:S(2)}) collective-permute-start(bf16[768,512]{1,0:T(8,128)(2,1)S(1)} %turn.1.refs_0_), channel_id=1, source_target_pairs={{0,128},{128,256},{256,384},{1,129},{129,257},{257,385},{2,130},{1... | collective-permute-start | bytes 2359304 | tf_op jit(solution)/shard_map/ppermute | solution.py:153
  48.5 54.6 %collective-permute-start.16 = (bf16[256,1536]{1,0:T(8,128)(2,1)}, bf16[256,1536]{1,0:T(8,128)(2,1)}, u32[]{:S(2)}, u32[]{:S(2)}) collective-permute-start(bf16[256,1536]{1,0:T(8,128)(2,1)} %constant_dynamic-update-slice_fusion.2), channel_id=1, source_target_pairs={{0,32},{8,40},{16,48},{24,56},{32,64},{40,72},{48,80},{56,88},{64,... | collective-permute-start | bytes 2359304 | tf_op jit(solution)/shard_map/ppermute | solution.py:145
  52.3 34.1 %collective-permute-start.7 = (bf16[64,1536]{1,0:T(8,128)(2,1)}, bf16[64,1536]{1,0:T(8,128)(2,1)}, u32[]{:S(2)}, u32[]{:S(2)}) collective-permute-start(bf16[64,1536]{1,0:T(8,128)(2,1)} %slice.32), channel_id=1, source_target_pairs={{0,8},{8,16},{16,24},{24,0},{32,40},{40,48},{48,56},{56,32},{64,72... | collective-permute-start | bytes 589832 | tf_op jit(solution)/shard_map/ppermute | solution.py:149
  54.5 70.2 %collective-permute-start.15 = (bf16[128,1536]{1,0:T(8,128)(2,1)S(1)}, bf16[128,1536]{1,0:T(8,128)(2,1)}, u32[]{:S(2)}, u32[]{:S(2)}) collective-permute-start(bf16[128,1536]{1,0:T(8,128)(2,1)S(1)} %bitcast.10), channel_id=1, source_target_pairs={{0,32},{8,40},{16,48},{24,56},{32,64},{40,72},{48,80},{56,88},{64,... | collective-permute-start | bytes 1179656 | tf_op jit(solution)/shard_map/ppermute | solution.py:145
  86.3 12.1 %collective-permute-start.8 = (bf16[64,1536]{1,0:T(8,128)(2,1)S(1)}, bf16[64,1536]{1,0:T(8,128)(2,1)S(1)}, u32[]{:S(2)}, u32[]{:S(2)}) collective-permute-start(bf16[64,1536]{1,0:T(8,128)(2,1)S(1)} %slice.33), channel_id=1, source_target_pairs={{0,24},{8,0},{16,8},{24,16},{32,56},{40,32},{48,40},{56,48},{64,88... | collective-permute-start | bytes 589832 | tf_op jit(solution)/shard_map/ppermute | solution.py:149
  91.3 24.5 %collective-permute-start.3 = (bf16[768,512]{1,0:T(8,128)(2,1)S(1)}, bf16[768,512]{1,0:T(8,128)(2,1)S(1)}, u32[]{:S(2)}, u32[]{:S(2)}) collective-permute-start(bf16[768,512]{1,0:T(8,128)(2,1)S(1)} %collective-permute-done.1.refs_2_), channel_id=1, source_target_pairs={{256,128},{128,0},{257,129},{129,1},{258,130},{130,2},{259,131},{1... | collective-permute-start | bytes 2359304 | tf_op jit(solution)/shard_map/ppermute | solution.py:153
  92.7 27.8 %collective-permute-start.2 = (bf16[768,512]{1,0:T(8,128)(2,1)S(1)}, bf16[768,512]{1,0:T(8,128)(2,1)S(1)}, u32[]{:S(2)}, u32[]{:S(2)}) collective-permute-start(bf16[768,512]{1,0:T(8,128)(2,1)S(1)} %collective-permute-done.refs_1_), channel_id=1, source_target_pairs={{128,256},{256,384},{129,257},{257,385},{130,258},{258,386},{131,2... | collective-permute-start | bytes 2359304 | tf_op jit(solution)/shard_map/ppermute | solution.py:153
  98.4 24.9 %collective-permute-start.13 = (bf16[256,1536]{1,0:T(8,128)(2,1)}, bf16[256,1536]{1,0:T(8,128)(2,1)S(1)}, u32[]{:S(2)}, u32[]{:S(2)}) collective-permute-start(bf16[256,1536]{1,0:T(8,128)(2,1)} %constant_dynamic-update-slice_fusion.2), channel_id=1, source_target_pairs={{0,64},{8,72},{16,80},{24,88},{32,96},{40,104},{48,112},{56,120},{... | collective-permute-start | bytes 2359304 | tf_op jit(solution)/shard_map/ppermute | solution.py:145
  103.1 38.2 %collective-permute-start.10 = (bf16[256,1536]{1,0:T(8,128)(2,1)}, bf16[256,1536]{1,0:T(8,128)(2,1)S(1)}, u32[]{:S(2)}, u32[]{:S(2)}) collective-permute-start(bf16[256,1536]{1,0:T(8,128)(2,1)} %constant_dynamic-update-slice_fusion.2), channel_id=1, source_target_pairs={{0,96},{8,104},{16,112},{24,120},{32,0},{40,8},{48,16},{56,24},{64... | collective-permute-start | bytes 2359304 | tf_op jit(solution)/shard_map/ppermute | solution.py:145
  115.8 13.6 %collective-permute-start.12 = (bf16[128,1536]{1,0:T(8,128)(2,1)S(1)}, bf16[128,1536]{1,0:T(8,128)(2,1)S(1)}, u32[]{:S(2)}, u32[]{:S(2)}) collective-permute-start(bf16[128,1536]{1,0:T(8,128)(2,1)S(1)} %bitcast.11), channel_id=1, source_target_pairs={{0,64},{8,72},{16,80},{24,88},{32,96},{40,104},{48,112},{56,120},{... | collective-permute-start | bytes 1179656 | tf_op jit(solution)/shard_map/ppermute | solution.py:145
  120.5 37.5 %collective-permute-start.9 = (bf16[128,1536]{1,0:T(8,128)(2,1)S(1)}, bf16[128,1536]{1,0:T(8,128)(2,1)S(1)}, u32[]{:S(2)}, u32[]{:S(2)}) collective-permute-start(bf16[128,1536]{1,0:T(8,128)(2,1)S(1)} %bitcast.12), channel_id=1, source_target_pairs={{0,96},{8,104},{16,112},{24,120},{32,0},{40,8},{48,16},{56,24},{64... | collective-permute-start | bytes 1179656 | tf_op jit(solution)/shard_map/ppermute | solution.py:145
  123.4 46.6 %collective-permute-start.4 = (bf16[768,512]{1,0:T(8,128)(2,1)S(1)}, bf16[768,512]{1,0:T(8,128)(2,1)S(1)}, u32[]{:S(2)}, u32[]{:S(2)}) collective-permute-start(bf16[768,512]{1,0:T(8,128)(2,1)S(1)} %broadcast_select_fusion), channel_id=1, source_target_pairs={{256,384},{128,0},{257,385},{129,1},{258,386},{130,2},{259,387},{1... | collective-permute-start | bytes 2359304 | tf_op jit(solution)/shard_map/ppermute | solution.py:153
  124.8 33.2 %collective-permute-start.17 = (bf16[128,1536]{1,0:T(8,128)(2,1)S(1)}, bf16[128,1536]{1,0:T(8,128)(2,1)S(1)}, u32[]{:S(2)}, u32[]{:S(2)}) collective-permute-start(bf16[128,1536]{1,0:T(8,128)(2,1)S(1)} %constant_dynamic-update-slice_fusion.refs_8_), channel_id=1, source_target_pairs={{0,32},{8,40},{16,48},{24,56},{32,64},{40,72},{48,80},{56,88},{64,... | collective-permute-start | bytes 1179656 | tf_op jit(solution)/shard_map/ppermute | solution.py:145
  129.4 28.6 %collective-permute-start.14 = (bf16[128,1536]{1,0:T(8,128)(2,1)S(1)}, bf16[128,1536]{1,0:T(8,128)(2,1)S(1)}, u32[]{:S(2)}, u32[]{:S(2)}) collective-permute-start(bf16[128,1536]{1,0:T(8,128)(2,1)S(1)} %constant_dynamic-update-slice_fusion.refs_8_), channel_id=1, source_target_pairs={{0,64},{8,72},{16,80},{24,88},{32,96},{40,104},{48,112},{56,120},{... | collective-permute-start | bytes 1179656 | tf_op jit(solution)/shard_map/ppermute | solution.py:145
  141.2 28.8 %collective-permute-start.11 = (bf16[128,1536]{1,0:T(8,128)(2,1)S(1)}, bf16[128,1536]{1,0:T(8,128)(2,1)S(1)}, u32[]{:S(2)}, u32[]{:S(2)}) collective-permute-start(bf16[128,1536]{1,0:T(8,128)(2,1)S(1)} %constant_dynamic-update-slice_fusion.refs_8_), channel_id=1, source_target_pairs={{0,96},{8,104},{16,112},{24,120},{32,0},{40,8},{48,16},{56,24},{64... | collective-permute-start | bytes 1179656 | tf_op jit(solution)/shard_map/ppermute | solution.py:145
  180.8 6.9 %collective-permute-start.18 = (bf16[4,96,1536]{2,1,0:T(8,128)(2,1)S(1)}, bf16[4,96,1536]{2,1,0:T(8,128)(2,1)S(1)}, u32[]{:S(2)}, u32[]{:S(2)}) collective-permute-start(bf16[4,96,1536]{2,1,0:T(8,128)(2,1)S(1)} %get-tuple-element.12), channel_id=1, source_target_pairs={{0,1},{1,0},{2,3},{3,2},{4,5},{5,4},{6,7},{7,6},{8,9},{9,8},{10,11... | collective-permute-start | bytes 3538952 | tf_op jit(solution)/shard_map/ppermute | solution.py:184
  188.5 10.1 %collective-permute-start.19 = (bf16[96,1536]{1,0:T(8,128)(2,1)S(1)}, bf16[96,1536]{1,0:T(8,128)(2,1)S(1)}, u32[]{:S(2)}, u32[]{:S(2)}) collective-permute-start(bf16[96,1536]{1,0:T(8,128)(2,1)S(1)} %get-tuple-element.14), channel_id=1, source_target_pairs={{0,2},{1,3},{2,4},{3,5},{4,6},{5,7},{6,0},{7,1},{8,10},{9,11},{10,... | collective-permute-start | bytes 884744 | tf_op jit(solution)/shard_map/ppermute | solution.py:157
  191.7 11.3 %collective-permute-start.20 = (bf16[96,1536]{1,0:T(8,128)(2,1)S(1)}, bf16[96,1536]{1,0:T(8,128)(2,1)S(1)}, u32[]{:S(2)}, u32[]{:S(2)}) collective-permute-start(bf16[96,1536]{1,0:T(8,128)(2,1)S(1)} %get-tuple-element.15), channel_id=1, source_target_pairs={{0,4},{1,5},{2,6},{3,7},{4,0},{5,1},{6,2},{7,3},{8,12},{9,13},{10,... | collective-permute-start | bytes 884744 | tf_op jit(solution)/shard_map/ppermute | solution.py:157
  194.3 16.0 %collective-permute-start.21 = (bf16[96,1536]{1,0:T(8,128)(2,1)S(1)}, bf16[96,1536]{1,0:T(8,128)(2,1)S(1)}, u32[]{:S(2)}, u32[]{:S(2)}) collective-permute-start(bf16[96,1536]{1,0:T(8,128)(2,1)S(1)} %get-tuple-element.16), channel_id=1, source_target_pairs={{0,6},{1,7},{2,0},{3,1},{4,2},{5,3},{6,4},{7,5},{8,14},{9,15},{10,... | collective-permute-start | bytes 884744 | tf_op jit(solution)/shard_map/ppermute | solution.py:157

commit v2 on v0

v2 whole, which is shorter than its diff:
```python
import jax
import jax.numpy as jnp
from jax import lax
from jax.experimental import pallas as pl
from jax.experimental.pallas import tpu as pltpu
from jax.sharding import Mesh, PartitionSpec as P

F32, BF16 = jnp.float32, jnp.bfloat16
TILE = 256
CHUNK = 512


def vmem_spec():
    return pl.BlockSpec(memory_space=pltpu.VMEM)


def smem_spec():
    return pl.BlockSpec(memory_space=pltpu.SMEM)


def hbm_spec():
    return pl.BlockSpec(memory_space=pltpu.HBM)


def params(mib):
    return pltpu.CompilerParams(vmem_limit_bytes=mib << 20)


def turn_kernel(where, a_ref, out_ref):
    h = where[2]
    for q, ahead in enumerate((0, 1, 3, 2)):
        start = pl.multiple_of(lax.rem(h + ahead, 4) * 128, 128)
        out_ref[:, q * 128 : (q + 1) * 128] = a_ref[pl.ds(start, 128), :].T


def turn(where, a):
    return pl.pallas_call(
        turn_kernel,
        out_shape=jax.ShapeDtypeStruct((a.shape[1], a.shape[0]), BF16),
        in_specs=[smem_spec(), vmem_spec()],
        out_specs=vmem_spec(),
        compiler_params=params(16),
        name="turn",
    )(where, a)


def load_grads(x, chunk, refs, place, sems, start):
    own_ref, near_ref, *far_refs = refs
    own_at, near_at, far_at = (place.at[pl.ds(at, size)] for at, size in ((0, 128), (128, 256), (384, 128)))
    if start:
        pltpu.make_async_copy(own_ref.at[chunk], own_at, sems.at[0]).start()
        pltpu.make_async_copy(near_ref.at[chunk], near_at, sems.at[1]).start()
        for t, ref in enumerate(far_refs):
            pl.when(lax.rem(x + t, 4) == chunk)(pltpu.make_async_copy(ref, far_at, sems.at[2]).start)
    else:
        pltpu.make_async_copy(own_ref.at[chunk], own_at, sems.at[0]).wait()
        pltpu.make_async_copy(near_ref.at[chunk], near_at, sems.at[1]).wait()
        pltpu.make_async_copy(far_refs[0], far_at, sems.at[2]).wait()


def early_kernel(where, own_ref, low_ref, high_ref, *refs):
    grads, (total_ref, rest_ref, left, right, in_sem, grad_sem, rest_sem) = refs[:6], refs[6:]
    line = where[0]
    steps = (
        (own_ref, line, None),
        (low_ref, line - 1, line > 0),
        (high_ref, line + 1, line < 3),
    )
    columns = total_ref.shape[1]

    def run(test, body):
        body() if test is None else pl.when(test)(body)

    for i, (source, chunk, test) in enumerate(steps):
        def begin():
            pltpu.make_async_copy(source, left.at[i], in_sem.at[i]).start()
            load_grads(where[1], chunk, grads, right.at[i], grad_sem.at[i], True)
        run(test, begin)
    rest = (lax.rem(line + 2, 4), 3 - line)
    for i, chunk in enumerate(rest):
        load_grads(where[1], chunk, grads, rest_ref.at[i], rest_sem.at[i], True)
    for i, (source, chunk, test) in enumerate(steps):
        def multiply():
            pltpu.make_async_copy(source, left.at[i], in_sem.at[i]).wait()
            load_grads(where[1], chunk, grads, right.at[i], grad_sem.at[i], False)

            def step(j, carry):
                at = pl.ds(pl.multiple_of(j * TILE, TILE), TILE)
                value = jnp.dot(left[i], right[i, :, at], preferred_element_type=F32)
                total_ref[:, at] = value if i == 0 else total_ref[:, at] + value
                return carry

            lax.fori_loop(0, columns // TILE, step, 0)
        run(test, multiply)
    for i, chunk in enumerate(rest):
        load_grads(where[1], chunk, grads, rest_ref.at[i], rest_sem.at[i], False)


def early(where, own, low, high, own_grads, near_grads, far_grads):
    rows, columns = own.shape[0], own_grads.shape[-1]
    return pl.pallas_call(
        early_kernel,
        out_shape=[
            jax.ShapeDtypeStruct((rows, columns), F32),
            jax.ShapeDtypeStruct((2, CHUNK, columns), BF16),
        ],
        in_specs=[smem_spec()] + [hbm_spec()] * 9,
        out_specs=[vmem_spec(), vmem_spec()],
        scratch_shapes=[
            pltpu.VMEM((3, rows, CHUNK), BF16),
            pltpu.VMEM((3, CHUNK, columns), BF16),
            pltpu.SemaphoreType.DMA((3,)),
            pltpu.SemaphoreType.DMA((3, 3)),
            pltpu.SemaphoreType.DMA((2, 3)),
        ],
        compiler_params=params(32),
        cost_estimate=pl.CostEstimate(flops=6 * rows * columns * CHUNK, bytes_accessed=16 << 20, transcendentals=0),
        name="early",
    )(where, own, low, high, own_grads, near_grads, *far_grads)


def late_kernel(where, total_ref, rest_ref, low_ref, high_ref, ends_ref, other_ref, own_ref, left, in_sem):
    line, core = where[0], where[4]
    at_end = jnp.logical_or(line == 0, line == 3)

    @pl.when(line >= 2)
    def _():
        pltpu.make_async_copy(low_ref, left.at[:, pl.ds(0, CHUNK)], in_sem.at[0]).start()

    @pl.when(line < 2)
    def _():
        pltpu.make_async_copy(high_ref, left.at[:, pl.ds(0, CHUNK)], in_sem.at[0]).start()

    end_copy = pltpu.make_async_copy(ends_ref, left.at[:, pl.ds(CHUNK, CHUNK)], in_sem.at[1])
    pl.when(at_end)(end_copy.start)
    pltpu.make_async_copy(low_ref, left.at[:, pl.ds(0, CHUNK)], in_sem.at[0]).wait()
    share = other_ref.shape[1]

    def add(chunks):
        def step(j, carry):
            at = pl.ds(pl.multiple_of(j * TILE, TILE), TILE)
            right = jnp.concatenate([rest_ref[i, :, at] for i in range(chunks)])
            value = total_ref[:, at] + jnp.dot(left[:, : chunks * CHUNK], right, preferred_element_type=F32)
            for y in range(4):
                even = value[2 * y * share : (2 * y + 1) * share]
                odd = value[(2 * y + 1) * share : (2 * y + 2) * share]
                own_ref[y, :, at] = jnp.where(core == 0, even, odd)
                other_ref[y, :, at] = jnp.where(core == 0, odd, even).astype(BF16)
            return carry

        lax.fori_loop(0, total_ref.shape[1] // TILE, step, 0)

    @pl.when(at_end)
    def _():
        end_copy.wait()
        add(2)

    @pl.when(jnp.logical_not(at_end))
    def _():
        add(1)


def late(where, total, rest, low, high, ends):
    rows, columns = total.shape
    return pl.pallas_call(
        late_kernel,
        out_shape=[
            jax.ShapeDtypeStruct((4, rows // 8, columns), BF16),
            jax.ShapeDtypeStruct((4, rows // 8, columns), F32),
        ],
        in_specs=[smem_spec(), vmem_spec(), vmem_spec()] + [hbm_spec()] * 3,
        out_specs=[vmem_spec(), vmem_spec()],
        scratch_shapes=[pltpu.VMEM((rows, 2 * CHUNK), BF16), pltpu.SemaphoreType.DMA((2,))],
        compiler_params=params(32),
        cost_estimate=pl.CostEstimate(flops=4 * rows * columns * CHUNK, bytes_accessed=8 << 20, transcendentals=0),
        name="late",
    )(where, total, rest, low, high, ends)


def add_cores_kernel(where, own_ref, got_ref, *outs):
    y = where[3]
    for k in range(4):
        at = lax.rem(y + k, 4)
        outs[k][...] = (own_ref[at] + got_ref[at].astype(F32)).astype(outs[k].dtype)


def add_cores(where, own, got):
    shape = own.shape[1:]
    return pl.pallas_call(
        add_cores_kernel,
        out_shape=[jax.ShapeDtypeStruct(shape, F32)] + [jax.ShapeDtypeStruct(shape, BF16)] * 3,
        in_specs=[smem_spec(), vmem_spec(), vmem_spec()],
        out_specs=[vmem_spec()] * 4,
        compiler_params=params(16),
        name="add_cores",
    )(where, own, got)


def add_chips_kernel(kept_ref, *refs):
    total = kept_ref[...]
    for ref in refs[:-1]:
        total += ref[...].astype(F32)
    refs[-1][...] = total.astype(BF16)


def add_chips(kept, got):
    return pl.pallas_call(
        add_chips_kernel,
        out_shape=jax.ShapeDtypeStruct(kept.shape, BF16),
        in_specs=[vmem_spec()] * (1 + len(got)),
        out_specs=vmem_spec(),
        compiler_params=params(16),
        name="add_chips",
    )(kept, *got)


def ring(value, axis, step):
    return lax.ppermute(value, axis, [(i, (i + step) % 4) for i in range(4)])


def shards(activations, out_grads):
    where = jnp.stack([lax.axis_index(n) for n in ("row", "x", "z_hi", "y", "core")]).astype(jnp.int32)
    line = where[0]
    grads = out_grads[0]
    half = grads.shape[0] // 2

    own_grads = lax.all_gather(grads, "x", axis=0)
    own = turn(where, activations[0])
    before = ring(grads, "z_hi", 1)
    after = ring(grads, "z_hi", -1)
    near = jnp.concatenate([after, before])
    near, top, bottom, own = lax.optimization_barrier((near, before[:half], after[half:], own))
    near_grads = lax.all_gather(near, "x", axis=0)

    far_top = ring(top, "z_hi", 1)
    far_bottom = ring(bottom, "z_hi", -1)
    low_1 = lax.ppermute(own, "row", [(0, 1), (1, 2), (2, 3)])
    high_1 = lax.ppermute(own, "row", [(3, 2), (2, 1), (1, 0)])
    far = jnp.concatenate([far_top, far_bottom])
    sent_on = jnp.where(line == 1, low_1, high_1)
    far, low_1, high_1, sent_on = lax.optimization_barrier((far, low_1, high_1, sent_on))

    ends = lax.ppermute(sent_on, "row", [(1, 3), (2, 0)])
    low_2 = lax.ppermute(low_1, "row", [(1, 2), (2, 3)])
    high_2 = lax.ppermute(high_1, "row", [(2, 1), (1, 0)])
    far_grads = [ring(far, "x", -t) for t in (2, 1, 3)]
    far_grads = [far, far_grads[1], far_grads[0], far_grads[2]]

    total, rest = early(where, own, low_1, high_1, own_grads, near_grads, far_grads)
    other, mine = late(where, total, rest, low_2, high_2, ends)
    got = lax.ppermute(other, "core", [(0, 1), (1, 0)])
    kept, *sends = add_cores(where, mine, got)
    return add_chips(kept, [ring(v, "y", k + 1) for k, v in enumerate(sends)])


def solution(mesh):
    parts = Mesh(mesh.devices.reshape(4, 4, 4, 4, 2), ("row", "x", "z_hi", "y", "core"))
    in_specs = (P(("y", "core"), "row", ("x", "z_hi")), P(("y", "core"), ("x", "z_hi"), "row"))
    out_specs = P(("x", "z_hi", "y", "core"), "row")
    return jax.shard_map(shards, mesh=parts, in_specs=in_specs, out_specs=out_specs, check_vma=False)
```

time: 320 us -> 190 us (0.59)
  the two profiles are of different devices: /device:TPU:1 before, /device:TPU:43 now
where the time goes in v2:
time: 190 us
  waiting for transfers between devices  88.1 us (46%)
  starting transfers between devices  58.6 us (31%)
  Pallas kernels  16.3 us (9%)
  between operations  13.7 us (7%)
  local copies, waits for them, and re-layouts  11 us (6%)
  other arithmetic  1.99 us (1%)
    ppermute x10, waiting for transfers between devices, ring(): return lax.ppermute(value, axis, [(i, (i + step) % 4) for i in range(4)])  84.9 us
    ppermute x10, starting transfers between devices, ring(): return lax.ppermute(value, axis, [(i, (i + step) % 4) for i in range(4)])  42.1 us
    unnamed x22, local copies, waits for them, and re-layouts  10.9 us
    pallas_call x1, Pallas kernels, early(): pl.pallas_call(early_kernel, out_shape=[jax.ShapeDtypeStruct((rows, colum...  9.95 us
    ppermute x1, starting transfers between devices, shards(): high_1 = lax.ppermute(own, 'row', [(3, 2), (2, 1), (1, 0)])  7.65 us
    pallas_call x1, Pallas kernels, late(): pl.pallas_call(late_kernel, out_shape=[jax.ShapeDtypeStruct((4, rows // 8...  3.94 us
  transfers between devices with their start and end apart: 18, of which 10 were waited for; matrix products, arithmetic and copies ran while one was open for 1% of the time, Pallas kernels for 6%

profile of v2, /device:TPU:43, one launch (start us, length us, event | category | flops | bytes accessed | tf_op | source)
XLA Modules:
  0.0 189.6 jit_solution(15441178011047360464)
XLA Ops:
  7.3 8.8 %collective-permute-start.1 = (bf16[128,1536]{1,0:T(8,128)(2,1)}, bf16[128,1536]{1,0:T(8,128)(2,1)S(1)}, u32[]{:S(2)}, u32[]{:S(2)}) collective-permute-start(bf16[128,1536]{1,0:T(8,128)(2,1)} %bitcast.10), channel_id=1, source_target_pairs={{0,8},{8,16},{16,24},{24,0},{1,9},{9,17},{17,25},{25,1},{2,10},{10... | collective-permute-start | bytes 1179656 | tf_op jit(solution)/shard_map/ppermute | solution.py:218
  16.1 4.7 %collective-permute-start = (bf16[128,1536]{1,0:T(8,128)(2,1)}, bf16[128,1536]{1,0:T(8,128)(2,1)S(1)}, u32[]{:S(2)}, u32[]{:S(2)}) collective-permute-start(bf16[128,1536]{1,0:T(8,128)(2,1)} %bitcast.11), channel_id=1, source_target_pairs={{0,24},{8,0},{16,8},{24,16},{1,25},{9,1},{17,9},{25,17},{2,26},{10... | collective-permute-start | bytes 1179656 | tf_op jit(solution)/shard_map/ppermute | solution.py:218
  20.9 1.1 copy-done
  22.8 20.1 %collective-permute-done.1 = bf16[128,1536]{1,0:T(8,128)(2,1)S(1)} collective-permute-done((bf16[128,1536]{1,0:T(8,128)(2,1)}, bf16[128,1536]{1,0:T(8,128)(2,1)S(1)}, u32[]{:S(2)}, u32[]{:S(2)}) %collective-permute-start.1) | collective-permute-done | bytes 393248 | tf_op jit(solution)/shard_map/ppermute | solution.py:218
  43.0 10.7 %collective-permute-done = bf16[128,1536]{1,0:T(8,128)(2,1)S(1)} collective-permute-done((bf16[128,1536]{1,0:T(8,128)(2,1)}, bf16[128,1536]{1,0:T(8,128)(2,1)S(1)}, u32[]{:S(2)}, u32[]{:S(2)}) %collective-permute-start) | collective-permute-done | bytes 393248 | tf_op jit(solution)/shard_map/ppermute | solution.py:218
  54.7 7.7 %collective-permute-start.5 = (bf16[768,512]{1,0:T(8,128)(2,1)S(1)}, bf16[768,512]{1,0:T(8,128)(2,1)S(1)}, u32[]{:S(2)}, u32[]{:S(2)}) collective-permute-start(bf16[768,512]{1,0:T(8,128)(2,1)S(1)} %turn.1.own_ref), channel_id=1, source_target_pairs={{384,256},{256,128},{128,0},{385,257},{257,129},{129,1},{386,258},... | collective-permute-start | bytes 2359304 | tf_op jit(solution)/shard_map/ppermute | solution.py:238
  62.4 1.9 %collective-permute-start.4 = (bf16[768,512]{1,0:T(8,128)(2,1)S(1)}, bf16[768,512]{1,0:T(8,128)(2,1)S(1)}, u32[]{:S(2)}, u32[]{:S(2)}) collective-permute-start(bf16[768,512]{1,0:T(8,128)(2,1)S(1)} %turn.1.own_ref), channel_id=1, source_target_pairs={{0,128},{128,256},{256,384},{1,129},{129,257},{257,385},{2,130},{1... | collective-permute-start | bytes 2359304 | tf_op jit(solution)/shard_map/ppermute | solution.py:237
  64.3 6.9 %collective-permute-start.2 = (bf16[64,1536]{1,0:T(8,128)(2,1)S(1)}, bf16[64,1536]{1,0:T(8,128)(2,1)S(1)}, u32[]{:S(2)}, u32[]{:S(2)}) collective-permute-start(bf16[64,1536]{1,0:T(8,128)(2,1)S(1)} %slice.8), channel_id=1, source_target_pairs={{0,8},{8,16},{16,24},{24,0},{1,9},{9,17},{17,25},{25,1},{2,10},{10... | collective-permute-start | bytes 589832 | tf_op jit(solution)/shard_map/ppermute | solution.py:218
  71.2 2.3 %collective-permute-start.3 = (bf16[64,1536]{1,0:T(8,128)(2,1)S(1)}, bf16[64,1536]{1,0:T(8,128)(2,1)S(1)}, u32[]{:S(2)}, u32[]{:S(2)}) collective-permute-start(bf16[64,1536]{1,0:T(8,128)(2,1)S(1)} %slice.9), channel_id=1, source_target_pairs={{0,24},{8,0},{16,8},{24,16},{1,25},{9,1},{17,9},{25,17},{2,26},{10... | collective-permute-start | bytes 589832 | tf_op jit(solution)/shard_map/ppermute | solution.py:218
  73.5 26.3 %collective-permute-done.2 = bf16[64,1536]{1,0:T(8,128)(2,1)S(1)} collective-permute-done((bf16[64,1536]{1,0:T(8,128)(2,1)S(1)}, bf16[64,1536]{1,0:T(8,128)(2,1)S(1)}, u32[]{:S(2)}, u32[]{:S(2)}) %collective-permute-start.2) | collective-permute-done | bytes 196640 | tf_op jit(solution)/shard_map/ppermute | solution.py:218
  101.7 3.1 %collective-permute-start.8 = (bf16[128,1536]{1,0:T(8,128)(2,1)S(1)}, bf16[128,1536]{1,0:T(8,128)(2,1)S(1)}, u32[]{:S(2)}, u32[]{:S(2)}) collective-permute-start(bf16[128,1536]{1,0:T(8,128)(2,1)S(1)} %pad_maximum_fusion.1.refs_2_), channel_id=1, source_target_pairs={{0,32},{32,64},{64,96},{96,0},{1,33},{33,65},{65,97},{97,1},{2,34}... | collective-permute-start | bytes 1179656 | tf_op jit(solution)/shard_map/ppermute | solution.py:218
  104.9 1.3 collective-permute-start.11
  106.2 1.3 collective-permute-start.9
  107.5 1.9 %collective-permute-start.10 = (bf16[768,512]{1,0:T(8,128)(2,1)S(1)}, bf16[768,512]{1,0:T(8,128)(2,1)}, u32[]{:S(2)}, u32[]{:S(2)}) collective-permute-start(bf16[768,512]{1,0:T(8,128)(2,1)S(1)} %collective-permute-done.5.high_ref), channel_id=1, source_target_pairs={{256,128},{128,0},{257,129},{129,1},{258,130},{130,2},{259,131},{1... | collective-permute-start | bytes 2359304 | tf_op jit(solution)/shard_map/ppermute | solution.py:245
  109.5 2.7 %collective-permute-start.7 = (bf16[128,1536]{1,0:T(8,128)(2,1)S(1)}, bf16[128,1536]{1,0:T(8,128)(2,1)S(1)}, u32[]{:S(2)}, u32[]{:S(2)}) collective-permute-start(bf16[128,1536]{1,0:T(8,128)(2,1)S(1)} %pad_maximum_fusion.1.refs_2_), channel_id=1, source_target_pairs={{0,64},{32,96},{64,0},{96,32},{1,65},{33,97},{65,1},{97,33},{2,66}... | collective-permute-start | bytes 1179656 | tf_op jit(solution)/shard_map/ppermute | solution.py:218
  113.0 3.8 %collective-permute-start.6 = (bf16[128,1536]{1,0:T(8,128)(2,1)S(1)}, bf16[128,1536]{1,0:T(8,128)(2,1)S(1)}, u32[]{:S(2)}, u32[]{:S(2)}) collective-permute-start(bf16[128,1536]{1,0:T(8,128)(2,1)S(1)} %pad_maximum_fusion.1.refs_2_), channel_id=1, source_target_pairs={{0,96},{32,0},{64,32},{96,64},{1,97},{33,1},{65,33},{97,65},{2,98}... | collective-permute-start | bytes 1179656 | tf_op jit(solution)/shard_map/ppermute | solution.py:218
  116.8 4.5 %collective-permute-done.7.refs_4_ = bf16[128,1536]{1,0:T(8,128)(2,1)S(1)} collective-permute-done((bf16[128,1536]{1,0:T(8,128)(2,1)S(1)}, bf16[128,1536]{1,0:T(8,128)(2,1)S(1)}, u32[]{:S(2)}, u32[]{:S(2)}) %collective-permute-start.7) | collective-permute-done | bytes 393248 | tf_op jit(solution)/shard_map/ppermute | solution.py:218
  122.1 10.4 %collective-permute-done.6.refs_3_ = bf16[128,1536]{1,0:T(8,128)(2,1)S(1)} collective-permute-done((bf16[128,1536]{1,0:T(8,128)(2,1)S(1)}, bf16[128,1536]{1,0:T(8,128)(2,1)S(1)}, u32[]{:S(2)}, u32[]{:S(2)}) %collective-permute-start.6) | collective-permute-done | bytes 393248 | tf_op jit(solution)/shard_map/ppermute | solution.py:218
  133.2 1.1 copy-done.2
  134.4 1.9 copy-done.3
  136.3 1.4 copy-done.4
  137.7 1.0 copy-done.6
  138.7 1.0 copy-done.8
  140.7 9.9 %early.1 = (f32[768,1536]{1,0:T(8,128)S(1)}, bf16[2,512,1536]{2,1,0:T(8,128)(2,1)S(1)}) custom-call(s32[5]{0:T(128)S(1)} %stack.23.where, bf16[768,512]{1,0:T(8,128)(2,1)S(1)} %copy-done.2, bf16[768,512]{1,0:T(8,128)(2,1)S(1)} %collective-permute-done.4.low_ref, bf16[768,512]{1,0:T(8,128)(2,1)S(1)} %collective-permute-done.5.high_ref, ...), custom_call_target="tpu_custom_call" | custom-call | flops 3623878656 | bytes 16777216 | tf_op jit(solution)/shard_map/early/pallas_call | solution.py:101
  150.7 3.9 %late.1 = (bf16[4,96,1536]{2,1,0:T(8,128)(2,1)S(1)}, f32[4,96,1536]{2,1,0:T(8,128)S(1)}) custom-call(s32[5]{0:T(128)S(1)} %stack.23.where, f32[768,1536]{1,0:T(8,128)S(1)} %get-tuple-element.28.total_ref, bf16[2,512,1536]{2,1,0:T(8,128)(2,1)S(1)} %get-tuple-element.29.rest_ref, bf16[768,512]{1,0:T(8,128)(2,1)S(1)} %collective-permute-done.9.low_ref, ...), custom_call_target="tpu_custom_call" | custom-call | flops 2415919104 | bytes 8388608 | tf_op jit(solution)/shard_map/late/pallas_call | solution.py:165
  154.6 2.3 %collective-permute-start.12 = (bf16[4,96,1536]{2,1,0:T(8,128)(2,1)S(1)}, bf16[4,96,1536]{2,1,0:T(8,128)(2,1)S(1)}, u32[]{:S(2)}, u32[]{:S(2)}) collective-permute-start(bf16[4,96,1536]{2,1,0:T(8,128)(2,1)S(1)} %get-tuple-element.32), channel_id=1, source_target_pairs={{0,1},{1,0},{2,3},{3,2},{4,5},{5,4},{6,7},{7,6},{8,9},{9,8},{10,11... | collective-permute-start | bytes 3538952 | tf_op jit(solution)/shard_map/ppermute | solution.py:251
  156.9 2.5 %collective-permute-done.12.got_ref = bf16[4,96,1536]{2,1,0:T(8,128)(2,1)S(1)} collective-permute-done((bf16[4,96,1536]{2,1,0:T(8,128)(2,1)S(1)}, bf16[4,96,1536]{2,1,0:T(8,128)(2,1)S(1)}, u32[]{:S(2)}, u32[]{:S(2)}) %collective-permute-start.12) | collective-permute-done | bytes 1179680 | tf_op jit(solution)/shard_map/ppermute | solution.py:251
  160.1 3.2 %collective-permute-start.13 = (bf16[96,1536]{1,0:T(8,128)(2,1)S(1)}, bf16[96,1536]{1,0:T(8,128)(2,1)S(1)}, u32[]{:S(2)}, u32[]{:S(2)}) collective-permute-start(bf16[96,1536]{1,0:T(8,128)(2,1)S(1)} %get-tuple-element.34), channel_id=1, source_target_pairs={{0,2},{2,4},{4,6},{6,0},{1,3},{3,5},{5,7},{7,1},{8,10},{10,12},{12... | collective-permute-start | bytes 884744 | tf_op jit(solution)/shard_map/ppermute | solution.py:218
  163.3 2.6 %collective-permute-start.14 = (bf16[96,1536]{1,0:T(8,128)(2,1)S(1)}, bf16[96,1536]{1,0:T(8,128)(2,1)S(1)}, u32[]{:S(2)}, u32[]{:S(2)}) collective-permute-start(bf16[96,1536]{1,0:T(8,128)(2,1)S(1)} %get-tuple-element.35), channel_id=1, source_target_pairs={{0,4},{2,6},{4,0},{6,2},{1,5},{3,7},{5,1},{7,3},{8,12},{10,14},{12... | collective-permute-start | bytes 884744 | tf_op jit(solution)/shard_map/ppermute | solution.py:218
  166.0 4.0 %collective-permute-start.15 = (bf16[96,1536]{1,0:T(8,128)(2,1)S(1)}, bf16[96,1536]{1,0:T(8,128)(2,1)S(1)}, u32[]{:S(2)}, u32[]{:S(2)}) collective-permute-start(bf16[96,1536]{1,0:T(8,128)(2,1)S(1)} %get-tuple-element.36), channel_id=1, source_target_pairs={{0,6},{2,0},{4,2},{6,4},{1,7},{3,1},{5,3},{7,5},{8,14},{10,8},{12,... | collective-permute-start | bytes 884744 | tf_op jit(solution)/shard_map/ppermute | solution.py:218
  170.2 4.4 %collective-permute-done.14.refs_1_ = bf16[96,1536]{1,0:T(8,128)(2,1)S(1)} collective-permute-done((bf16[96,1536]{1,0:T(8,128)(2,1)S(1)}, bf16[96,1536]{1,0:T(8,128)(2,1)S(1)}, u32[]{:S(2)}, u32[]{:S(2)}) %collective-permute-start.14) | collective-permute-done | bytes 294944 | tf_op jit(solution)/shard_map/ppermute | solution.py:218
  174.7 7.3 %collective-permute-done.15.refs_2_ = bf16[96,1536]{1,0:T(8,128)(2,1)S(1)} collective-permute-done((bf16[96,1536]{1,0:T(8,128)(2,1)S(1)}, bf16[96,1536]{1,0:T(8,128)(2,1)S(1)}, u32[]{:S(2)}, u32[]{:S(2)}) %collective-permute-start.15) | collective-permute-done | bytes 294944 | tf_op jit(solution)/shard_map/ppermute | solution.py:218
  (39 shorter events, 9.8 us)
Async XLA Ops:
  6.5 126.7 %all-gather.4.cloned.1.call-start = ((), (), s32[]{:S(2)}) async-start(), calls=%async_computation | async-start | bytes 1966080 | tf_op jit(solution)/shard_map/all_gather | solution.py:227
  7.3 126.0 %all-gather.6.cloned.1.call-start = ((), (), s32[]{:S(2)}) async-start(), calls=%async_computation.1 | async-start | bytes 3932160 | tf_op jit(solution)/shard_map/all_gather | solution.py:233
  7.3 35.6 %collective-permute-start.1 = (bf16[128,1536]{1,0:T(8,128)(2,1)}, bf16[128,1536]{1,0:T(8,128)(2,1)S(1)}, u32[]{:S(2)}, u32[]{:S(2)}) collective-permute-start(bf16[128,1536]{1,0:T(8,128)(2,1)} %bitcast.10), channel_id=1, source_target_pairs={{0,8},{8,16},{16,24},{24,0},{1,9},{9,17},{17,25},{25,1},{2,10},{10... | collective-permute-start | bytes 1179656 | tf_op jit(solution)/shard_map/ppermute | solution.py:218
  16.1 37.6 %collective-permute-start = (bf16[128,1536]{1,0:T(8,128)(2,1)}, bf16[128,1536]{1,0:T(8,128)(2,1)S(1)}, u32[]{:S(2)}, u32[]{:S(2)}) collective-permute-start(bf16[128,1536]{1,0:T(8,128)(2,1)} %bitcast.11), channel_id=1, source_target_pairs={{0,24},{8,0},{16,8},{24,16},{1,25},{9,1},{17,9},{25,17},{2,26},{10... | collective-permute-start | bytes 1179656 | tf_op jit(solution)/shard_map/ppermute | solution.py:218
  20.9 1.1 copy-start
  22.8 39.6 %copy-start.1 = (bf16[768,512]{1,0:T(8,128)(2,1)}, bf16[768,512]{1,0:T(8,128)(2,1)S(1)}, u32[]{:S(2)}) copy-start(bf16[768,512]{1,0:T(8,128)(2,1)S(1)} %turn.1.own_ref) | copy-start | bytes 2359300
  54.7 46.0 %collective-permute-start.5 = (bf16[768,512]{1,0:T(8,128)(2,1)S(1)}, bf16[768,512]{1,0:T(8,128)(2,1)S(1)}, u32[]{:S(2)}, u32[]{:S(2)}) collective-permute-start(bf16[768,512]{1,0:T(8,128)(2,1)S(1)} %turn.1.own_ref), channel_id=1, source_target_pairs={{384,256},{256,128},{128,0},{385,257},{257,129},{129,1},{386,258},... | collective-permute-start | bytes 2359304 | tf_op jit(solution)/shard_map/ppermute | solution.py:238
  62.4 38.4 %collective-permute-start.4 = (bf16[768,512]{1,0:T(8,128)(2,1)S(1)}, bf16[768,512]{1,0:T(8,128)(2,1)S(1)}, u32[]{:S(2)}, u32[]{:S(2)}) collective-permute-start(bf16[768,512]{1,0:T(8,128)(2,1)S(1)} %turn.1.own_ref), channel_id=1, source_target_pairs={{0,128},{128,256},{256,384},{1,129},{129,257},{257,385},{2,130},{1... | collective-permute-start | bytes 2359304 | tf_op jit(solution)/shard_map/ppermute | solution.py:237
  64.3 35.5 %collective-permute-start.2 = (bf16[64,1536]{1,0:T(8,128)(2,1)S(1)}, bf16[64,1536]{1,0:T(8,128)(2,1)S(1)}, u32[]{:S(2)}, u32[]{:S(2)}) collective-permute-start(bf16[64,1536]{1,0:T(8,128)(2,1)S(1)} %slice.8), channel_id=1, source_target_pairs={{0,8},{8,16},{16,24},{24,0},{1,9},{9,17},{17,25},{25,1},{2,10},{10... | collective-permute-start | bytes 589832 | tf_op jit(solution)/shard_map/ppermute | solution.py:218
  71.2 29.5 %collective-permute-start.3 = (bf16[64,1536]{1,0:T(8,128)(2,1)S(1)}, bf16[64,1536]{1,0:T(8,128)(2,1)S(1)}, u32[]{:S(2)}, u32[]{:S(2)}) collective-permute-start(bf16[64,1536]{1,0:T(8,128)(2,1)S(1)} %slice.9), channel_id=1, source_target_pairs={{0,24},{8,0},{16,8},{24,16},{1,25},{9,1},{17,9},{25,17},{2,26},{10... | collective-permute-start | bytes 589832 | tf_op jit(solution)/shard_map/ppermute | solution.py:218
  101.7 10.5 %collective-permute-start.8 = (bf16[128,1536]{1,0:T(8,128)(2,1)S(1)}, bf16[128,1536]{1,0:T(8,128)(2,1)S(1)}, u32[]{:S(2)}, u32[]{:S(2)}) collective-permute-start(bf16[128,1536]{1,0:T(8,128)(2,1)S(1)} %pad_maximum_fusion.1.refs_2_), channel_id=1, source_target_pairs={{0,32},{32,64},{64,96},{96,0},{1,33},{33,65},{65,97},{97,1},{2,34}... | collective-permute-start | bytes 1179656 | tf_op jit(solution)/shard_map/ppermute | solution.py:218
  104.9 45.8 %collective-permute-start.11 = (bf16[768,512]{1,0:T(8,128)(2,1)}, bf16[768,512]{1,0:T(8,128)(2,1)S(1)}, u32[]{:S(2)}, u32[]{:S(2)}) collective-permute-start(bf16[768,512]{1,0:T(8,128)(2,1)} %broadcast_select_fusion), channel_id=1, source_target_pairs={{128,384},{256,0},{129,385},{257,1},{130,386},{258,2},{131,387},{2... | collective-permute-start | bytes 2359304 | tf_op jit(solution)/shard_map/ppermute | solution.py:243
  106.2 44.4 %collective-permute-start.9 = (bf16[768,512]{1,0:T(8,128)(2,1)S(1)}, bf16[768,512]{1,0:T(8,128)(2,1)S(1)}, u32[]{:S(2)}, u32[]{:S(2)}) collective-permute-start(bf16[768,512]{1,0:T(8,128)(2,1)S(1)} %collective-permute-done.4.low_ref), channel_id=1, source_target_pairs={{128,256},{256,384},{129,257},{257,385},{130,258},{258,386},{131,2... | collective-permute-start | bytes 2359304 | tf_op jit(solution)/shard_map/ppermute | solution.py:244
  107.5 43.1 %collective-permute-start.10 = (bf16[768,512]{1,0:T(8,128)(2,1)S(1)}, bf16[768,512]{1,0:T(8,128)(2,1)}, u32[]{:S(2)}, u32[]{:S(2)}) collective-permute-start(bf16[768,512]{1,0:T(8,128)(2,1)S(1)} %collective-permute-done.5.high_ref), channel_id=1, source_target_pairs={{256,128},{128,0},{257,129},{129,1},{258,130},{130,2},{259,131},{1... | collective-permute-start | bytes 2359304 | tf_op jit(solution)/shard_map/ppermute | solution.py:245
  109.5 11.8 %collective-permute-start.7 = (bf16[128,1536]{1,0:T(8,128)(2,1)S(1)}, bf16[128,1536]{1,0:T(8,128)(2,1)S(1)}, u32[]{:S(2)}, u32[]{:S(2)}) collective-permute-start(bf16[128,1536]{1,0:T(8,128)(2,1)S(1)} %pad_maximum_fusion.1.refs_2_), channel_id=1, source_target_pairs={{0,64},{32,96},{64,0},{96,32},{1,65},{33,97},{65,1},{97,33},{2,66}... | collective-permute-start | bytes 1179656 | tf_op jit(solution)/shard_map/ppermute | solution.py:218
  112.3 0.8 copy-start.5
  113.0 19.4 %collective-permute-start.6 = (bf16[128,1536]{1,0:T(8,128)(2,1)S(1)}, bf16[128,1536]{1,0:T(8,128)(2,1)S(1)}, u32[]{:S(2)}, u32[]{:S(2)}) collective-permute-start(bf16[128,1536]{1,0:T(8,128)(2,1)S(1)} %pad_maximum_fusion.1.refs_2_), channel_id=1, source_target_pairs={{0,96},{32,0},{64,32},{96,64},{1,97},{33,1},{65,33},{97,65},{2,98}... | collective-permute-start | bytes 1179656 | tf_op jit(solution)/shard_map/ppermute | solution.py:218
  121.3 0.8 copy-start.7
  132.4 0.8 copy-start.9
  133.2 1.1 copy-start.2
  134.4 1.9 copy-start.3
  136.3 1.4 copy-start.4
  137.7 1.0 copy-start.6
  138.7 1.0 copy-start.8
  139.7 1.0 copy-start.10
  154.6 4.8 %collective-permute-start.12 = (bf16[4,96,1536]{2,1,0:T(8,128)(2,1)S(1)}, bf16[4,96,1536]{2,1,0:T(8,128)(2,1)S(1)}, u32[]{:S(2)}, u32[]{:S(2)}) collective-permute-start(bf16[4,96,1536]{2,1,0:T(8,128)(2,1)S(1)} %get-tuple-element.32), channel_id=1, source_target_pairs={{0,1},{1,0},{2,3},{3,2},{4,5},{5,4},{6,7},{7,6},{8,9},{9,8},{10,11... | collective-permute-start | bytes 3538952 | tf_op jit(solution)/shard_map/ppermute | solution.py:251
  160.1 10.1 %collective-permute-start.13 = (bf16[96,1536]{1,0:T(8,128)(2,1)S(1)}, bf16[96,1536]{1,0:T(8,128)(2,1)S(1)}, u32[]{:S(2)}, u32[]{:S(2)}) collective-permute-start(bf16[96,1536]{1,0:T(8,128)(2,1)S(1)} %get-tuple-element.34), channel_id=1, source_target_pairs={{0,2},{2,4},{4,6},{6,0},{1,3},{3,5},{5,7},{7,1},{8,10},{10,12},{12... | collective-permute-start | bytes 884744 | tf_op jit(solution)/shard_map/ppermute | solution.py:218
  163.3 11.3 %collective-permute-start.14 = (bf16[96,1536]{1,0:T(8,128)(2,1)S(1)}, bf16[96,1536]{1,0:T(8,128)(2,1)S(1)}, u32[]{:S(2)}, u32[]{:S(2)}) collective-permute-start(bf16[96,1536]{1,0:T(8,128)(2,1)S(1)} %get-tuple-element.35), channel_id=1, source_target_pairs={{0,4},{2,6},{4,0},{6,2},{1,5},{3,7},{5,1},{7,3},{8,12},{10,14},{12... | collective-permute-start | bytes 884744 | tf_op jit(solution)/shard_map/ppermute | solution.py:218
  166.0 16.0 %collective-permute-start.15 = (bf16[96,1536]{1,0:T(8,128)(2,1)S(1)}, bf16[96,1536]{1,0:T(8,128)(2,1)S(1)}, u32[]{:S(2)}, u32[]{:S(2)}) collective-permute-start(bf16[96,1536]{1,0:T(8,128)(2,1)S(1)} %get-tuple-element.36), channel_id=1, source_target_pairs={{0,6},{2,0},{4,2},{6,4},{1,7},{3,1},{5,3},{7,5},{8,14},{10,8},{12,... | collective-permute-start | bytes 884744 | tf_op jit(solution)/shard_map/ppermute | solution.py:218
Sparse Core Ops, SparseCore 0:
  9.5 37.1 all-gather.3
  54.8 50.3 all-gather.5

commit v3 on v0

v3 whole, which is shorter than its diff:
```python
import jax
import jax.numpy as jnp
from jax import lax
from jax.experimental import pallas as pl
from jax.experimental.pallas import tpu as pltpu
from jax.sharding import Mesh, PartitionSpec as P

F32, BF16 = jnp.float32, jnp.bfloat16
TILE = 512
CHUNK = 512


def vmem_spec():
    return pl.BlockSpec(memory_space=pltpu.VMEM)


def smem_spec():
    return pl.BlockSpec(memory_space=pltpu.SMEM)


def any_spec():
    return pl.BlockSpec(memory_space=pl.ANY)


def params(mib):
    return pltpu.CompilerParams(vmem_limit_bytes=mib << 20)


def turn_kernel(where, a_ref, out_ref, turned):
    h, core = where[2], where[4]
    share = out_ref.shape[0] // 8
    for q, ahead in enumerate((0, 1, 3, 2)):
        start = pl.multiple_of(lax.rem(h + ahead, 4) * 128, 128)
        turned[:, q * 128 : (q + 1) * 128] = a_ref[pl.ds(start, 128), :].T
    for y in range(4):
        for i, keeper in enumerate((1 - core, core)):
            at = pl.multiple_of((2 * y + keeper) * share, 32)
            out_ref[(4 * i + y) * share : (4 * i + y + 1) * share, :] = turned[pl.ds(at, share), :]


def turn(where, a):
    shape = (a.shape[1], a.shape[0])
    return pl.pallas_call(
        turn_kernel,
        out_shape=jax.ShapeDtypeStruct(shape, BF16),
        in_specs=[smem_spec(), vmem_spec()],
        out_specs=vmem_spec(),
        scratch_shapes=[pltpu.VMEM(shape, BF16)],
        compiler_params=params(16),
        name="turn",
    )(where, a)


def stage_kernel(*refs):
    pieces, (out_ref, sems) = refs[:-2], refs[-2:]
    at, copies = 0, []
    for i, ref in enumerate(pieces):
        copies.append(pltpu.make_async_copy(ref, out_ref.at[pl.ds(at, ref.shape[0])], sems.at[i]))
        at += ref.shape[0]
    for copy in copies:
        copy.start()
    for copy in copies:
        copy.wait()


def stage(pieces):
    tokens = sum(p.shape[0] for p in pieces)
    return pl.pallas_call(
        stage_kernel,
        out_shape=jax.ShapeDtypeStruct((tokens, pieces[0].shape[1]), BF16),
        in_specs=[any_spec()] * len(pieces),
        out_specs=vmem_spec(),
        scratch_shapes=[pltpu.SemaphoreType.DMA((len(pieces),))],
        compiler_params=params(54),
        cost_estimate=pl.CostEstimate(flops=0, bytes_accessed=12 << 20, transcendentals=0),
        name="stage",
    )(*pieces)


def product_kernel(where, a_ref, right_ref, other_ref, own_ref, left, sems):
    copies = []
    for t in range(4):
        chunk = lax.rem(where[1] + t, 4)
        copies.append(pltpu.make_async_copy(a_ref.at[chunk], left.at[:, pl.ds(t * CHUNK, CHUNK)], sems.at[t]))
    for copy in copies:
        copy.start()
    for copy in copies:
        copy.wait()
    share = other_ref.shape[1]

    def step(j, carry):
        at = pl.ds(pl.multiple_of(j * TILE, TILE), TILE)
        value = jnp.dot(left[...], right_ref[:, at], preferred_element_type=F32)
        for y in range(4):
            other_ref[y, :, at] = value[y * share : (y + 1) * share].astype(BF16)
            own_ref[y, :, at] = value[(4 + y) * share : (5 + y) * share]
        return carry

    lax.fori_loop(0, right_ref.shape[1] // TILE, step, 0)


def product(where, inputs, right):
    rows, (tokens, columns) = inputs.shape[1], right.shape
    return pl.pallas_call(
        product_kernel,
        out_shape=[
            jax.ShapeDtypeStruct((4, rows // 8, columns), BF16),
            jax.ShapeDtypeStruct((4, rows // 8, columns), F32),
        ],
        in_specs=[smem_spec(), any_spec(), vmem_spec()],
        out_specs=[vmem_spec(), vmem_spec()],
        scratch_shapes=[pltpu.VMEM((rows, tokens), BF16), pltpu.SemaphoreType.DMA((4,))],
        compiler_params=params(50),
        cost_estimate=pl.CostEstimate(flops=2 * rows * columns * tokens, bytes_accessed=10 << 20, transcendentals=0),
        name="product",
    )(where, inputs, right)


def add_cores_kernel(where, own_ref, got_ref, *outs):
    y = where[3]
    for k in range(4):
        at = lax.rem(y + k, 4)
        outs[k][...] = (own_ref[at] + got_ref[at].astype(F32)).astype(outs[k].dtype)


def add_cores(where, own, got):
    shape = own.shape[1:]
    return pl.pallas_call(
        add_cores_kernel,
        out_shape=[jax.ShapeDtypeStruct(shape, F32)] + [jax.ShapeDtypeStruct(shape, BF16)] * 3,
        in_specs=[smem_spec(), vmem_spec(), vmem_spec()],
        out_specs=[vmem_spec()] * 4,
        compiler_params=params(16),
        name="add_cores",
    )(where, own, got)


def add_chips_kernel(kept_ref, *refs):
    total = kept_ref[...]
    for ref in refs[:-1]:
        total += ref[...].astype(F32)
    refs[-1][...] = total.astype(BF16)


def add_chips(kept, got):
    return pl.pallas_call(
        add_chips_kernel,
        out_shape=jax.ShapeDtypeStruct(kept.shape, BF16),
        in_specs=[vmem_spec()] * (1 + len(got)),
        out_specs=vmem_spec(),
        compiler_params=params(16),
        name="add_chips",
    )(kept, *got)


def ring(value, axis, step):
    return lax.ppermute(value, axis, [(i, (i + step) % 4) for i in range(4)])


def shards(activations, out_grads):
    where = jnp.stack([lax.axis_index(n) for n in ("row", "x", "z_hi", "y", "core")]).astype(jnp.int32)
    grads = out_grads[0]
    half = grads.shape[0] // 2

    inputs = lax.all_gather(turn(where, activations[0]), "row", axis=0)

    before = ring(grads, "z_hi", 1)
    after = ring(grads, "z_hi", -1)
    owns = [ring(grads, "x", -t) for t in (1, 2, 3)]
    near = jnp.concatenate([after, before])
    near, top, bottom, *owns = lax.optimization_barrier((near, before[:half], after[half:], *owns))

    far_top = ring(top, "z_hi", 1)
    far_bottom = ring(bottom, "z_hi", -1)
    nears = [ring(near, "x", -t) for t in (1, 2, 3)]
    far_top, far_bottom, *nears = lax.optimization_barrier((far_top, far_bottom, *nears))

    far = jnp.concatenate([far_top, far_bottom])
    fars = [ring(far, "x", -t) for t in (1, 2, 3)]

    right = stage([grads, near, far] + [p for group in zip(owns, nears, fars) for p in group])
    other, mine = product(where, inputs, right)
    got = lax.ppermute(other, "core", [(0, 1), (1, 0)])
    kept, *sends = add_cores(where, mine, got)
    return add_chips(kept, [ring(sends[k - 1], "y", k) for k in (2, 1, 3)])


def solution(mesh):
    parts = Mesh(mesh.devices.reshape(4, 4, 4, 4, 2), ("row", "x", "z_hi", "y", "core"))
    in_specs = (P(("y", "core"), "row", ("x", "z_hi")), P(("y", "core"), ("x", "z_hi"), "row"))
    out_specs = P(("x", "z_hi", "y", "core"), "row")
    return jax.shard_map(shards, mesh=parts, in_specs=in_specs, out_specs=out_specs, check_vma=False)
```

time: 320 us -> 190 us (0.59)
  the two profiles are of different devices: /device:TPU:1 before, /device:TPU:56 now
where the time goes in v3:
time: 190 us
  waiting for transfers between devices  87.3 us (46%)
  starting transfers between devices  67.5 us (36%)
  Pallas kernels  18.9 us (10%)
  between operations  13.8 us (7%)
  local copies, waits for them, and re-layouts  2.07 us (1%)
    ppermute x16, waiting for transfers between devices, ring(): return lax.ppermute(value, axis, [(i, (i + step) % 4) for i in range(4)])  84.4 us
    ppermute x16, starting transfers between devices, ring(): return lax.ppermute(value, axis, [(i, (i + step) % 4) for i in range(4)])  65.6 us
    pallas_call x1, Pallas kernels, product(): pl.pallas_call(product_kernel, out_shape=[jax.ShapeDtypeStruct((4, rows /...  10 us
    pallas_call x1, Pallas kernels, stage(): pl.pallas_call(stage_kernel, out_shape=jax.ShapeDtypeStruct((tokens, piec...  5.49 us
  transfers between devices with their start and end apart: 18, of which 11 were waited for; matrix products, arithmetic and copies ran while one was open for 0% of the time, Pallas kernels for 3%

profile of v3, /device:TPU:56, one launch (start us, length us, event | category | flops | bytes accessed | tf_op | source)
XLA Modules:
  0.0 189.5 jit_solution(993267721133386146)
XLA Ops:
  6.6 1.1 copy-done
  7.8 1.8 turn.1
  9.5 9.1 %collective-permute-start.1 = (bf16[128,1536]{1,0:T(8,128)(2,1)S(1)}, bf16[128,1536]{1,0:T(8,128)(2,1)S(1)}, u32[]{:S(2)}, u32[]{:S(2)}) collective-permute-start(bf16[128,1536]{1,0:T(8,128)(2,1)S(1)} %bitcast.10), channel_id=1, source_target_pairs={{0,8},{8,16},{16,24},{24,0},{1,9},{9,17},{17,25},{25,1},{2,10},{10... | collective-permute-start | bytes 1179656 | tf_op jit(solution)/shard_map/ppermute | solution.py:157
  18.6 4.7 %collective-permute-start = (bf16[128,1536]{1,0:T(8,128)(2,1)S(1)}, bf16[128,1536]{1,0:T(8,128)(2,1)S(1)}, u32[]{:S(2)}, u32[]{:S(2)}) collective-permute-start(bf16[128,1536]{1,0:T(8,128)(2,1)S(1)} %bitcast.11), channel_id=1, source_target_pairs={{0,24},{8,0},{16,8},{24,16},{1,25},{9,1},{17,9},{25,17},{2,26},{10... | collective-permute-start | bytes 1179656 | tf_op jit(solution)/shard_map/ppermute | solution.py:157
  23.3 4.7 %collective-permute-start.2 = (bf16[128,1536]{1,0:T(8,128)(2,1)S(1)}, bf16[128,1536]{1,0:T(8,128)(2,1)S(1)}, u32[]{:S(2)}, u32[]{:S(2)}) collective-permute-start(bf16[128,1536]{1,0:T(8,128)(2,1)S(1)} %bitcast.12), channel_id=1, source_target_pairs={{0,96},{32,0},{64,32},{96,64},{1,97},{33,1},{65,33},{97,65},{2,98}... | collective-permute-start | bytes 1179656 | tf_op jit(solution)/shard_map/ppermute | solution.py:157
  28.0 2.7 %collective-permute-start.3 = (bf16[128,1536]{1,0:T(8,128)(2,1)S(1)}, bf16[128,1536]{1,0:T(8,128)(2,1)S(1)}, u32[]{:S(2)}, u32[]{:S(2)}) collective-permute-start(bf16[128,1536]{1,0:T(8,128)(2,1)S(1)} %bitcast.13), channel_id=1, source_target_pairs={{0,64},{32,96},{64,0},{96,32},{1,65},{33,97},{65,1},{97,33},{2,66}... | collective-permute-start | bytes 1179656 | tf_op jit(solution)/shard_map/ppermute | solution.py:157
  30.7 2.8 %collective-permute-start.4 = (bf16[128,1536]{1,0:T(8,128)(2,1)S(1)}, bf16[128,1536]{1,0:T(8,128)(2,1)S(1)}, u32[]{:S(2)}, u32[]{:S(2)}) collective-permute-start(bf16[128,1536]{1,0:T(8,128)(2,1)S(1)} %bitcast.14), channel_id=1, source_target_pairs={{0,32},{32,64},{64,96},{96,0},{1,33},{33,65},{65,97},{97,1},{2,34}... | collective-permute-start | bytes 1179656 | tf_op jit(solution)/shard_map/ppermute | solution.py:157
  33.5 31.1 %collective-permute-done.1 = bf16[128,1536]{1,0:T(8,128)(2,1)S(1)} collective-permute-done((bf16[128,1536]{1,0:T(8,128)(2,1)S(1)}, bf16[128,1536]{1,0:T(8,128)(2,1)S(1)}, u32[]{:S(2)}, u32[]{:S(2)}) %collective-permute-start.1) | collective-permute-done | bytes 393248 | tf_op jit(solution)/shard_map/ppermute | solution.py:157
  64.6 10.8 %collective-permute-done = bf16[128,1536]{1,0:T(8,128)(2,1)S(1)} collective-permute-done((bf16[128,1536]{1,0:T(8,128)(2,1)S(1)}, bf16[128,1536]{1,0:T(8,128)(2,1)S(1)}, u32[]{:S(2)}, u32[]{:S(2)}) %collective-permute-start) | collective-permute-done | bytes 393248 | tf_op jit(solution)/shard_map/ppermute | solution.py:157
  75.5 4.7 %collective-permute-start.7 = (bf16[256,1536]{1,0:T(8,128)(2,1)S(1)}, bf16[256,1536]{1,0:T(8,128)(2,1)S(1)}, u32[]{:S(2)}, u32[]{:S(2)}) collective-permute-start(bf16[256,1536]{1,0:T(8,128)(2,1)S(1)} %pad_maximum_fusion.refs_1_), channel_id=1, source_target_pairs={{0,96},{32,0},{64,32},{96,64},{1,97},{33,1},{65,33},{97,65},{2,98}... | collective-permute-start | bytes 2359304 | tf_op jit(solution)/shard_map/ppermute | solution.py:157
  80.3 2.7 %collective-permute-start.8 = (bf16[256,1536]{1,0:T(8,128)(2,1)S(1)}, bf16[256,1536]{1,0:T(8,128)(2,1)S(1)}, u32[]{:S(2)}, u32[]{:S(2)}) collective-permute-start(bf16[256,1536]{1,0:T(8,128)(2,1)S(1)} %pad_maximum_fusion.refs_1_), channel_id=1, source_target_pairs={{0,64},{32,96},{64,0},{96,32},{1,65},{33,97},{65,1},{97,33},{2,66}... | collective-permute-start | bytes 2359304 | tf_op jit(solution)/shard_map/ppermute | solution.py:157
  82.9 2.8 %collective-permute-start.9 = (bf16[256,1536]{1,0:T(8,128)(2,1)S(1)}, bf16[256,1536]{1,0:T(8,128)(2,1)S(1)}, u32[]{:S(2)}, u32[]{:S(2)}) collective-permute-start(bf16[256,1536]{1,0:T(8,128)(2,1)S(1)} %pad_maximum_fusion.refs_1_), channel_id=1, source_target_pairs={{0,32},{32,64},{64,96},{96,0},{1,33},{33,65},{65,97},{97,1},{2,34}... | collective-permute-start | bytes 2359304 | tf_op jit(solution)/shard_map/ppermute | solution.py:157
  85.8 10.8 %collective-permute-start.5 = (bf16[64,1536]{1,0:T(8,128)(2,1)S(1)}, bf16[64,1536]{1,0:T(8,128)(2,1)S(1)}, u32[]{:S(2)}, u32[]{:S(2)}) collective-permute-start(bf16[64,1536]{1,0:T(8,128)(2,1)S(1)} %slice.8), channel_id=1, source_target_pairs={{0,8},{8,16},{16,24},{24,0},{1,9},{9,17},{17,25},{25,1},{2,10},{10... | collective-permute-start | bytes 589832 | tf_op jit(solution)/shard_map/ppermute | solution.py:157
  96.6 1.9 %collective-permute-start.6 = (bf16[64,1536]{1,0:T(8,128)(2,1)S(1)}, bf16[64,1536]{1,0:T(8,128)(2,1)S(1)}, u32[]{:S(2)}, u32[]{:S(2)}) collective-permute-start(bf16[64,1536]{1,0:T(8,128)(2,1)S(1)} %slice.9), channel_id=1, source_target_pairs={{0,24},{8,0},{16,8},{24,16},{1,25},{9,1},{17,9},{25,17},{2,26},{10... | collective-permute-start | bytes 589832 | tf_op jit(solution)/shard_map/ppermute | solution.py:157
  98.5 12.5 %collective-permute-done.5 = bf16[64,1536]{1,0:T(8,128)(2,1)S(1)} collective-permute-done((bf16[64,1536]{1,0:T(8,128)(2,1)S(1)}, bf16[64,1536]{1,0:T(8,128)(2,1)S(1)}, u32[]{:S(2)}, u32[]{:S(2)}) %collective-permute-start.5) | collective-permute-done | bytes 196640 | tf_op jit(solution)/shard_map/ppermute | solution.py:157
  111.0 9.2 %collective-permute-done.6 = bf16[64,1536]{1,0:T(8,128)(2,1)S(1)} collective-permute-done((bf16[64,1536]{1,0:T(8,128)(2,1)S(1)}, bf16[64,1536]{1,0:T(8,128)(2,1)S(1)}, u32[]{:S(2)}, u32[]{:S(2)}) %collective-permute-start.6) | collective-permute-done | bytes 196640 | tf_op jit(solution)/shard_map/ppermute | solution.py:157
  120.3 4.2 %collective-permute-start.10 = (bf16[128,1536]{1,0:T(8,128)(2,1)S(1)}, bf16[128,1536]{1,0:T(8,128)(2,1)S(1)}, u32[]{:S(2)}, u32[]{:S(2)}) collective-permute-start(bf16[128,1536]{1,0:T(8,128)(2,1)S(1)} %constant_dynamic-update-slice_fusion.refs_2_), channel_id=1, source_target_pairs={{0,96},{32,0},{64,32},{96,64},{1,97},{33,1},{65,33},{97,65},{2,98}... | collective-permute-start | bytes 1179656 | tf_op jit(solution)/shard_map/ppermute | solution.py:157
  124.6 3.4 %collective-permute-start.11 = (bf16[128,1536]{1,0:T(8,128)(2,1)S(1)}, bf16[128,1536]{1,0:T(8,128)(2,1)S(1)}, u32[]{:S(2)}, u32[]{:S(2)}) collective-permute-start(bf16[128,1536]{1,0:T(8,128)(2,1)S(1)} %constant_dynamic-update-slice_fusion.refs_2_), channel_id=1, source_target_pairs={{0,64},{32,96},{64,0},{96,32},{1,65},{33,97},{65,1},{97,33},{2,66}... | collective-permute-start | bytes 1179656 | tf_op jit(solution)/shard_map/ppermute | solution.py:157
  128.0 1.9 %collective-permute-start.12 = (bf16[128,1536]{1,0:T(8,128)(2,1)S(1)}, bf16[128,1536]{1,0:T(8,128)(2,1)S(1)}, u32[]{:S(2)}, u32[]{:S(2)}) collective-permute-start(bf16[128,1536]{1,0:T(8,128)(2,1)S(1)} %constant_dynamic-update-slice_fusion.refs_2_), channel_id=1, source_target_pairs={{0,32},{32,64},{64,96},{96,0},{1,33},{33,65},{65,97},{97,1},{2,34}... | collective-permute-start | bytes 1179656 | tf_op jit(solution)/shard_map/ppermute | solution.py:157
  129.9 6.0 %collective-permute-done.10.refs_5_ = bf16[128,1536]{1,0:T(8,128)(2,1)S(1)} collective-permute-done((bf16[128,1536]{1,0:T(8,128)(2,1)S(1)}, bf16[128,1536]{1,0:T(8,128)(2,1)S(1)}, u32[]{:S(2)}, u32[]{:S(2)}) %collective-permute-start.10) | collective-permute-done | bytes 393248 | tf_op jit(solution)/shard_map/ppermute | solution.py:157
  136.6 4.1 %collective-permute-done.12.refs_11_ = bf16[128,1536]{1,0:T(8,128)(2,1)S(1)} collective-permute-done((bf16[128,1536]{1,0:T(8,128)(2,1)S(1)}, bf16[128,1536]{1,0:T(8,128)(2,1)S(1)}, u32[]{:S(2)}, u32[]{:S(2)}) %collective-permute-start.12) | collective-permute-done | bytes 393248 | tf_op jit(solution)/shard_map/ppermute | solution.py:157
  141.6 5.5 %stage.1.right_ref = bf16[2048,1536]{1,0:T(8,128)(2,1)} custom-call(bf16[128,1536]{1,0:T(8,128)(2,1)} %bitcast.9, bf16[256,1536]{1,0:T(8,128)(2,1)} %copy-done.1, bf16[128,1536]{1,0:T(8,128)(2,1)} %copy-done.2, bf16[128,1536]{1,0:T(8,128)(2,1)} %copy-done.7, bf16[256,1536]{1,0:T(8,128)(2,1)} %copy-done.3, bf16[128,1536]{1,0:T(8,128)(2,1)} %copy-done.10, ...), custom_call_target="tpu_custom_call" | custom-call | bytes 12582912 | tf_op jit(solution)/shard_map/stage/pallas_call | solution.py:68
  147.1 10.0 %product.1 = (bf16[4,96,1536]{2,1,0:T(8,128)(2,1)S(1)}, f32[4,96,1536]{2,1,0:T(8,128)S(1)}) custom-call(s32[5]{0:T(128)S(1)} %stack.23.where, bf16[4,768,512]{2,1,0:T(8,128)(2,1)} %bitcast.15, bf16[2048,1536]{1,0:T(8,128)(2,1)} %stage.1.right_ref), custom_call_target="tpu_custom_call" | custom-call | flops 4831838208 | bytes 10485760 | tf_op jit(solution)/shard_map/product/pallas_call | solution.py:104
  157.2 1.9 %collective-permute-start.13 = (bf16[4,96,1536]{2,1,0:T(8,128)(2,1)S(1)}, bf16[4,96,1536]{2,1,0:T(8,128)(2,1)S(1)}, u32[]{:S(2)}, u32[]{:S(2)}) collective-permute-start(bf16[4,96,1536]{2,1,0:T(8,128)(2,1)S(1)} %get-tuple-element.34), channel_id=1, source_target_pairs={{0,1},{1,0},{2,3},{3,2},{4,5},{5,4},{6,7},{7,6},{8,9},{9,8},{10,11... | collective-permute-start | bytes 3538952 | tf_op jit(solution)/shard_map/ppermute | solution.py:183
  159.1 2.8 %collective-permute-done.13.got_ref = bf16[4,96,1536]{2,1,0:T(8,128)(2,1)S(1)} collective-permute-done((bf16[4,96,1536]{2,1,0:T(8,128)(2,1)S(1)}, bf16[4,96,1536]{2,1,0:T(8,128)(2,1)S(1)}, u32[]{:S(2)}, u32[]{:S(2)}) %collective-permute-start.13) | collective-permute-done | bytes 1179680 | tf_op jit(solution)/shard_map/ppermute | solution.py:183
  162.7 3.0 %collective-permute-start.14 = (bf16[96,1536]{1,0:T(8,128)(2,1)S(1)}, bf16[96,1536]{1,0:T(8,128)(2,1)S(1)}, u32[]{:S(2)}, u32[]{:S(2)}) collective-permute-start(bf16[96,1536]{1,0:T(8,128)(2,1)S(1)} %get-tuple-element.36), channel_id=1, source_target_pairs={{0,4},{2,6},{4,0},{6,2},{1,5},{3,7},{5,1},{7,3},{8,12},{10,14},{12... | collective-permute-start | bytes 884744 | tf_op jit(solution)/shard_map/ppermute | solution.py:157
  165.7 4.2 %collective-permute-start.15 = (bf16[96,1536]{1,0:T(8,128)(2,1)S(1)}, bf16[96,1536]{1,0:T(8,128)(2,1)S(1)}, u32[]{:S(2)}, u32[]{:S(2)}) collective-permute-start(bf16[96,1536]{1,0:T(8,128)(2,1)S(1)} %get-tuple-element.37), channel_id=1, source_target_pairs={{0,2},{2,4},{4,6},{6,0},{1,3},{3,5},{5,7},{7,1},{8,10},{10,12},{12... | collective-permute-start | bytes 884744 | tf_op jit(solution)/shard_map/ppermute | solution.py:157
  169.9 1.9 %collective-permute-start.16 = (bf16[96,1536]{1,0:T(8,128)(2,1)S(1)}, bf16[96,1536]{1,0:T(8,128)(2,1)S(1)}, u32[]{:S(2)}, u32[]{:S(2)}) collective-permute-start(bf16[96,1536]{1,0:T(8,128)(2,1)S(1)} %get-tuple-element.38), channel_id=1, source_target_pairs={{0,6},{2,0},{4,2},{6,4},{1,7},{3,1},{5,3},{7,5},{8,14},{10,8},{12,... | collective-permute-start | bytes 884744 | tf_op jit(solution)/shard_map/ppermute | solution.py:157
  171.8 4.1 %collective-permute-done.14.refs_0_ = bf16[96,1536]{1,0:T(8,128)(2,1)S(1)} collective-permute-done((bf16[96,1536]{1,0:T(8,128)(2,1)S(1)}, bf16[96,1536]{1,0:T(8,128)(2,1)S(1)}, u32[]{:S(2)}, u32[]{:S(2)}) %collective-permute-start.14) | collective-permute-done | bytes 294944 | tf_op jit(solution)/shard_map/ppermute | solution.py:157
  175.9 3.0 %collective-permute-done.15.refs_1_ = bf16[96,1536]{1,0:T(8,128)(2,1)S(1)} collective-permute-done((bf16[96,1536]{1,0:T(8,128)(2,1)S(1)}, bf16[96,1536]{1,0:T(8,128)(2,1)S(1)}, u32[]{:S(2)}, u32[]{:S(2)}) %collective-permute-start.15) | collective-permute-done | bytes 294944 | tf_op jit(solution)/shard_map/ppermute | solution.py:157
  178.9 2.9 %collective-permute-done.16.refs_2_ = bf16[96,1536]{1,0:T(8,128)(2,1)S(1)} collective-permute-done((bf16[96,1536]{1,0:T(8,128)(2,1)S(1)}, bf16[96,1536]{1,0:T(8,128)(2,1)S(1)}, u32[]{:S(2)}, u32[]{:S(2)}) %collective-permute-start.16) | collective-permute-done | bytes 294944 | tf_op jit(solution)/shard_map/ppermute | solution.py:157
  181.9 0.8 add_chips.1
  (42 shorter events, 2.5 us)
Async XLA Ops:
  6.5 140.6 %all-gather.3.cloned.1.call-start = ((), (), s32[]{:S(2)}) async-start(), calls=%async_computation | async-start | bytes 3932160 | tf_op jit(solution)/shard_map/all_gather | solution.py:165
  6.6 1.1 copy-start
  7.8 1.8 copy-start.6
  9.5 55.0 %collective-permute-start.1 = (bf16[128,1536]{1,0:T(8,128)(2,1)S(1)}, bf16[128,1536]{1,0:T(8,128)(2,1)S(1)}, u32[]{:S(2)}, u32[]{:S(2)}) collective-permute-start(bf16[128,1536]{1,0:T(8,128)(2,1)S(1)} %bitcast.10), channel_id=1, source_target_pairs={{0,8},{8,16},{16,24},{24,0},{1,9},{9,17},{17,25},{25,1},{2,10},{10... | collective-permute-start | bytes 1179656 | tf_op jit(solution)/shard_map/ppermute | solution.py:157
  18.6 56.7 %collective-permute-start = (bf16[128,1536]{1,0:T(8,128)(2,1)S(1)}, bf16[128,1536]{1,0:T(8,128)(2,1)S(1)}, u32[]{:S(2)}, u32[]{:S(2)}) collective-permute-start(bf16[128,1536]{1,0:T(8,128)(2,1)S(1)} %bitcast.11), channel_id=1, source_target_pairs={{0,24},{8,0},{16,8},{24,16},{1,25},{9,1},{17,9},{25,17},{2,26},{10... | collective-permute-start | bytes 1179656 | tf_op jit(solution)/shard_map/ppermute | solution.py:157
  23.3 52.1 %collective-permute-start.2 = (bf16[128,1536]{1,0:T(8,128)(2,1)S(1)}, bf16[128,1536]{1,0:T(8,128)(2,1)S(1)}, u32[]{:S(2)}, u32[]{:S(2)}) collective-permute-start(bf16[128,1536]{1,0:T(8,128)(2,1)S(1)} %bitcast.12), channel_id=1, source_target_pairs={{0,96},{32,0},{64,32},{96,64},{1,97},{33,1},{65,33},{97,65},{2,98}... | collective-permute-start | bytes 1179656 | tf_op jit(solution)/shard_map/ppermute | solution.py:157
  28.0 47.5 %collective-permute-start.3 = (bf16[128,1536]{1,0:T(8,128)(2,1)S(1)}, bf16[128,1536]{1,0:T(8,128)(2,1)S(1)}, u32[]{:S(2)}, u32[]{:S(2)}) collective-permute-start(bf16[128,1536]{1,0:T(8,128)(2,1)S(1)} %bitcast.13), channel_id=1, source_target_pairs={{0,64},{32,96},{64,0},{96,32},{1,65},{33,97},{65,1},{97,33},{2,66}... | collective-permute-start | bytes 1179656 | tf_op jit(solution)/shard_map/ppermute | solution.py:157
  30.7 44.8 %collective-permute-start.4 = (bf16[128,1536]{1,0:T(8,128)(2,1)S(1)}, bf16[128,1536]{1,0:T(8,128)(2,1)S(1)}, u32[]{:S(2)}, u32[]{:S(2)}) collective-permute-start(bf16[128,1536]{1,0:T(8,128)(2,1)S(1)} %bitcast.14), channel_id=1, source_target_pairs={{0,32},{32,64},{64,96},{96,0},{1,33},{33,65},{65,97},{97,1},{2,34}... | collective-permute-start | bytes 1179656 | tf_op jit(solution)/shard_map/ppermute | solution.py:157
  75.4 65.3 %copy-start.1 = (bf16[256,1536]{1,0:T(8,128)(2,1)}, bf16[256,1536]{1,0:T(8,128)(2,1)S(1)}, u32[]{:S(2)}) copy-start(bf16[256,1536]{1,0:T(8,128)(2,1)S(1)} %pad_maximum_fusion.refs_1_) | copy-start | bytes 2359300
  75.5 65.3 %copy-start.7 = (bf16[128,1536]{1,0:T(8,128)(2,1)}, bf16[128,1536]{1,0:T(8,128)(2,1)S(1)}, u32[]{:S(2)}) copy-start(bf16[128,1536]{1,0:T(8,128)(2,1)S(1)} %collective-permute-done.2.refs_3_) | copy-start | bytes 1179652
  75.5 65.3 %copy-start.8 = (bf16[128,1536]{1,0:T(8,128)(2,1)}, bf16[128,1536]{1,0:T(8,128)(2,1)S(1)}, u32[]{:S(2)}) copy-start(bf16[128,1536]{1,0:T(8,128)(2,1)S(1)} %collective-permute-done.3.refs_6_) | copy-start | bytes 1179652
  75.5 65.3 %copy-start.9 = (bf16[128,1536]{1,0:T(8,128)(2,1)}, bf16[128,1536]{1,0:T(8,128)(2,1)S(1)}, u32[]{:S(2)}) copy-start(bf16[128,1536]{1,0:T(8,128)(2,1)S(1)} %collective-permute-done.4.refs_9_) | copy-start | bytes 1179652
  75.5 44.7 %collective-permute-start.7 = (bf16[256,1536]{1,0:T(8,128)(2,1)S(1)}, bf16[256,1536]{1,0:T(8,128)(2,1)S(1)}, u32[]{:S(2)}, u32[]{:S(2)}) collective-permute-start(bf16[256,1536]{1,0:T(8,128)(2,1)S(1)} %pad_maximum_fusion.refs_1_), channel_id=1, source_target_pairs={{0,96},{32,0},{64,32},{96,64},{1,97},{33,1},{65,33},{97,65},{2,98}... | collective-permute-start | bytes 2359304 | tf_op jit(solution)/shard_map/ppermute | solution.py:157
  80.3 40.0 %collective-permute-start.8 = (bf16[256,1536]{1,0:T(8,128)(2,1)S(1)}, bf16[256,1536]{1,0:T(8,128)(2,1)S(1)}, u32[]{:S(2)}, u32[]{:S(2)}) collective-permute-start(bf16[256,1536]{1,0:T(8,128)(2,1)S(1)} %pad_maximum_fusion.refs_1_), channel_id=1, source_target_pairs={{0,64},{32,96},{64,0},{96,32},{1,65},{33,97},{65,1},{97,33},{2,66}... | collective-permute-start | bytes 2359304 | tf_op jit(solution)/shard_map/ppermute | solution.py:157
  82.9 37.3 %collective-permute-start.9 = (bf16[256,1536]{1,0:T(8,128)(2,1)S(1)}, bf16[256,1536]{1,0:T(8,128)(2,1)S(1)}, u32[]{:S(2)}, u32[]{:S(2)}) collective-permute-start(bf16[256,1536]{1,0:T(8,128)(2,1)S(1)} %pad_maximum_fusion.refs_1_), channel_id=1, source_target_pairs={{0,32},{32,64},{64,96},{96,0},{1,33},{33,65},{65,97},{97,1},{2,34}... | collective-permute-start | bytes 2359304 | tf_op jit(solution)/shard_map/ppermute | solution.py:157
  85.8 25.3 %collective-permute-start.5 = (bf16[64,1536]{1,0:T(8,128)(2,1)S(1)}, bf16[64,1536]{1,0:T(8,128)(2,1)S(1)}, u32[]{:S(2)}, u32[]{:S(2)}) collective-permute-start(bf16[64,1536]{1,0:T(8,128)(2,1)S(1)} %slice.8), channel_id=1, source_target_pairs={{0,8},{8,16},{16,24},{24,0},{1,9},{9,17},{17,25},{25,1},{2,10},{10... | collective-permute-start | bytes 589832 | tf_op jit(solution)/shard_map/ppermute | solution.py:157
  96.6 23.6 %collective-permute-start.6 = (bf16[64,1536]{1,0:T(8,128)(2,1)S(1)}, bf16[64,1536]{1,0:T(8,128)(2,1)S(1)}, u32[]{:S(2)}, u32[]{:S(2)}) collective-permute-start(bf16[64,1536]{1,0:T(8,128)(2,1)S(1)} %slice.9), channel_id=1, source_target_pairs={{0,24},{8,0},{16,8},{24,16},{1,25},{9,1},{17,9},{25,17},{2,26},{10... | collective-permute-start | bytes 589832 | tf_op jit(solution)/shard_map/ppermute | solution.py:157
  120.2 20.6 %copy-start.3 = (bf16[256,1536]{1,0:T(8,128)(2,1)}, bf16[256,1536]{1,0:T(8,128)(2,1)S(1)}, u32[]{:S(2)}) copy-start(bf16[256,1536]{1,0:T(8,128)(2,1)S(1)} %collective-permute-done.7.refs_4_) | copy-start | bytes 2359300
  120.2 20.6 %copy-start.4 = (bf16[256,1536]{1,0:T(8,128)(2,1)}, bf16[256,1536]{1,0:T(8,128)(2,1)S(1)}, u32[]{:S(2)}) copy-start(bf16[256,1536]{1,0:T(8,128)(2,1)S(1)} %collective-permute-done.8.refs_7_) | copy-start | bytes 2359300
  120.2 20.5 %copy-start.5 = (bf16[256,1536]{1,0:T(8,128)(2,1)}, bf16[256,1536]{1,0:T(8,128)(2,1)S(1)}, u32[]{:S(2)}) copy-start(bf16[256,1536]{1,0:T(8,128)(2,1)S(1)} %collective-permute-done.9.refs_10_) | copy-start | bytes 2359300
  120.3 20.5 %copy-start.2 = (bf16[128,1536]{1,0:T(8,128)(2,1)}, bf16[128,1536]{1,0:T(8,128)(2,1)S(1)}, u32[]{:S(2)}) copy-start(bf16[128,1536]{1,0:T(8,128)(2,1)S(1)} %constant_dynamic-update-slice_fusion.refs_2_) | copy-start | bytes 1179652
  120.3 15.6 %collective-permute-start.10 = (bf16[128,1536]{1,0:T(8,128)(2,1)S(1)}, bf16[128,1536]{1,0:T(8,128)(2,1)S(1)}, u32[]{:S(2)}, u32[]{:S(2)}) collective-permute-start(bf16[128,1536]{1,0:T(8,128)(2,1)S(1)} %constant_dynamic-update-slice_fusion.refs_2_), channel_id=1, source_target_pairs={{0,96},{32,0},{64,32},{96,64},{1,97},{33,1},{65,33},{97,65},{2,98}... | collective-permute-start | bytes 1179656 | tf_op jit(solution)/shard_map/ppermute | solution.py:157
  124.6 12.1 %collective-permute-start.11 = (bf16[128,1536]{1,0:T(8,128)(2,1)S(1)}, bf16[128,1536]{1,0:T(8,128)(2,1)S(1)}, u32[]{:S(2)}, u32[]{:S(2)}) collective-permute-start(bf16[128,1536]{1,0:T(8,128)(2,1)S(1)} %constant_dynamic-update-slice_fusion.refs_2_), channel_id=1, source_target_pairs={{0,64},{32,96},{64,0},{96,32},{1,65},{33,97},{65,1},{97,33},{2,66}... | collective-permute-start | bytes 1179656 | tf_op jit(solution)/shard_map/ppermute | solution.py:157
  128.0 12.8 %collective-permute-start.12 = (bf16[128,1536]{1,0:T(8,128)(2,1)S(1)}, bf16[128,1536]{1,0:T(8,128)(2,1)S(1)}, u32[]{:S(2)}, u32[]{:S(2)}) collective-permute-start(bf16[128,1536]{1,0:T(8,128)(2,1)S(1)} %constant_dynamic-update-slice_fusion.refs_2_), channel_id=1, source_target_pairs={{0,32},{32,64},{64,96},{96,0},{1,33},{33,65},{65,97},{97,1},{2,34}... | collective-permute-start | bytes 1179656 | tf_op jit(solution)/shard_map/ppermute | solution.py:157
  135.9 4.9 %copy-start.10 = (bf16[128,1536]{1,0:T(8,128)(2,1)}, bf16[128,1536]{1,0:T(8,128)(2,1)S(1)}, u32[]{:S(2)}) copy-start(bf16[128,1536]{1,0:T(8,128)(2,1)S(1)} %collective-permute-done.10.refs_5_) | copy-start | bytes 1179652
  136.6 4.2 %copy-start.11 = (bf16[128,1536]{1,0:T(8,128)(2,1)}, bf16[128,1536]{1,0:T(8,128)(2,1)S(1)}, u32[]{:S(2)}) copy-start(bf16[128,1536]{1,0:T(8,128)(2,1)S(1)} %collective-permute-done.11.refs_8_) | copy-start | bytes 1179652
  140.8 0.8 copy-start.12
  157.2 4.7 %collective-permute-start.13 = (bf16[4,96,1536]{2,1,0:T(8,128)(2,1)S(1)}, bf16[4,96,1536]{2,1,0:T(8,128)(2,1)S(1)}, u32[]{:S(2)}, u32[]{:S(2)}) collective-permute-start(bf16[4,96,1536]{2,1,0:T(8,128)(2,1)S(1)} %get-tuple-element.34), channel_id=1, source_target_pairs={{0,1},{1,0},{2,3},{3,2},{4,5},{5,4},{6,7},{7,6},{8,9},{9,8},{10,11... | collective-permute-start | bytes 3538952 | tf_op jit(solution)/shard_map/ppermute | solution.py:183
  162.7 13.2 %collective-permute-start.14 = (bf16[96,1536]{1,0:T(8,128)(2,1)S(1)}, bf16[96,1536]{1,0:T(8,128)(2,1)S(1)}, u32[]{:S(2)}, u32[]{:S(2)}) collective-permute-start(bf16[96,1536]{1,0:T(8,128)(2,1)S(1)} %get-tuple-element.36), channel_id=1, source_target_pairs={{0,4},{2,6},{4,0},{6,2},{1,5},{3,7},{5,1},{7,3},{8,12},{10,14},{12... | collective-permute-start | bytes 884744 | tf_op jit(solution)/shard_map/ppermute | solution.py:157
  165.7 13.2 %collective-permute-start.15 = (bf16[96,1536]{1,0:T(8,128)(2,1)S(1)}, bf16[96,1536]{1,0:T(8,128)(2,1)S(1)}, u32[]{:S(2)}, u32[]{:S(2)}) collective-permute-start(bf16[96,1536]{1,0:T(8,128)(2,1)S(1)} %get-tuple-element.37), channel_id=1, source_target_pairs={{0,2},{2,4},{4,6},{6,0},{1,3},{3,5},{5,7},{7,1},{8,10},{10,12},{12... | collective-permute-start | bytes 884744 | tf_op jit(solution)/shard_map/ppermute | solution.py:157
  169.9 12.0 %collective-permute-start.16 = (bf16[96,1536]{1,0:T(8,128)(2,1)S(1)}, bf16[96,1536]{1,0:T(8,128)(2,1)S(1)}, u32[]{:S(2)}, u32[]{:S(2)}) collective-permute-start(bf16[96,1536]{1,0:T(8,128)(2,1)S(1)} %get-tuple-element.38), channel_id=1, source_target_pairs={{0,6},{2,0},{4,2},{6,4},{1,7},{3,1},{5,3},{7,5},{8,14},{10,8},{12,... | collective-permute-start | bytes 884744 | tf_op jit(solution)/shard_map/ppermute | solution.py:157
Sparse Core Ops, SparseCore 0:
  9.7 116.6 all-gather.2

commit v4 on v3

--- a/solution.py
+++ b/solution.py
@@ -93,7 +93,7 @@
         value = jnp.dot(left[...], right_ref[:, at], preferred_element_type=F32)
         for y in range(4):
             other_ref[y, :, at] = value[y * share : (y + 1) * share].astype(BF16)
-            own_ref[y, :, at] = value[(4 + y) * share : (5 + y) * share]
+            own_ref[y, :, at] = value[(4 + y) * share : (5 + y) * share].astype(BF16)
         return carry
 
     lax.fori_loop(0, right_ref.shape[1] // TILE, step, 0)
@@ -105,7 +105,7 @@
         product_kernel,
         out_shape=[
             jax.ShapeDtypeStruct((4, rows // 8, columns), BF16),
-            jax.ShapeDtypeStruct((4, rows // 8, columns), F32),
+            jax.ShapeDtypeStruct((4, rows // 8, columns), BF16),
         ],
         in_specs=[smem_spec(), any_spec(), vmem_spec()],
         out_specs=[vmem_spec(), vmem_spec()],
@@ -120,7 +120,7 @@
     y = where[3]
     for k in range(4):
         at = lax.rem(y + k, 4)
-        outs[k][...] = (own_ref[at] + got_ref[at].astype(F32)).astype(outs[k].dtype)
+        outs[k][...] = (own_ref[at].astype(F32) + got_ref[at].astype(F32)).astype(outs[k].dtype)
 
 
 def add_cores(where, own, got):
@@ -162,13 +162,14 @@
     grads = out_grads[0]
     half = grads.shape[0] // 2
 
-    inputs = lax.all_gather(turn(where, activations[0]), "row", axis=0)
-
+    turned = turn(where, activations[0])
     before = ring(grads, "z_hi", 1)
     after = ring(grads, "z_hi", -1)
     owns = [ring(grads, "x", -t) for t in (1, 2, 3)]
     near = jnp.concatenate([after, before])
-    near, top, bottom, *owns = lax.optimization_barrier((near, before[:half], after[half:], *owns))
+    near, top, bottom, turned, *owns = lax.optimization_barrier((near, before[:half], after[half:], turned, *owns))
+
+    inputs = lax.all_gather(turned, "row", axis=0)
 
     far_top = ring(top, "z_hi", 1)
     far_bottom = ring(bottom, "z_hi", -1)

time: 190 us -> 186 us (0.979)
  the two profiles are of different devices: /device:TPU:56 before, /device:TPU:1 now
where the time goes in v4:
time: 186 us; the launch traced here: 185 us
  waiting for transfers between devices  86.8 us (47%)
  starting transfers between devices  63.9 us (34%)
  Pallas kernels  18.9 us (10%)
  between operations  13.7 us (7%)
  local copies, waits for them, and re-layouts  2.05 us (1%)
    ppermute x16, waiting for transfers between devices, ring(): return lax.ppermute(value, axis, [(i, (i + step) % 4) for i in range(4)])  76.2 us
    ppermute x16, starting transfers between devices, ring(): return lax.ppermute(value, axis, [(i, (i + step) % 4) for i in range(4)])  61.6 us
    pallas_call x1, Pallas kernels, product(): pl.pallas_call(product_kernel, out_shape=[jax.ShapeDtypeStruct((4, rows /...  10 us
    all_gather x1, waiting for transfers between devices, shards(): inputs = lax.all_gather(turned, 'row', axis=0)  8.11 us
    pallas_call x1, Pallas kernels, stage(): pl.pallas_call(stage_kernel, out_shape=jax.ShapeDtypeStruct((tokens, piec...  5.5 us
  transfers between devices with their start and end apart: 18, of which 10 were waited for; matrix products, arithmetic and copies ran while one was open for 0% of the time, Pallas kernels for 4%

profile of v4, /device:TPU:1, one launch (start us, length us, event | category | flops | bytes accessed | tf_op | source)
XLA Modules:
  0.0 185.5 jit_solution(16440173049619687585)
XLA Ops:
  6.5 9.6 %collective-permute-start.1 = (bf16[128,1536]{1,0:T(8,128)(2,1)}, bf16[128,1536]{1,0:T(8,128)(2,1)S(1)}, u32[]{:S(2)}, u32[]{:S(2)}) collective-permute-start(bf16[128,1536]{1,0:T(8,128)(2,1)} %bitcast.9), channel_id=1, source_target_pairs={{0,8},{8,16},{16,24},{24,0},{1,9},{9,17},{17,25},{25,1},{2,10},{10... | collective-permute-start | bytes 1179656 | tf_op jit(solution)/shard_map/ppermute | solution.py:157
  16.2 5.6 %collective-permute-start = (bf16[128,1536]{1,0:T(8,128)(2,1)}, bf16[128,1536]{1,0:T(8,128)(2,1)S(1)}, u32[]{:S(2)}, u32[]{:S(2)}) collective-permute-start(bf16[128,1536]{1,0:T(8,128)(2,1)} %bitcast.10), channel_id=1, source_target_pairs={{0,24},{8,0},{16,8},{24,16},{1,25},{9,1},{17,9},{25,17},{2,26},{10... | collective-permute-start | bytes 1179656 | tf_op jit(solution)/shard_map/ppermute | solution.py:157
  21.8 4.4 %collective-permute-start.2 = (bf16[128,1536]{1,0:T(8,128)(2,1)}, bf16[128,1536]{1,0:T(8,128)(2,1)S(1)}, u32[]{:S(2)}, u32[]{:S(2)}) collective-permute-start(bf16[128,1536]{1,0:T(8,128)(2,1)} %bitcast.11), channel_id=1, source_target_pairs={{0,96},{32,0},{64,32},{96,64},{1,97},{33,1},{65,33},{97,65},{2,98}... | collective-permute-start | bytes 1179656 | tf_op jit(solution)/shard_map/ppermute | solution.py:157
  26.1 2.4 %collective-permute-start.3 = (bf16[128,1536]{1,0:T(8,128)(2,1)}, bf16[128,1536]{1,0:T(8,128)(2,1)S(1)}, u32[]{:S(2)}, u32[]{:S(2)}) collective-permute-start(bf16[128,1536]{1,0:T(8,128)(2,1)} %bitcast.12), channel_id=1, source_target_pairs={{0,64},{32,96},{64,0},{96,32},{1,65},{33,97},{65,1},{97,33},{2,66}... | collective-permute-start | bytes 1179656 | tf_op jit(solution)/shard_map/ppermute | solution.py:157
  28.6 2.5 %collective-permute-start.4 = (bf16[128,1536]{1,0:T(8,128)(2,1)}, bf16[128,1536]{1,0:T(8,128)(2,1)S(1)}, u32[]{:S(2)}, u32[]{:S(2)}) collective-permute-start(bf16[128,1536]{1,0:T(8,128)(2,1)} %bitcast.13), channel_id=1, source_target_pairs={{0,32},{32,64},{64,96},{96,0},{1,33},{33,65},{65,97},{97,1},{2,34}... | collective-permute-start | bytes 1179656 | tf_op jit(solution)/shard_map/ppermute | solution.py:157
  31.2 1.1 copy-done
  32.3 1.8 turn.1
  34.1 25.6 %collective-permute-done = bf16[128,1536]{1,0:T(8,128)(2,1)S(1)} collective-permute-done((bf16[128,1536]{1,0:T(8,128)(2,1)}, bf16[128,1536]{1,0:T(8,128)(2,1)S(1)}, u32[]{:S(2)}, u32[]{:S(2)}) %collective-permute-start) | collective-permute-done | bytes 393248 | tf_op jit(solution)/shard_map/ppermute | solution.py:157
  59.8 4.4 %collective-permute-start.7 = (bf16[256,1536]{1,0:T(8,128)(2,1)S(1)}, bf16[256,1536]{1,0:T(8,128)(2,1)S(1)}, u32[]{:S(2)}, u32[]{:S(2)}) collective-permute-start(bf16[256,1536]{1,0:T(8,128)(2,1)S(1)} %pad_maximum_fusion.refs_1_), channel_id=1, source_target_pairs={{0,96},{32,0},{64,32},{96,64},{1,97},{33,1},{65,33},{97,65},{2,98}... | collective-permute-start | bytes 2359304 | tf_op jit(solution)/shard_map/ppermute | solution.py:157
  64.2 2.4 %collective-permute-start.8 = (bf16[256,1536]{1,0:T(8,128)(2,1)S(1)}, bf16[256,1536]{1,0:T(8,128)(2,1)S(1)}, u32[]{:S(2)}, u32[]{:S(2)}) collective-permute-start(bf16[256,1536]{1,0:T(8,128)(2,1)S(1)} %pad_maximum_fusion.refs_1_), channel_id=1, source_target_pairs={{0,64},{32,96},{64,0},{96,32},{1,65},{33,97},{65,1},{97,33},{2,66}... | collective-permute-start | bytes 2359304 | tf_op jit(solution)/shard_map/ppermute | solution.py:157
  66.7 2.5 %collective-permute-start.9 = (bf16[256,1536]{1,0:T(8,128)(2,1)S(1)}, bf16[256,1536]{1,0:T(8,128)(2,1)S(1)}, u32[]{:S(2)}, u32[]{:S(2)}) collective-permute-start(bf16[256,1536]{1,0:T(8,128)(2,1)S(1)} %pad_maximum_fusion.refs_1_), channel_id=1, source_target_pairs={{0,32},{32,64},{64,96},{96,0},{1,33},{33,65},{65,97},{97,1},{2,34}... | collective-permute-start | bytes 2359304 | tf_op jit(solution)/shard_map/ppermute | solution.py:157
  69.2 6.9 %collective-permute-start.5 = (bf16[64,1536]{1,0:T(8,128)(2,1)S(1)}, bf16[64,1536]{1,0:T(8,128)(2,1)S(1)}, u32[]{:S(2)}, u32[]{:S(2)}) collective-permute-start(bf16[64,1536]{1,0:T(8,128)(2,1)S(1)} %slice.8), channel_id=1, source_target_pairs={{0,8},{8,16},{16,24},{24,0},{1,9},{9,17},{17,25},{25,1},{2,10},{10... | collective-permute-start | bytes 589832 | tf_op jit(solution)/shard_map/ppermute | solution.py:157
  76.1 2.3 %collective-permute-start.6 = (bf16[64,1536]{1,0:T(8,128)(2,1)S(1)}, bf16[64,1536]{1,0:T(8,128)(2,1)S(1)}, u32[]{:S(2)}, u32[]{:S(2)}) collective-permute-start(bf16[64,1536]{1,0:T(8,128)(2,1)S(1)} %slice.9), channel_id=1, source_target_pairs={{0,24},{8,0},{16,8},{24,16},{1,25},{9,1},{17,9},{25,17},{2,26},{10... | collective-permute-start | bytes 589832 | tf_op jit(solution)/shard_map/ppermute | solution.py:157
  78.4 13.9 %collective-permute-done.5 = bf16[64,1536]{1,0:T(8,128)(2,1)S(1)} collective-permute-done((bf16[64,1536]{1,0:T(8,128)(2,1)S(1)}, bf16[64,1536]{1,0:T(8,128)(2,1)S(1)}, u32[]{:S(2)}, u32[]{:S(2)}) %collective-permute-start.5) | collective-permute-done | bytes 196640 | tf_op jit(solution)/shard_map/ppermute | solution.py:157
  92.3 11.7 %collective-permute-done.9.refs_10_ = bf16[256,1536]{1,0:T(8,128)(2,1)S(1)} collective-permute-done((bf16[256,1536]{1,0:T(8,128)(2,1)S(1)}, bf16[256,1536]{1,0:T(8,128)(2,1)S(1)}, u32[]{:S(2)}, u32[]{:S(2)}) %collective-permute-start.9) | collective-permute-done | bytes 786464 | tf_op jit(solution)/shard_map/ppermute | solution.py:157
  104.1 1.9 %collective-permute-start.10 = (bf16[128,1536]{1,0:T(8,128)(2,1)S(1)}, bf16[128,1536]{1,0:T(8,128)(2,1)S(1)}, u32[]{:S(2)}, u32[]{:S(2)}) collective-permute-start(bf16[128,1536]{1,0:T(8,128)(2,1)S(1)} %constant_dynamic-update-slice_fusion.refs_2_), channel_id=1, source_target_pairs={{0,96},{32,0},{64,32},{96,64},{1,97},{33,1},{65,33},{97,65},{2,98}... | collective-permute-start | bytes 1179656 | tf_op jit(solution)/shard_map/ppermute | solution.py:157
  106.0 2.4 %collective-permute-start.11 = (bf16[128,1536]{1,0:T(8,128)(2,1)S(1)}, bf16[128,1536]{1,0:T(8,128)(2,1)S(1)}, u32[]{:S(2)}, u32[]{:S(2)}) collective-permute-start(bf16[128,1536]{1,0:T(8,128)(2,1)S(1)} %constant_dynamic-update-slice_fusion.refs_2_), channel_id=1, source_target_pairs={{0,64},{32,96},{64,0},{96,32},{1,65},{33,97},{65,1},{97,33},{2,66}... | collective-permute-start | bytes 1179656 | tf_op jit(solution)/shard_map/ppermute | solution.py:157
  108.5 2.9 %collective-permute-start.12 = (bf16[128,1536]{1,0:T(8,128)(2,1)S(1)}, bf16[128,1536]{1,0:T(8,128)(2,1)S(1)}, u32[]{:S(2)}, u32[]{:S(2)}) collective-permute-start(bf16[128,1536]{1,0:T(8,128)(2,1)S(1)} %constant_dynamic-update-slice_fusion.refs_2_), channel_id=1, source_target_pairs={{0,32},{32,64},{64,96},{96,0},{1,33},{33,65},{65,97},{97,1},{2,34}... | collective-permute-start | bytes 1179656 | tf_op jit(solution)/shard_map/ppermute | solution.py:157
  111.3 5.1 %collective-permute-done.10.refs_5_ = bf16[128,1536]{1,0:T(8,128)(2,1)S(1)} collective-permute-done((bf16[128,1536]{1,0:T(8,128)(2,1)S(1)}, bf16[128,1536]{1,0:T(8,128)(2,1)S(1)}, u32[]{:S(2)}, u32[]{:S(2)}) %collective-permute-start.10) | collective-permute-done | bytes 393248 | tf_op jit(solution)/shard_map/ppermute | solution.py:157
  116.4 2.7 %collective-permute-done.11.refs_8_ = bf16[128,1536]{1,0:T(8,128)(2,1)S(1)} collective-permute-done((bf16[128,1536]{1,0:T(8,128)(2,1)S(1)}, bf16[128,1536]{1,0:T(8,128)(2,1)S(1)}, u32[]{:S(2)}, u32[]{:S(2)}) %collective-permute-start.11) | collective-permute-done | bytes 393248 | tf_op jit(solution)/shard_map/ppermute | solution.py:157
  119.1 9.9 %collective-permute-done.12.refs_11_ = bf16[128,1536]{1,0:T(8,128)(2,1)S(1)} collective-permute-done((bf16[128,1536]{1,0:T(8,128)(2,1)S(1)}, bf16[128,1536]{1,0:T(8,128)(2,1)S(1)}, u32[]{:S(2)}, u32[]{:S(2)}) %collective-permute-start.12) | collective-permute-done | bytes 393248 | tf_op jit(solution)/shard_map/ppermute | solution.py:157
  129.8 5.5 %stage.1.right_ref = bf16[2048,1536]{1,0:T(8,128)(2,1)} custom-call(bf16[128,1536]{1,0:T(8,128)(2,1)} %bitcast.14, bf16[256,1536]{1,0:T(8,128)(2,1)} %copy-done.1, bf16[128,1536]{1,0:T(8,128)(2,1)} %copy-done.2, bf16[128,1536]{1,0:T(8,128)(2,1)} %copy-done.6, bf16[256,1536]{1,0:T(8,128)(2,1)} %copy-done.3, bf16[128,1536]{1,0:T(8,128)(2,1)} %copy-done.9, ...), custom_call_target="tpu_custom_call" | custom-call | bytes 12582912 | tf_op jit(solution)/shard_map/stage/pallas_call | solution.py:68
  135.3 8.1 %all-gather.3.cloned.1.call-done = bf16[3072,512]{1,0:T(8,128)(2,1)} async-done(((bf16[768,512]{1,0:T(8,128)(2,1)}), bf16[3072,512]{1,0:T(8,128)(2,1)}) %all-gather.3.cloned.1.call-update) | async-done | bytes 3145744 | tf_op jit(solution)/shard_map/all_gather | solution.py:172
  143.4 10.0 %product.1 = (bf16[4,96,1536]{2,1,0:T(8,128)(2,1)S(1)}, bf16[4,96,1536]{2,1,0:T(8,128)(2,1)S(1)}) custom-call(s32[5]{0:T(128)S(1)} %stack.23.where, bf16[4,768,512]{2,1,0:T(8,128)(2,1)} %bitcast.15, bf16[2048,1536]{1,0:T(8,128)(2,1)} %stage.1.right_ref), custom_call_target="tpu_custom_call" | custom-call | flops 4831838208 | bytes 10485760 | tf_op jit(solution)/shard_map/product/pallas_call | solution.py:104
  153.5 2.4 %collective-permute-start.13 = (bf16[4,96,1536]{2,1,0:T(8,128)(2,1)S(1)}, bf16[4,96,1536]{2,1,0:T(8,128)(2,1)S(1)}, u32[]{:S(2)}, u32[]{:S(2)}) collective-permute-start(bf16[4,96,1536]{2,1,0:T(8,128)(2,1)S(1)} %get-tuple-element.36), channel_id=1, source_target_pairs={{0,1},{1,0},{2,3},{3,2},{4,5},{5,4},{6,7},{7,6},{8,9},{9,8},{10,11... | collective-permute-start | bytes 3538952 | tf_op jit(solution)/shard_map/ppermute | solution.py:184
  155.9 2.5 %collective-permute-done.13.got_ref = bf16[4,96,1536]{2,1,0:T(8,128)(2,1)S(1)} collective-permute-done((bf16[4,96,1536]{2,1,0:T(8,128)(2,1)S(1)}, bf16[4,96,1536]{2,1,0:T(8,128)(2,1)S(1)}, u32[]{:S(2)}, u32[]{:S(2)}) %collective-permute-start.13) | collective-permute-done | bytes 1179680 | tf_op jit(solution)/shard_map/ppermute | solution.py:184
  158.3 0.8 add_cores.1
  159.1 4.8 %collective-permute-start.14 = (bf16[96,1536]{1,0:T(8,128)(2,1)S(1)}, bf16[96,1536]{1,0:T(8,128)(2,1)S(1)}, u32[]{:S(2)}, u32[]{:S(2)}) collective-permute-start(bf16[96,1536]{1,0:T(8,128)(2,1)S(1)} %get-tuple-element.38), channel_id=1, source_target_pairs={{0,4},{2,6},{4,0},{6,2},{1,5},{3,7},{5,1},{7,3},{8,12},{10,14},{12... | collective-permute-start | bytes 884744 | tf_op jit(solution)/shard_map/ppermute | solution.py:157
  164.0 2.3 %collective-permute-start.15 = (bf16[96,1536]{1,0:T(8,128)(2,1)S(1)}, bf16[96,1536]{1,0:T(8,128)(2,1)S(1)}, u32[]{:S(2)}, u32[]{:S(2)}) collective-permute-start(bf16[96,1536]{1,0:T(8,128)(2,1)S(1)} %get-tuple-element.39), channel_id=1, source_target_pairs={{0,2},{2,4},{4,6},{6,0},{1,3},{3,5},{5,7},{7,1},{8,10},{10,12},{12... | collective-permute-start | bytes 884744 | tf_op jit(solution)/shard_map/ppermute | solution.py:157
  166.3 4.2 %collective-permute-start.16 = (bf16[96,1536]{1,0:T(8,128)(2,1)S(1)}, bf16[96,1536]{1,0:T(8,128)(2,1)S(1)}, u32[]{:S(2)}, u32[]{:S(2)}) collective-permute-start(bf16[96,1536]{1,0:T(8,128)(2,1)S(1)} %get-tuple-element.40), channel_id=1, source_target_pairs={{0,6},{2,0},{4,2},{6,4},{1,7},{3,1},{5,3},{7,5},{8,14},{10,8},{12,... | collective-permute-start | bytes 884744 | tf_op jit(solution)/shard_map/ppermute | solution.py:157
  170.8 7.0 %collective-permute-done.15.refs_1_ = bf16[96,1536]{1,0:T(8,128)(2,1)S(1)} collective-permute-done((bf16[96,1536]{1,0:T(8,128)(2,1)S(1)}, bf16[96,1536]{1,0:T(8,128)(2,1)S(1)}, u32[]{:S(2)}, u32[]{:S(2)}) %collective-permute-start.15) | collective-permute-done | bytes 294944 | tf_op jit(solution)/shard_map/ppermute | solution.py:157
  177.8 0.8 add_chips.1
  (40 shorter events, 1.3 us)
Async XLA Ops:
  6.5 136.9 %all-gather.3.cloned.1.call-start = ((), (), s32[]{:S(2)}) async-start(), calls=%async_computation | async-start | bytes 3932160 | tf_op jit(solution)/shard_map/all_gather | solution.py:172
  6.5 27.6 %collective-permute-start.1 = (bf16[128,1536]{1,0:T(8,128)(2,1)}, bf16[128,1536]{1,0:T(8,128)(2,1)S(1)}, u32[]{:S(2)}, u32[]{:S(2)}) collective-permute-start(bf16[128,1536]{1,0:T(8,128)(2,1)} %bitcast.9), channel_id=1, source_target_pairs={{0,8},{8,16},{16,24},{24,0},{1,9},{9,17},{17,25},{25,1},{2,10},{10... | collective-permute-start | bytes 1179656 | tf_op jit(solution)/shard_map/ppermute | solution.py:157
  16.2 43.5 %collective-permute-start = (bf16[128,1536]{1,0:T(8,128)(2,1)}, bf16[128,1536]{1,0:T(8,128)(2,1)S(1)}, u32[]{:S(2)}, u32[]{:S(2)}) collective-permute-start(bf16[128,1536]{1,0:T(8,128)(2,1)} %bitcast.10), channel_id=1, source_target_pairs={{0,24},{8,0},{16,8},{24,16},{1,25},{9,1},{17,9},{25,17},{2,26},{10... | collective-permute-start | bytes 1179656 | tf_op jit(solution)/shard_map/ppermute | solution.py:157
  21.8 38.0 %collective-permute-start.2 = (bf16[128,1536]{1,0:T(8,128)(2,1)}, bf16[128,1536]{1,0:T(8,128)(2,1)S(1)}, u32[]{:S(2)}, u32[]{:S(2)}) collective-permute-start(bf16[128,1536]{1,0:T(8,128)(2,1)} %bitcast.11), channel_id=1, source_target_pairs={{0,96},{32,0},{64,32},{96,64},{1,97},{33,1},{65,33},{97,65},{2,98}... | collective-permute-start | bytes 1179656 | tf_op jit(solution)/shard_map/ppermute | solution.py:157
  26.1 33.6 %collective-permute-start.3 = (bf16[128,1536]{1,0:T(8,128)(2,1)}, bf16[128,1536]{1,0:T(8,128)(2,1)S(1)}, u32[]{:S(2)}, u32[]{:S(2)}) collective-permute-start(bf16[128,1536]{1,0:T(8,128)(2,1)} %bitcast.12), channel_id=1, source_target_pairs={{0,64},{32,96},{64,0},{96,32},{1,65},{33,97},{65,1},{97,33},{2,66}... | collective-permute-start | bytes 1179656 | tf_op jit(solution)/shard_map/ppermute | solution.py:157
  28.6 31.2 %collective-permute-start.4 = (bf16[128,1536]{1,0:T(8,128)(2,1)}, bf16[128,1536]{1,0:T(8,128)(2,1)S(1)}, u32[]{:S(2)}, u32[]{:S(2)}) collective-permute-start(bf16[128,1536]{1,0:T(8,128)(2,1)} %bitcast.13), channel_id=1, source_target_pairs={{0,32},{32,64},{64,96},{96,0},{1,33},{33,65},{65,97},{97,1},{2,34}... | collective-permute-start | bytes 1179656 | tf_op jit(solution)/shard_map/ppermute | solution.py:157
  31.2 1.1 copy-start
  59.8 69.3 %copy-start.1 = (bf16[256,1536]{1,0:T(8,128)(2,1)}, bf16[256,1536]{1,0:T(8,128)(2,1)S(1)}, u32[]{:S(2)}) copy-start(bf16[256,1536]{1,0:T(8,128)(2,1)S(1)} %pad_maximum_fusion.refs_1_) | copy-start | bytes 2359300
  59.8 69.2 %copy-start.6 = (bf16[128,1536]{1,0:T(8,128)(2,1)}, bf16[128,1536]{1,0:T(8,128)(2,1)S(1)}, u32[]{:S(2)}) copy-start(bf16[128,1536]{1,0:T(8,128)(2,1)S(1)} %collective-permute-done.2.refs_3_) | copy-start | bytes 1179652
  59.8 69.2 %copy-start.7 = (bf16[128,1536]{1,0:T(8,128)(2,1)}, bf16[128,1536]{1,0:T(8,128)(2,1)S(1)}, u32[]{:S(2)}) copy-start(bf16[128,1536]{1,0:T(8,128)(2,1)S(1)} %collective-permute-done.3.refs_6_) | copy-start | bytes 1179652
  59.8 69.2 %copy-start.8 = (bf16[128,1536]{1,0:T(8,128)(2,1)}, bf16[128,1536]{1,0:T(8,128)(2,1)S(1)}, u32[]{:S(2)}) copy-start(bf16[128,1536]{1,0:T(8,128)(2,1)S(1)} %collective-permute-done.4.refs_9_) | copy-start | bytes 1179652
  59.8 32.5 %collective-permute-start.7 = (bf16[256,1536]{1,0:T(8,128)(2,1)S(1)}, bf16[256,1536]{1,0:T(8,128)(2,1)S(1)}, u32[]{:S(2)}, u32[]{:S(2)}) collective-permute-start(bf16[256,1536]{1,0:T(8,128)(2,1)S(1)} %pad_maximum_fusion.refs_1_), channel_id=1, source_target_pairs={{0,96},{32,0},{64,32},{96,64},{1,97},{33,1},{65,33},{97,65},{2,98}... | collective-permute-start | bytes 2359304 | tf_op jit(solution)/shard_map/ppermute | solution.py:157
  64.2 28.1 %collective-permute-start.8 = (bf16[256,1536]{1,0:T(8,128)(2,1)S(1)}, bf16[256,1536]{1,0:T(8,128)(2,1)S(1)}, u32[]{:S(2)}, u32[]{:S(2)}) collective-permute-start(bf16[256,1536]{1,0:T(8,128)(2,1)S(1)} %pad_maximum_fusion.refs_1_), channel_id=1, source_target_pairs={{0,64},{32,96},{64,0},{96,32},{1,65},{33,97},{65,1},{97,33},{2,66}... | collective-permute-start | bytes 2359304 | tf_op jit(solution)/shard_map/ppermute | solution.py:157
  66.7 37.4 %collective-permute-start.9 = (bf16[256,1536]{1,0:T(8,128)(2,1)S(1)}, bf16[256,1536]{1,0:T(8,128)(2,1)S(1)}, u32[]{:S(2)}, u32[]{:S(2)}) collective-permute-start(bf16[256,1536]{1,0:T(8,128)(2,1)S(1)} %pad_maximum_fusion.refs_1_), channel_id=1, source_target_pairs={{0,32},{32,64},{64,96},{96,0},{1,33},{33,65},{65,97},{97,1},{2,34}... | collective-permute-start | bytes 2359304 | tf_op jit(solution)/shard_map/ppermute | solution.py:157
  69.2 23.1 %collective-permute-start.5 = (bf16[64,1536]{1,0:T(8,128)(2,1)S(1)}, bf16[64,1536]{1,0:T(8,128)(2,1)S(1)}, u32[]{:S(2)}, u32[]{:S(2)}) collective-permute-start(bf16[64,1536]{1,0:T(8,128)(2,1)S(1)} %slice.8), channel_id=1, source_target_pairs={{0,8},{8,16},{16,24},{24,0},{1,9},{9,17},{17,25},{25,1},{2,10},{10... | collective-permute-start | bytes 589832 | tf_op jit(solution)/shard_map/ppermute | solution.py:157
  76.1 16.2 %collective-permute-start.6 = (bf16[64,1536]{1,0:T(8,128)(2,1)S(1)}, bf16[64,1536]{1,0:T(8,128)(2,1)S(1)}, u32[]{:S(2)}, u32[]{:S(2)}) collective-permute-start(bf16[64,1536]{1,0:T(8,128)(2,1)S(1)} %slice.9), channel_id=1, source_target_pairs={{0,24},{8,0},{16,8},{24,16},{1,25},{9,1},{17,9},{25,17},{2,26},{10... | collective-permute-start | bytes 589832 | tf_op jit(solution)/shard_map/ppermute | solution.py:157
  92.3 36.7 %copy-start.3 = (bf16[256,1536]{1,0:T(8,128)(2,1)}, bf16[256,1536]{1,0:T(8,128)(2,1)S(1)}, u32[]{:S(2)}) copy-start(bf16[256,1536]{1,0:T(8,128)(2,1)S(1)} %collective-permute-done.7.refs_4_) | copy-start | bytes 2359300
  92.3 36.7 %copy-start.4 = (bf16[256,1536]{1,0:T(8,128)(2,1)}, bf16[256,1536]{1,0:T(8,128)(2,1)S(1)}, u32[]{:S(2)}) copy-start(bf16[256,1536]{1,0:T(8,128)(2,1)S(1)} %collective-permute-done.8.refs_7_) | copy-start | bytes 2359300
  104.1 25.0 %copy-start.5 = (bf16[256,1536]{1,0:T(8,128)(2,1)}, bf16[256,1536]{1,0:T(8,128)(2,1)S(1)}, u32[]{:S(2)}) copy-start(bf16[256,1536]{1,0:T(8,128)(2,1)S(1)} %collective-permute-done.9.refs_10_) | copy-start | bytes 2359300
  104.1 25.0 %copy-start.2 = (bf16[128,1536]{1,0:T(8,128)(2,1)}, bf16[128,1536]{1,0:T(8,128)(2,1)S(1)}, u32[]{:S(2)}) copy-start(bf16[128,1536]{1,0:T(8,128)(2,1)S(1)} %constant_dynamic-update-slice_fusion.refs_2_) | copy-start | bytes 1179652
  104.1 12.3 %collective-permute-start.10 = (bf16[128,1536]{1,0:T(8,128)(2,1)S(1)}, bf16[128,1536]{1,0:T(8,128)(2,1)S(1)}, u32[]{:S(2)}, u32[]{:S(2)}) collective-permute-start(bf16[128,1536]{1,0:T(8,128)(2,1)S(1)} %constant_dynamic-update-slice_fusion.refs_2_), channel_id=1, source_target_pairs={{0,96},{32,0},{64,32},{96,64},{1,97},{33,1},{65,33},{97,65},{2,98}... | collective-permute-start | bytes 1179656 | tf_op jit(solution)/shard_map/ppermute | solution.py:157
  106.0 13.1 %collective-permute-start.11 = (bf16[128,1536]{1,0:T(8,128)(2,1)S(1)}, bf16[128,1536]{1,0:T(8,128)(2,1)S(1)}, u32[]{:S(2)}, u32[]{:S(2)}) collective-permute-start(bf16[128,1536]{1,0:T(8,128)(2,1)S(1)} %constant_dynamic-update-slice_fusion.refs_2_), channel_id=1, source_target_pairs={{0,64},{32,96},{64,0},{96,32},{1,65},{33,97},{65,1},{97,33},{2,66}... | collective-permute-start | bytes 1179656 | tf_op jit(solution)/shard_map/ppermute | solution.py:157
  108.5 20.5 %collective-permute-start.12 = (bf16[128,1536]{1,0:T(8,128)(2,1)S(1)}, bf16[128,1536]{1,0:T(8,128)(2,1)S(1)}, u32[]{:S(2)}, u32[]{:S(2)}) collective-permute-start(bf16[128,1536]{1,0:T(8,128)(2,1)S(1)} %constant_dynamic-update-slice_fusion.refs_2_), channel_id=1, source_target_pairs={{0,32},{32,64},{64,96},{96,0},{1,33},{33,65},{65,97},{97,1},{2,34}... | collective-permute-start | bytes 1179656 | tf_op jit(solution)/shard_map/ppermute | solution.py:157
  116.4 12.7 %copy-start.9 = (bf16[128,1536]{1,0:T(8,128)(2,1)}, bf16[128,1536]{1,0:T(8,128)(2,1)S(1)}, u32[]{:S(2)}) copy-start(bf16[128,1536]{1,0:T(8,128)(2,1)S(1)} %collective-permute-done.10.refs_5_) | copy-start | bytes 1179652
  119.1 10.0 %copy-start.10 = (bf16[128,1536]{1,0:T(8,128)(2,1)}, bf16[128,1536]{1,0:T(8,128)(2,1)S(1)}, u32[]{:S(2)}) copy-start(bf16[128,1536]{1,0:T(8,128)(2,1)S(1)} %collective-permute-done.11.refs_8_) | copy-start | bytes 1179652
  129.1 0.7 copy-start.11
  153.5 4.8 %collective-permute-start.13 = (bf16[4,96,1536]{2,1,0:T(8,128)(2,1)S(1)}, bf16[4,96,1536]{2,1,0:T(8,128)(2,1)S(1)}, u32[]{:S(2)}, u32[]{:S(2)}) collective-permute-start(bf16[4,96,1536]{2,1,0:T(8,128)(2,1)S(1)} %get-tuple-element.36), channel_id=1, source_target_pairs={{0,1},{1,0},{2,3},{3,2},{4,5},{5,4},{6,7},{7,6},{8,9},{9,8},{10,11... | collective-permute-start | bytes 3538952 | tf_op jit(solution)/shard_map/ppermute | solution.py:184
  159.1 11.6 %collective-permute-start.14 = (bf16[96,1536]{1,0:T(8,128)(2,1)S(1)}, bf16[96,1536]{1,0:T(8,128)(2,1)S(1)}, u32[]{:S(2)}, u32[]{:S(2)}) collective-permute-start(bf16[96,1536]{1,0:T(8,128)(2,1)S(1)} %get-tuple-element.38), channel_id=1, source_target_pairs={{0,4},{2,6},{4,0},{6,2},{1,5},{3,7},{5,1},{7,3},{8,12},{10,14},{12... | collective-permute-start | bytes 884744 | tf_op jit(solution)/shard_map/ppermute | solution.py:157
  164.0 13.8 %collective-permute-start.15 = (bf16[96,1536]{1,0:T(8,128)(2,1)S(1)}, bf16[96,1536]{1,0:T(8,128)(2,1)S(1)}, u32[]{:S(2)}, u32[]{:S(2)}) collective-permute-start(bf16[96,1536]{1,0:T(8,128)(2,1)S(1)} %get-tuple-element.39), channel_id=1, source_target_pairs={{0,2},{2,4},{4,6},{6,0},{1,3},{3,5},{5,7},{7,1},{8,10},{10,12},{12... | collective-permute-start | bytes 884744 | tf_op jit(solution)/shard_map/ppermute | solution.py:157
  166.3 11.5 %collective-permute-start.16 = (bf16[96,1536]{1,0:T(8,128)(2,1)S(1)}, bf16[96,1536]{1,0:T(8,128)(2,1)S(1)}, u32[]{:S(2)}, u32[]{:S(2)}) collective-permute-start(bf16[96,1536]{1,0:T(8,128)(2,1)S(1)} %get-tuple-element.40), channel_id=1, source_target_pairs={{0,6},{2,0},{4,2},{6,4},{1,7},{3,1},{5,3},{7,5},{8,14},{10,8},{12,... | collective-permute-start | bytes 884744 | tf_op jit(solution)/shard_map/ppermute | solution.py:157
Sparse Core Ops, SparseCore 0:
  60.0 83.4 all-gather.2

commit v5 on v4

--- a/solution.py
+++ b/solution.py
@@ -6,7 +6,6 @@
 from jax.sharding import Mesh, PartitionSpec as P
 
 F32, BF16 = jnp.float32, jnp.bfloat16
-TILE = 512
 CHUNK = 512
 
 
@@ -77,43 +76,52 @@
     )(*pieces)
 
 
-def product_kernel(where, a_ref, right_ref, other_ref, own_ref, left, sems):
-    copies = []
+def product_kernel(where, a_ref, grads_ref, other_ref, own_ref, left, right, total, sems):
+    waits = []
     for t in range(4):
         chunk = lax.rem(where[1] + t, 4)
-        copies.append(pltpu.make_async_copy(a_ref.at[chunk], left.at[:, pl.ds(t * CHUNK, CHUNK)], sems.at[t]))
-    for copy in copies:
-        copy.start()
-    for copy in copies:
-        copy.wait()
+        here = pl.ds(t * CHUNK, CHUNK)
+        waits.append([
+            pltpu.make_async_copy(a_ref.at[chunk], left.at[:, here], sems.at[t, 0]),
+            pltpu.make_async_copy(grads_ref.at[here], right.at[here], sems.at[t, 1]),
+        ])
+    for copies in waits:
+        for copy in copies:
+            copy.start()
     share = other_ref.shape[1]
-
-    def step(j, carry):
-        at = pl.ds(pl.multiple_of(j * TILE, TILE), TILE)
-        value = jnp.dot(left[...], right_ref[:, at], preferred_element_type=F32)
-        for y in range(4):
-            other_ref[y, :, at] = value[y * share : (y + 1) * share].astype(BF16)
-            own_ref[y, :, at] = value[(4 + y) * share : (5 + y) * share].astype(BF16)
-        return carry
-
-    lax.fori_loop(0, right_ref.shape[1] // TILE, step, 0)
-
-
-def product(where, inputs, right):
-    rows, (tokens, columns) = inputs.shape[1], right.shape
+    for first, last in ((0, 1), (1, 2), (2, 4)):
+        for copies in waits[first:last]:
+            for copy in copies:
+                copy.wait()
+        across = slice(first * CHUNK, last * CHUNK)
+        value = jnp.dot(left[:, across], right[across, :], preferred_element_type=F32)
+        if first > 0:
+            value = total[...] + value
+        if last < 4:
+            total[...] = value
+        else:
+            for y in range(4):
+                other_ref[y] = value[y * share : (y + 1) * share].astype(BF16)
+                own_ref[y] = value[(4 + y) * share : (5 + y) * share].astype(BF16)
+
+
+def product(where, inputs, grads):
+    rows, (tokens, columns) = inputs.shape[1], grads.shape
     return pl.pallas_call(
         product_kernel,
-        out_shape=[
-            jax.ShapeDtypeStruct((4, rows // 8, columns), BF16),
-            jax.ShapeDtypeStruct((4, rows // 8, columns), BF16),
+        out_shape=[jax.ShapeDtypeStruct((4, rows // 8, columns), BF16)] * 2,
+        in_specs=[smem_spec(), any_spec(), any_spec()],
+        out_specs=[vmem_spec(), vmem_spec()],
+        scratch_shapes=[
+            pltpu.VMEM((rows, tokens), BF16),
+            pltpu.VMEM((tokens, columns), BF16),
+            pltpu.VMEM((rows, columns), F32),
+            pltpu.SemaphoreType.DMA((4, 2)),
         ],
-        in_specs=[smem_spec(), any_spec(), vmem_spec()],
-        out_specs=[vmem_spec(), vmem_spec()],
-        scratch_shapes=[pltpu.VMEM((rows, tokens), BF16), pltpu.SemaphoreType.DMA((4,))],
         compiler_params=params(50),
-        cost_estimate=pl.CostEstimate(flops=2 * rows * columns * tokens, bytes_accessed=10 << 20, transcendentals=0),
+        cost_estimate=pl.CostEstimate(flops=2 * rows * columns * tokens, bytes_accessed=12 << 20, transcendentals=0),
         name="product",
-    )(where, inputs, right)
+    )(where, inputs, grads)
 
 
 def add_cores_kernel(where, own_ref, got_ref, *outs):

time: 186 us -> 184 us (0.989)
  Pallas kernels: 18.9 us -> 16.5 us
    pallas_call x1, Pallas kernels: 10 us -> 7.64 us  [product(): pl.pallas_call(product_kernel, out_shape=[jax.ShapeDtypeStruct((4, rows /...]
where the time goes in v5:
time: 184 us; the launch traced here: 183 us
  waiting for transfers between devices  86.8 us (47%)
  starting transfers between devices  63.9 us (35%)
  Pallas kernels  16.5 us (9%)
  between operations  13.7 us (7%)
  local copies, waits for them, and re-layouts  2.05 us (1%)
    ppermute x16, waiting for transfers between devices, ring(): return lax.ppermute(value, axis, [(i, (i + step) % 4) for i in range(4)])  76.2 us
    ppermute x16, starting transfers between devices, ring(): return lax.ppermute(value, axis, [(i, (i + step) % 4) for i in range(4)])  61.6 us
    all_gather x1, waiting for transfers between devices, shards(): inputs = lax.all_gather(turned, 'row', axis=0)  8.11 us
    pallas_call x1, Pallas kernels, product(): pl.pallas_call(product_kernel, out_shape=[jax.ShapeDtypeStruct((4, rows /...  7.64 us
    pallas_call x1, Pallas kernels, stage(): pl.pallas_call(stage_kernel, out_shape=jax.ShapeDtypeStruct((tokens, piec...  5.5 us
  transfers between devices with their start and end apart: 18, of which 10 were waited for; matrix products, arithmetic and copies ran while one was open for 0% of the time, Pallas kernels for 4%

profile of v5, /device:TPU:1, one launch (start us, length us, event | category | flops | bytes accessed | tf_op | source)
XLA Modules:
  0.0 183.1 jit_solution(8033250346600305206)
XLA Ops:
  6.5 9.6 %collective-permute-start.1 = (bf16[128,1536]{1,0:T(8,128)(2,1)}, bf16[128,1536]{1,0:T(8,128)(2,1)S(1)}, u32[]{:S(2)}, u32[]{:S(2)}) collective-permute-start(bf16[128,1536]{1,0:T(8,128)(2,1)} %bitcast.9), channel_id=1, source_target_pairs={{0,8},{8,16},{16,24},{24,0},{1,9},{9,17},{17,25},{25,1},{2,10},{10... | collective-permute-start | bytes 1179656 | tf_op jit(solution)/shard_map/ppermute | solution.py:165
  16.2 5.6 %collective-permute-start = (bf16[128,1536]{1,0:T(8,128)(2,1)}, bf16[128,1536]{1,0:T(8,128)(2,1)S(1)}, u32[]{:S(2)}, u32[]{:S(2)}) collective-permute-start(bf16[128,1536]{1,0:T(8,128)(2,1)} %bitcast.10), channel_id=1, source_target_pairs={{0,24},{8,0},{16,8},{24,16},{1,25},{9,1},{17,9},{25,17},{2,26},{10... | collective-permute-start | bytes 1179656 | tf_op jit(solution)/shard_map/ppermute | solution.py:165
  21.8 4.4 %collective-permute-start.2 = (bf16[128,1536]{1,0:T(8,128)(2,1)}, bf16[128,1536]{1,0:T(8,128)(2,1)S(1)}, u32[]{:S(2)}, u32[]{:S(2)}) collective-permute-start(bf16[128,1536]{1,0:T(8,128)(2,1)} %bitcast.11), channel_id=1, source_target_pairs={{0,96},{32,0},{64,32},{96,64},{1,97},{33,1},{65,33},{97,65},{2,98}... | collective-permute-start | bytes 1179656 | tf_op jit(solution)/shard_map/ppermute | solution.py:165
  26.1 2.4 %collective-permute-start.3 = (bf16[128,1536]{1,0:T(8,128)(2,1)}, bf16[128,1536]{1,0:T(8,128)(2,1)S(1)}, u32[]{:S(2)}, u32[]{:S(2)}) collective-permute-start(bf16[128,1536]{1,0:T(8,128)(2,1)} %bitcast.12), channel_id=1, source_target_pairs={{0,64},{32,96},{64,0},{96,32},{1,65},{33,97},{65,1},{97,33},{2,66}... | collective-permute-start | bytes 1179656 | tf_op jit(solution)/shard_map/ppermute | solution.py:165
  28.6 2.5 %collective-permute-start.4 = (bf16[128,1536]{1,0:T(8,128)(2,1)}, bf16[128,1536]{1,0:T(8,128)(2,1)S(1)}, u32[]{:S(2)}, u32[]{:S(2)}) collective-permute-start(bf16[128,1536]{1,0:T(8,128)(2,1)} %bitcast.13), channel_id=1, source_target_pairs={{0,32},{32,64},{64,96},{96,0},{1,33},{33,65},{65,97},{97,1},{2,34}... | collective-permute-start | bytes 1179656 | tf_op jit(solution)/shard_map/ppermute | solution.py:165
  31.2 1.1 copy-done
  32.3 1.8 turn.1
  34.1 25.6 %collective-permute-done = bf16[128,1536]{1,0:T(8,128)(2,1)S(1)} collective-permute-done((bf16[128,1536]{1,0:T(8,128)(2,1)}, bf16[128,1536]{1,0:T(8,128)(2,1)S(1)}, u32[]{:S(2)}, u32[]{:S(2)}) %collective-permute-start) | collective-permute-done | bytes 393248 | tf_op jit(solution)/shard_map/ppermute | solution.py:165
  59.8 4.4 %collective-permute-start.7 = (bf16[256,1536]{1,0:T(8,128)(2,1)S(1)}, bf16[256,1536]{1,0:T(8,128)(2,1)S(1)}, u32[]{:S(2)}, u32[]{:S(2)}) collective-permute-start(bf16[256,1536]{1,0:T(8,128)(2,1)S(1)} %pad_maximum_fusion.refs_1_), channel_id=1, source_target_pairs={{0,96},{32,0},{64,32},{96,64},{1,97},{33,1},{65,33},{97,65},{2,98}... | collective-permute-start | bytes 2359304 | tf_op jit(solution)/shard_map/ppermute | solution.py:165
  64.2 2.4 %collective-permute-start.8 = (bf16[256,1536]{1,0:T(8,128)(2,1)S(1)}, bf16[256,1536]{1,0:T(8,128)(2,1)S(1)}, u32[]{:S(2)}, u32[]{:S(2)}) collective-permute-start(bf16[256,1536]{1,0:T(8,128)(2,1)S(1)} %pad_maximum_fusion.refs_1_), channel_id=1, source_target_pairs={{0,64},{32,96},{64,0},{96,32},{1,65},{33,97},{65,1},{97,33},{2,66}... | collective-permute-start | bytes 2359304 | tf_op jit(solution)/shard_map/ppermute | solution.py:165
  66.7 2.5 %collective-permute-start.9 = (bf16[256,1536]{1,0:T(8,128)(2,1)S(1)}, bf16[256,1536]{1,0:T(8,128)(2,1)S(1)}, u32[]{:S(2)}, u32[]{:S(2)}) collective-permute-start(bf16[256,1536]{1,0:T(8,128)(2,1)S(1)} %pad_maximum_fusion.refs_1_), channel_id=1, source_target_pairs={{0,32},{32,64},{64,96},{96,0},{1,33},{33,65},{65,97},{97,1},{2,34}... | collective-permute-start | bytes 2359304 | tf_op jit(solution)/shard_map/ppermute | solution.py:165
  69.2 6.9 %collective-permute-start.5 = (bf16[64,1536]{1,0:T(8,128)(2,1)S(1)}, bf16[64,1536]{1,0:T(8,128)(2,1)S(1)}, u32[]{:S(2)}, u32[]{:S(2)}) collective-permute-start(bf16[64,1536]{1,0:T(8,128)(2,1)S(1)} %slice.8), channel_id=1, source_target_pairs={{0,8},{8,16},{16,24},{24,0},{1,9},{9,17},{17,25},{25,1},{2,10},{10... | collective-permute-start | bytes 589832 | tf_op jit(solution)/shard_map/ppermute | solution.py:165
  76.1 2.3 %collective-permute-start.6 = (bf16[64,1536]{1,0:T(8,128)(2,1)S(1)}, bf16[64,1536]{1,0:T(8,128)(2,1)S(1)}, u32[]{:S(2)}, u32[]{:S(2)}) collective-permute-start(bf16[64,1536]{1,0:T(8,128)(2,1)S(1)} %slice.9), channel_id=1, source_target_pairs={{0,24},{8,0},{16,8},{24,16},{1,25},{9,1},{17,9},{25,17},{2,26},{10... | collective-permute-start | bytes 589832 | tf_op jit(solution)/shard_map/ppermute | solution.py:165
  78.4 13.9 %collective-permute-done.5 = bf16[64,1536]{1,0:T(8,128)(2,1)S(1)} collective-permute-done((bf16[64,1536]{1,0:T(8,128)(2,1)S(1)}, bf16[64,1536]{1,0:T(8,128)(2,1)S(1)}, u32[]{:S(2)}, u32[]{:S(2)}) %collective-permute-start.5) | collective-permute-done | bytes 196640 | tf_op jit(solution)/shard_map/ppermute | solution.py:165
  92.3 11.7 %collective-permute-done.9.refs_10_ = bf16[256,1536]{1,0:T(8,128)(2,1)S(1)} collective-permute-done((bf16[256,1536]{1,0:T(8,128)(2,1)S(1)}, bf16[256,1536]{1,0:T(8,128)(2,1)S(1)}, u32[]{:S(2)}, u32[]{:S(2)}) %collective-permute-start.9) | collective-permute-done | bytes 786464 | tf_op jit(solution)/shard_map/ppermute | solution.py:165
  104.1 1.9 %collective-permute-start.10 = (bf16[128,1536]{1,0:T(8,128)(2,1)S(1)}, bf16[128,1536]{1,0:T(8,128)(2,1)S(1)}, u32[]{:S(2)}, u32[]{:S(2)}) collective-permute-start(bf16[128,1536]{1,0:T(8,128)(2,1)S(1)} %constant_dynamic-update-slice_fusion.refs_2_), channel_id=1, source_target_pairs={{0,96},{32,0},{64,32},{96,64},{1,97},{33,1},{65,33},{97,65},{2,98}... | collective-permute-start | bytes 1179656 | tf_op jit(solution)/shard_map/ppermute | solution.py:165
  106.0 2.4 %collective-permute-start.11 = (bf16[128,1536]{1,0:T(8,128)(2,1)S(1)}, bf16[128,1536]{1,0:T(8,128)(2,1)S(1)}, u32[]{:S(2)}, u32[]{:S(2)}) collective-permute-start(bf16[128,1536]{1,0:T(8,128)(2,1)S(1)} %constant_dynamic-update-slice_fusion.refs_2_), channel_id=1, source_target_pairs={{0,64},{32,96},{64,0},{96,32},{1,65},{33,97},{65,1},{97,33},{2,66}... | collective-permute-start | bytes 1179656 | tf_op jit(solution)/shard_map/ppermute | solution.py:165
  108.5 2.9 %collective-permute-start.12 = (bf16[128,1536]{1,0:T(8,128)(2,1)S(1)}, bf16[128,1536]{1,0:T(8,128)(2,1)S(1)}, u32[]{:S(2)}, u32[]{:S(2)}) collective-permute-start(bf16[128,1536]{1,0:T(8,128)(2,1)S(1)} %constant_dynamic-update-slice_fusion.refs_2_), channel_id=1, source_target_pairs={{0,32},{32,64},{64,96},{96,0},{1,33},{33,65},{65,97},{97,1},{2,34}... | collective-permute-start | bytes 1179656 | tf_op jit(solution)/shard_map/ppermute | solution.py:165
  111.3 5.1 %collective-permute-done.10.refs_5_ = bf16[128,1536]{1,0:T(8,128)(2,1)S(1)} collective-permute-done((bf16[128,1536]{1,0:T(8,128)(2,1)S(1)}, bf16[128,1536]{1,0:T(8,128)(2,1)S(1)}, u32[]{:S(2)}, u32[]{:S(2)}) %collective-permute-start.10) | collective-permute-done | bytes 393248 | tf_op jit(solution)/shard_map/ppermute | solution.py:165
  116.4 2.7 %collective-permute-done.11.refs_8_ = bf16[128,1536]{1,0:T(8,128)(2,1)S(1)} collective-permute-done((bf16[128,1536]{1,0:T(8,128)(2,1)S(1)}, bf16[128,1536]{1,0:T(8,128)(2,1)S(1)}, u32[]{:S(2)}, u32[]{:S(2)}) %collective-permute-start.11) | collective-permute-done | bytes 393248 | tf_op jit(solution)/shard_map/ppermute | solution.py:165
  119.1 9.9 %collective-permute-done.12.refs_11_ = bf16[128,1536]{1,0:T(8,128)(2,1)S(1)} collective-permute-done((bf16[128,1536]{1,0:T(8,128)(2,1)S(1)}, bf16[128,1536]{1,0:T(8,128)(2,1)S(1)}, u32[]{:S(2)}, u32[]{:S(2)}) %collective-permute-start.12) | collective-permute-done | bytes 393248 | tf_op jit(solution)/shard_map/ppermute | solution.py:165
  129.8 5.5 %stage.1.grads_ref = bf16[2048,1536]{1,0:T(8,128)(2,1)} custom-call(bf16[128,1536]{1,0:T(8,128)(2,1)} %bitcast.14, bf16[256,1536]{1,0:T(8,128)(2,1)} %copy-done.1, bf16[128,1536]{1,0:T(8,128)(2,1)} %copy-done.2, bf16[128,1536]{1,0:T(8,128)(2,1)} %copy-done.6, bf16[256,1536]{1,0:T(8,128)(2,1)} %copy-done.3, bf16[128,1536]{1,0:T(8,128)(2,1)} %copy-done.9, ...), custom_call_target="tpu_custom_call" | custom-call | bytes 12582912 | tf_op jit(solution)/shard_map/stage/pallas_call | solution.py:67
  135.3 8.1 %all-gather.3.cloned.1.call-done = bf16[3072,512]{1,0:T(8,128)(2,1)} async-done(((bf16[768,512]{1,0:T(8,128)(2,1)}), bf16[3072,512]{1,0:T(8,128)(2,1)}) %all-gather.3.cloned.1.call-update) | async-done | bytes 3145744 | tf_op jit(solution)/shard_map/all_gather | solution.py:180
  143.4 7.6 %product.1 = (bf16[4,96,1536]{2,1,0:T(8,128)(2,1)S(1)}, bf16[4,96,1536]{2,1,0:T(8,128)(2,1)S(1)}) custom-call(s32[5]{0:T(128)S(1)} %stack.23.where, bf16[4,768,512]{2,1,0:T(8,128)(2,1)} %bitcast.15, bf16[2048,1536]{1,0:T(8,128)(2,1)} %stage.1.grads_ref), custom_call_target="tpu_custom_call" | custom-call | flops 4831838208 | bytes 12582912 | tf_op jit(solution)/shard_map/product/pallas_call | solution.py:110
  151.1 2.4 %collective-permute-start.13 = (bf16[4,96,1536]{2,1,0:T(8,128)(2,1)S(1)}, bf16[4,96,1536]{2,1,0:T(8,128)(2,1)S(1)}, u32[]{:S(2)}, u32[]{:S(2)}) collective-permute-start(bf16[4,96,1536]{2,1,0:T(8,128)(2,1)S(1)} %get-tuple-element.36), channel_id=1, source_target_pairs={{0,1},{1,0},{2,3},{3,2},{4,5},{5,4},{6,7},{7,6},{8,9},{9,8},{10,11... | collective-permute-start | bytes 3538952 | tf_op jit(solution)/shard_map/ppermute | solution.py:192
  153.5 2.5 %collective-permute-done.13.got_ref = bf16[4,96,1536]{2,1,0:T(8,128)(2,1)S(1)} collective-permute-done((bf16[4,96,1536]{2,1,0:T(8,128)(2,1)S(1)}, bf16[4,96,1536]{2,1,0:T(8,128)(2,1)S(1)}, u32[]{:S(2)}, u32[]{:S(2)}) %collective-permute-start.13) | collective-permute-done | bytes 1179680 | tf_op jit(solution)/shard_map/ppermute | solution.py:192
  155.9 0.8 add_cores.1
  156.7 4.8 %collective-permute-start.14 = (bf16[96,1536]{1,0:T(8,128)(2,1)S(1)}, bf16[96,1536]{1,0:T(8,128)(2,1)S(1)}, u32[]{:S(2)}, u32[]{:S(2)}) collective-permute-start(bf16[96,1536]{1,0:T(8,128)(2,1)S(1)} %get-tuple-element.38), channel_id=1, source_target_pairs={{0,4},{2,6},{4,0},{6,2},{1,5},{3,7},{5,1},{7,3},{8,12},{10,14},{12... | collective-permute-start | bytes 884744 | tf_op jit(solution)/shard_map/ppermute | solution.py:165
  161.6 2.3 %collective-permute-start.15 = (bf16[96,1536]{1,0:T(8,128)(2,1)S(1)}, bf16[96,1536]{1,0:T(8,128)(2,1)S(1)}, u32[]{:S(2)}, u32[]{:S(2)}) collective-permute-start(bf16[96,1536]{1,0:T(8,128)(2,1)S(1)} %get-tuple-element.39), channel_id=1, source_target_pairs={{0,2},{2,4},{4,6},{6,0},{1,3},{3,5},{5,7},{7,1},{8,10},{10,12},{12... | collective-permute-start | bytes 884744 | tf_op jit(solution)/shard_map/ppermute | solution.py:165
  163.9 4.2 %collective-permute-start.16 = (bf16[96,1536]{1,0:T(8,128)(2,1)S(1)}, bf16[96,1536]{1,0:T(8,128)(2,1)S(1)}, u32[]{:S(2)}, u32[]{:S(2)}) collective-permute-start(bf16[96,1536]{1,0:T(8,128)(2,1)S(1)} %get-tuple-element.40), channel_id=1, source_target_pairs={{0,6},{2,0},{4,2},{6,4},{1,7},{3,1},{5,3},{7,5},{8,14},{10,8},{12,... | collective-permute-start | bytes 884744 | tf_op jit(solution)/shard_map/ppermute | solution.py:165
  168.4 7.0 %collective-permute-done.15.refs_1_ = bf16[96,1536]{1,0:T(8,128)(2,1)S(1)} collective-permute-done((bf16[96,1536]{1,0:T(8,128)(2,1)S(1)}, bf16[96,1536]{1,0:T(8,128)(2,1)S(1)}, u32[]{:S(2)}, u32[]{:S(2)}) %collective-permute-start.15) | collective-permute-done | bytes 294944 | tf_op jit(solution)/shard_map/ppermute | solution.py:165
  175.4 0.8 add_chips.1
  (40 shorter events, 1.3 us)
Async XLA Ops:
  6.5 136.9 %all-gather.3.cloned.1.call-start = ((), (), s32[]{:S(2)}) async-start(), calls=%async_computation | async-start | bytes 3932160 | tf_op jit(solution)/shard_map/all_gather | solution.py:180
  6.5 27.6 %collective-permute-start.1 = (bf16[128,1536]{1,0:T(8,128)(2,1)}, bf16[128,1536]{1,0:T(8,128)(2,1)S(1)}, u32[]{:S(2)}, u32[]{:S(2)}) collective-permute-start(bf16[128,1536]{1,0:T(8,128)(2,1)} %bitcast.9), channel_id=1, source_target_pairs={{0,8},{8,16},{16,24},{24,0},{1,9},{9,17},{17,25},{25,1},{2,10},{10... | collective-permute-start | bytes 1179656 | tf_op jit(solution)/shard_map/ppermute | solution.py:165
  16.2 43.5 %collective-permute-start = (bf16[128,1536]{1,0:T(8,128)(2,1)}, bf16[128,1536]{1,0:T(8,128)(2,1)S(1)}, u32[]{:S(2)}, u32[]{:S(2)}) collective-permute-start(bf16[128,1536]{1,0:T(8,128)(2,1)} %bitcast.10), channel_id=1, source_target_pairs={{0,24},{8,0},{16,8},{24,16},{1,25},{9,1},{17,9},{25,17},{2,26},{10... | collective-permute-start | bytes 1179656 | tf_op jit(solution)/shard_map/ppermute | solution.py:165
  21.8 38.0 %collective-permute-start.2 = (bf16[128,1536]{1,0:T(8,128)(2,1)}, bf16[128,1536]{1,0:T(8,128)(2,1)S(1)}, u32[]{:S(2)}, u32[]{:S(2)}) collective-permute-start(bf16[128,1536]{1,0:T(8,128)(2,1)} %bitcast.11), channel_id=1, source_target_pairs={{0,96},{32,0},{64,32},{96,64},{1,97},{33,1},{65,33},{97,65},{2,98}... | collective-permute-start | bytes 1179656 | tf_op jit(solution)/shard_map/ppermute | solution.py:165
  26.1 33.6 %collective-permute-start.3 = (bf16[128,1536]{1,0:T(8,128)(2,1)}, bf16[128,1536]{1,0:T(8,128)(2,1)S(1)}, u32[]{:S(2)}, u32[]{:S(2)}) collective-permute-start(bf16[128,1536]{1,0:T(8,128)(2,1)} %bitcast.12), channel_id=1, source_target_pairs={{0,64},{32,96},{64,0},{96,32},{1,65},{33,97},{65,1},{97,33},{2,66}... | collective-permute-start | bytes 1179656 | tf_op jit(solution)/shard_map/ppermute | solution.py:165
  28.6 31.2 %collective-permute-start.4 = (bf16[128,1536]{1,0:T(8,128)(2,1)}, bf16[128,1536]{1,0:T(8,128)(2,1)S(1)}, u32[]{:S(2)}, u32[]{:S(2)}) collective-permute-start(bf16[128,1536]{1,0:T(8,128)(2,1)} %bitcast.13), channel_id=1, source_target_pairs={{0,32},{32,64},{64,96},{96,0},{1,33},{33,65},{65,97},{97,1},{2,34}... | collective-permute-start | bytes 1179656 | tf_op jit(solution)/shard_map/ppermute | solution.py:165
  31.2 1.1 copy-start
  59.8 69.3 %copy-start.1 = (bf16[256,1536]{1,0:T(8,128)(2,1)}, bf16[256,1536]{1,0:T(8,128)(2,1)S(1)}, u32[]{:S(2)}) copy-start(bf16[256,1536]{1,0:T(8,128)(2,1)S(1)} %pad_maximum_fusion.refs_1_) | copy-start | bytes 2359300
  59.8 69.2 %copy-start.6 = (bf16[128,1536]{1,0:T(8,128)(2,1)}, bf16[128,1536]{1,0:T(8,128)(2,1)S(1)}, u32[]{:S(2)}) copy-start(bf16[128,1536]{1,0:T(8,128)(2,1)S(1)} %collective-permute-done.2.refs_3_) | copy-start | bytes 1179652
  59.8 69.2 %copy-start.7 = (bf16[128,1536]{1,0:T(8,128)(2,1)}, bf16[128,1536]{1,0:T(8,128)(2,1)S(1)}, u32[]{:S(2)}) copy-start(bf16[128,1536]{1,0:T(8,128)(2,1)S(1)} %collective-permute-done.3.refs_6_) | copy-start | bytes 1179652
  59.8 69.2 %copy-start.8 = (bf16[128,1536]{1,0:T(8,128)(2,1)}, bf16[128,1536]{1,0:T(8,128)(2,1)S(1)}, u32[]{:S(2)}) copy-start(bf16[128,1536]{1,0:T(8,128)(2,1)S(1)} %collective-permute-done.4.refs_9_) | copy-start | bytes 1179652
  59.8 32.5 %collective-permute-start.7 = (bf16[256,1536]{1,0:T(8,128)(2,1)S(1)}, bf16[256,1536]{1,0:T(8,128)(2,1)S(1)}, u32[]{:S(2)}, u32[]{:S(2)}) collective-permute-start(bf16[256,1536]{1,0:T(8,128)(2,1)S(1)} %pad_maximum_fusion.refs_1_), channel_id=1, source_target_pairs={{0,96},{32,0},{64,32},{96,64},{1,97},{33,1},{65,33},{97,65},{2,98}... | collective-permute-start | bytes 2359304 | tf_op jit(solution)/shard_map/ppermute | solution.py:165
  64.2 28.1 %collective-permute-start.8 = (bf16[256,1536]{1,0:T(8,128)(2,1)S(1)}, bf16[256,1536]{1,0:T(8,128)(2,1)S(1)}, u32[]{:S(2)}, u32[]{:S(2)}) collective-permute-start(bf16[256,1536]{1,0:T(8,128)(2,1)S(1)} %pad_maximum_fusion.refs_1_), channel_id=1, source_target_pairs={{0,64},{32,96},{64,0},{96,32},{1,65},{33,97},{65,1},{97,33},{2,66}... | collective-permute-start | bytes 2359304 | tf_op jit(solution)/shard_map/ppermute | solution.py:165
  66.7 37.4 %collective-permute-start.9 = (bf16[256,1536]{1,0:T(8,128)(2,1)S(1)}, bf16[256,1536]{1,0:T(8,128)(2,1)S(1)}, u32[]{:S(2)}, u32[]{:S(2)}) collective-permute-start(bf16[256,1536]{1,0:T(8,128)(2,1)S(1)} %pad_maximum_fusion.refs_1_), channel_id=1, source_target_pairs={{0,32},{32,64},{64,96},{96,0},{1,33},{33,65},{65,97},{97,1},{2,34}... | collective-permute-start | bytes 2359304 | tf_op jit(solution)/shard_map/ppermute | solution.py:165
  69.2 23.1 %collective-permute-start.5 = (bf16[64,1536]{1,0:T(8,128)(2,1)S(1)}, bf16[64,1536]{1,0:T(8,128)(2,1)S(1)}, u32[]{:S(2)}, u32[]{:S(2)}) collective-permute-start(bf16[64,1536]{1,0:T(8,128)(2,1)S(1)} %slice.8), channel_id=1, source_target_pairs={{0,8},{8,16},{16,24},{24,0},{1,9},{9,17},{17,25},{25,1},{2,10},{10... | collective-permute-start | bytes 589832 | tf_op jit(solution)/shard_map/ppermute | solution.py:165
  76.1 16.2 %collective-permute-start.6 = (bf16[64,1536]{1,0:T(8,128)(2,1)S(1)}, bf16[64,1536]{1,0:T(8,128)(2,1)S(1)}, u32[]{:S(2)}, u32[]{:S(2)}) collective-permute-start(bf16[64,1536]{1,0:T(8,128)(2,1)S(1)} %slice.9), channel_id=1, source_target_pairs={{0,24},{8,0},{16,8},{24,16},{1,25},{9,1},{17,9},{25,17},{2,26},{10... | collective-permute-start | bytes 589832 | tf_op jit(solution)/shard_map/ppermute | solution.py:165
  92.3 36.7 %copy-start.3 = (bf16[256,1536]{1,0:T(8,128)(2,1)}, bf16[256,1536]{1,0:T(8,128)(2,1)S(1)}, u32[]{:S(2)}) copy-start(bf16[256,1536]{1,0:T(8,128)(2,1)S(1)} %collective-permute-done.7.refs_4_) | copy-start | bytes 2359300
  92.3 36.7 %copy-start.4 = (bf16[256,1536]{1,0:T(8,128)(2,1)}, bf16[256,1536]{1,0:T(8,128)(2,1)S(1)}, u32[]{:S(2)}) copy-start(bf16[256,1536]{1,0:T(8,128)(2,1)S(1)} %collective-permute-done.8.refs_7_) | copy-start | bytes 2359300
  104.1 25.0 %copy-start.5 = (bf16[256,1536]{1,0:T(8,128)(2,1)}, bf16[256,1536]{1,0:T(8,128)(2,1)S(1)}, u32[]{:S(2)}) copy-start(bf16[256,1536]{1,0:T(8,128)(2,1)S(1)} %collective-permute-done.9.refs_10_) | copy-start | bytes 2359300
  104.1 25.0 %copy-start.2 = (bf16[128,1536]{1,0:T(8,128)(2,1)}, bf16[128,1536]{1,0:T(8,128)(2,1)S(1)}, u32[]{:S(2)}) copy-start(bf16[128,1536]{1,0:T(8,128)(2,1)S(1)} %constant_dynamic-update-slice_fusion.refs_2_) | copy-start | bytes 1179652
  104.1 12.3 %collective-permute-start.10 = (bf16[128,1536]{1,0:T(8,128)(2,1)S(1)}, bf16[128,1536]{1,0:T(8,128)(2,1)S(1)}, u32[]{:S(2)}, u32[]{:S(2)}) collective-permute-start(bf16[128,1536]{1,0:T(8,128)(2,1)S(1)} %constant_dynamic-update-slice_fusion.refs_2_), channel_id=1, source_target_pairs={{0,96},{32,0},{64,32},{96,64},{1,97},{33,1},{65,33},{97,65},{2,98}... | collective-permute-start | bytes 1179656 | tf_op jit(solution)/shard_map/ppermute | solution.py:165
  106.0 13.1 %collective-permute-start.11 = (bf16[128,1536]{1,0:T(8,128)(2,1)S(1)}, bf16[128,1536]{1,0:T(8,128)(2,1)S(1)}, u32[]{:S(2)}, u32[]{:S(2)}) collective-permute-start(bf16[128,1536]{1,0:T(8,128)(2,1)S(1)} %constant_dynamic-update-slice_fusion.refs_2_), channel_id=1, source_target_pairs={{0,64},{32,96},{64,0},{96,32},{1,65},{33,97},{65,1},{97,33},{2,66}... | collective-permute-start | bytes 1179656 | tf_op jit(solution)/shard_map/ppermute | solution.py:165
  108.5 20.5 %collective-permute-start.12 = (bf16[128,1536]{1,0:T(8,128)(2,1)S(1)}, bf16[128,1536]{1,0:T(8,128)(2,1)S(1)}, u32[]{:S(2)}, u32[]{:S(2)}) collective-permute-start(bf16[128,1536]{1,0:T(8,128)(2,1)S(1)} %constant_dynamic-update-slice_fusion.refs_2_), channel_id=1, source_target_pairs={{0,32},{32,64},{64,96},{96,0},{1,33},{33,65},{65,97},{97,1},{2,34}... | collective-permute-start | bytes 1179656 | tf_op jit(solution)/shard_map/ppermute | solution.py:165
  116.4 12.7 %copy-start.9 = (bf16[128,1536]{1,0:T(8,128)(2,1)}, bf16[128,1536]{1,0:T(8,128)(2,1)S(1)}, u32[]{:S(2)}) copy-start(bf16[128,1536]{1,0:T(8,128)(2,1)S(1)} %collective-permute-done.10.refs_5_) | copy-start | bytes 1179652
  119.1 10.0 %copy-start.10 = (bf16[128,1536]{1,0:T(8,128)(2,1)}, bf16[128,1536]{1,0:T(8,128)(2,1)S(1)}, u32[]{:S(2)}) copy-start(bf16[128,1536]{1,0:T(8,128)(2,1)S(1)} %collective-permute-done.11.refs_8_) | copy-start | bytes 1179652
  129.1 0.7 copy-start.11
  151.1 4.8 %collective-permute-start.13 = (bf16[4,96,1536]{2,1,0:T(8,128)(2,1)S(1)}, bf16[4,96,1536]{2,1,0:T(8,128)(2,1)S(1)}, u32[]{:S(2)}, u32[]{:S(2)}) collective-permute-start(bf16[4,96,1536]{2,1,0:T(8,128)(2,1)S(1)} %get-tuple-element.36), channel_id=1, source_target_pairs={{0,1},{1,0},{2,3},{3,2},{4,5},{5,4},{6,7},{7,6},{8,9},{9,8},{10,11... | collective-permute-start | bytes 3538952 | tf_op jit(solution)/shard_map/ppermute | solution.py:192
  156.7 11.6 %collective-permute-start.14 = (bf16[96,1536]{1,0:T(8,128)(2,1)S(1)}, bf16[96,1536]{1,0:T(8,128)(2,1)S(1)}, u32[]{:S(2)}, u32[]{:S(2)}) collective-permute-start(bf16[96,1536]{1,0:T(8,128)(2,1)S(1)} %get-tuple-element.38), channel_id=1, source_target_pairs={{0,4},{2,6},{4,0},{6,2},{1,5},{3,7},{5,1},{7,3},{8,12},{10,14},{12... | collective-permute-start | bytes 884744 | tf_op jit(solution)/shard_map/ppermute | solution.py:165
  161.6 13.8 %collective-permute-start.15 = (bf16[96,1536]{1,0:T(8,128)(2,1)S(1)}, bf16[96,1536]{1,0:T(8,128)(2,1)S(1)}, u32[]{:S(2)}, u32[]{:S(2)}) collective-permute-start(bf16[96,1536]{1,0:T(8,128)(2,1)S(1)} %get-tuple-element.39), channel_id=1, source_target_pairs={{0,2},{2,4},{4,6},{6,0},{1,3},{3,5},{5,7},{7,1},{8,10},{10,12},{12... | collective-permute-start | bytes 884744 | tf_op jit(solution)/shard_map/ppermute | solution.py:165
  163.9 11.5 %collective-permute-start.16 = (bf16[96,1536]{1,0:T(8,128)(2,1)S(1)}, bf16[96,1536]{1,0:T(8,128)(2,1)S(1)}, u32[]{:S(2)}, u32[]{:S(2)}) collective-permute-start(bf16[96,1536]{1,0:T(8,128)(2,1)S(1)} %get-tuple-element.40), channel_id=1, source_target_pairs={{0,6},{2,0},{4,2},{6,4},{1,7},{3,1},{5,3},{7,5},{8,14},{10,8},{12,... | collective-permute-start | bytes 884744 | tf_op jit(solution)/shard_map/ppermute | solution.py:165
Sparse Core Ops, SparseCore 0:
  60.0 83.4 all-gather.2

commit v6 on v5

--- a/solution.py
+++ b/solution.py
@@ -50,30 +50,33 @@
     )(where, a)
 
 
-def stage_kernel(*refs):
+def stage_kernel(where, own_ref, *refs):
     pieces, (out_ref, sems) = refs[:-2], refs[-2:]
-    at, copies = 0, []
-    for i, ref in enumerate(pieces):
-        copies.append(pltpu.make_async_copy(ref, out_ref.at[pl.ds(at, ref.shape[0])], sems.at[i]))
-        at += ref.shape[0]
+    copies = []
+    for t in range(4):
+        chunk = lax.rem(where[1] + t, 4)
+        at = t * CHUNK
+        for i, ref in enumerate((own_ref.at[chunk], *pieces[2 * t : 2 * t + 2])):
+            size = (128, 256, 128)[i]
+            copies.append(pltpu.make_async_copy(ref, out_ref.at[pl.ds(at, size)], sems.at[t, i]))
+            at += size
     for copy in copies:
         copy.start()
     for copy in copies:
         copy.wait()
 
 
-def stage(pieces):
-    tokens = sum(p.shape[0] for p in pieces)
+def stage(where, owns, pieces):
     return pl.pallas_call(
         stage_kernel,
-        out_shape=jax.ShapeDtypeStruct((tokens, pieces[0].shape[1]), BF16),
-        in_specs=[any_spec()] * len(pieces),
+        out_shape=jax.ShapeDtypeStruct((4 * CHUNK, owns.shape[-1]), BF16),
+        in_specs=[smem_spec()] + [any_spec()] * (1 + len(pieces)),
         out_specs=vmem_spec(),
-        scratch_shapes=[pltpu.SemaphoreType.DMA((len(pieces),))],
+        scratch_shapes=[pltpu.SemaphoreType.DMA((4, 3))],
         compiler_params=params(54),
         cost_estimate=pl.CostEstimate(flops=0, bytes_accessed=12 << 20, transcendentals=0),
         name="stage",
-    )(*pieces)
+    )(where, owns, *pieces)
 
 
 def product_kernel(where, a_ref, grads_ref, other_ref, own_ref, left, right, total, sems):
@@ -171,11 +174,12 @@
     half = grads.shape[0] // 2
 
     turned = turn(where, activations[0])
+
+    owns = lax.all_gather(grads, "x", axis=0)
     before = ring(grads, "z_hi", 1)
     after = ring(grads, "z_hi", -1)
-    owns = [ring(grads, "x", -t) for t in (1, 2, 3)]
     near = jnp.concatenate([after, before])
-    near, top, bottom, turned, *owns = lax.optimization_barrier((near, before[:half], after[half:], turned, *owns))
+    near, top, bottom, turned = lax.optimization_barrier((near, before[:half], after[half:], turned))
 
     inputs = lax.all_gather(turned, "row", axis=0)
 
@@ -187,7 +191,7 @@
     far = jnp.concatenate([far_top, far_bottom])
     fars = [ring(far, "x", -t) for t in (1, 2, 3)]
 
-    right = stage([grads, near, far] + [p for group in zip(owns, nears, fars) for p in group])
+    right = stage(where, owns, [p for group in zip([near] + nears, [far] + fars) for p in group])
     other, mine = product(where, inputs, right)
     got = lax.ppermute(other, "core", [(0, 1), (1, 0)])
     kept, *sends = add_cores(where, mine, got)

time: 184 us -> 184 us (level)
  waiting for transfers between devices: 86.8 us -> 96.1 us
  starting transfers between devices: 63.9 us -> 54.8 us
    ppermute x16 -> x13, starting transfers between devices: 61.6 us -> 52.4 us  [ring(): return lax.ppermute(value, axis, [(i, (i + step) % 4) for i in range(4)])]
    ppermute x16 -> x13, waiting for transfers between devices: 76.2 us -> 84.8 us  [ring(): return lax.ppermute(value, axis, [(i, (i + step) % 4) for i in range(4)])]
  transfers between devices with their start and end apart: 18 -> 16, of which waited for: 10 -> 11; matrix products, arithmetic and copies ran while one was open for 0% -> 0% of each run, Pallas kernels for 4% -> 4%
where the time goes in v6:
time: 184 us
  waiting for transfers between devices  96.1 us (52%)
  starting transfers between devices  54.8 us (30%)
  Pallas kernels  17.2 us (9%)
  between operations  13.7 us (7%)
  local copies, waits for them, and re-layouts  2.05 us (1%)
    ppermute x13, waiting for transfers between devices, ring(): return lax.ppermute(value, axis, [(i, (i + step) % 4) for i in range(4)])  84.8 us
    ppermute x13, starting transfers between devices, ring(): return lax.ppermute(value, axis, [(i, (i + step) % 4) for i in range(4)])  52.4 us
    all_gather x1, waiting for transfers between devices, shards(): inputs = lax.all_gather(turned, 'row', axis=0)  8.08 us
    pallas_call x1, Pallas kernels, product(): pl.pallas_call(product_kernel, out_shape=[jax.ShapeDtypeStruct((4, rows /...  7.64 us
    pallas_call x1, Pallas kernels, stage(): pl.pallas_call(stage_kernel, out_shape=jax.ShapeDtypeStruct((4 * CHUNK, o...  6.17 us
  transfers between devices with their start and end apart: 16, of which 11 were waited for; matrix products, arithmetic and copies ran while one was open for 0% of the time, Pallas kernels for 4%

profile of v6, /device:TPU:1, one launch (start us, length us, event | category | flops | bytes accessed | tf_op | source)
XLA Modules:
  0.0 183.8 jit_solution(8794309880466522353)
XLA Ops:
  6.5 0.7 all-gather.4.cloned.1.call-update
  7.3 9.6 %collective-permute-start.1 = (bf16[128,1536]{1,0:T(8,128)(2,1)}, bf16[128,1536]{1,0:T(8,128)(2,1)S(1)}, u32[]{:S(2)}, u32[]{:S(2)}) collective-permute-start(bf16[128,1536]{1,0:T(8,128)(2,1)} %bitcast.9), channel_id=1, source_target_pairs={{0,8},{8,16},{16,24},{24,0},{1,9},{9,17},{17,25},{25,1},{2,10},{10... | collective-permute-start | bytes 1179656 | tf_op jit(solution)/shard_map/ppermute | solution.py:168
  17.0 5.6 %collective-permute-start = (bf16[128,1536]{1,0:T(8,128)(2,1)}, bf16[128,1536]{1,0:T(8,128)(2,1)S(1)}, u32[]{:S(2)}, u32[]{:S(2)}) collective-permute-start(bf16[128,1536]{1,0:T(8,128)(2,1)} %bitcast.10), channel_id=1, source_target_pairs={{0,24},{8,0},{16,8},{24,16},{1,25},{9,1},{17,9},{25,17},{2,26},{10... | collective-permute-start | bytes 1179656 | tf_op jit(solution)/shard_map/ppermute | solution.py:168
  22.6 1.1 copy-done
  23.8 1.7 turn.1
  25.5 8.4 %collective-permute-done.1 = bf16[128,1536]{1,0:T(8,128)(2,1)S(1)} collective-permute-done((bf16[128,1536]{1,0:T(8,128)(2,1)}, bf16[128,1536]{1,0:T(8,128)(2,1)S(1)}, u32[]{:S(2)}, u32[]{:S(2)}) %collective-permute-start.1) | collective-permute-done | bytes 393248 | tf_op jit(solution)/shard_map/ppermute | solution.py:168
  33.9 26.6 %collective-permute-done = bf16[128,1536]{1,0:T(8,128)(2,1)S(1)} collective-permute-done((bf16[128,1536]{1,0:T(8,128)(2,1)}, bf16[128,1536]{1,0:T(8,128)(2,1)S(1)}, u32[]{:S(2)}, u32[]{:S(2)}) %collective-permute-start) | collective-permute-done | bytes 393248 | tf_op jit(solution)/shard_map/ppermute | solution.py:168
  60.6 4.4 %collective-permute-start.4 = (bf16[256,1536]{1,0:T(8,128)(2,1)S(1)}, bf16[256,1536]{1,0:T(8,128)(2,1)S(1)}, u32[]{:S(2)}, u32[]{:S(2)}) collective-permute-start(bf16[256,1536]{1,0:T(8,128)(2,1)S(1)} %pad_maximum_fusion.refs_0_), channel_id=1, source_target_pairs={{0,96},{32,0},{64,32},{96,64},{1,97},{33,1},{65,33},{97,65},{2,98}... | collective-permute-start | bytes 2359304 | tf_op jit(solution)/shard_map/ppermute | solution.py:168
  65.0 2.4 %collective-permute-start.5 = (bf16[256,1536]{1,0:T(8,128)(2,1)S(1)}, bf16[256,1536]{1,0:T(8,128)(2,1)S(1)}, u32[]{:S(2)}, u32[]{:S(2)}) collective-permute-start(bf16[256,1536]{1,0:T(8,128)(2,1)S(1)} %pad_maximum_fusion.refs_0_), channel_id=1, source_target_pairs={{0,64},{32,96},{64,0},{96,32},{1,65},{33,97},{65,1},{97,33},{2,66}... | collective-permute-start | bytes 2359304 | tf_op jit(solution)/shard_map/ppermute | solution.py:168
  67.4 2.5 %collective-permute-start.6 = (bf16[256,1536]{1,0:T(8,128)(2,1)S(1)}, bf16[256,1536]{1,0:T(8,128)(2,1)S(1)}, u32[]{:S(2)}, u32[]{:S(2)}) collective-permute-start(bf16[256,1536]{1,0:T(8,128)(2,1)S(1)} %pad_maximum_fusion.refs_0_), channel_id=1, source_target_pairs={{0,32},{32,64},{64,96},{96,0},{1,33},{33,65},{65,97},{97,1},{2,34}... | collective-permute-start | bytes 2359304 | tf_op jit(solution)/shard_map/ppermute | solution.py:168
  69.9 6.9 %collective-permute-start.2 = (bf16[64,1536]{1,0:T(8,128)(2,1)S(1)}, bf16[64,1536]{1,0:T(8,128)(2,1)S(1)}, u32[]{:S(2)}, u32[]{:S(2)}) collective-permute-start(bf16[64,1536]{1,0:T(8,128)(2,1)S(1)} %slice.8), channel_id=1, source_target_pairs={{0,8},{8,16},{16,24},{24,0},{1,9},{9,17},{17,25},{25,1},{2,10},{10... | collective-permute-start | bytes 589832 | tf_op jit(solution)/shard_map/ppermute | solution.py:168
  76.8 2.3 %collective-permute-start.3 = (bf16[64,1536]{1,0:T(8,128)(2,1)S(1)}, bf16[64,1536]{1,0:T(8,128)(2,1)S(1)}, u32[]{:S(2)}, u32[]{:S(2)}) collective-permute-start(bf16[64,1536]{1,0:T(8,128)(2,1)S(1)} %slice.9), channel_id=1, source_target_pairs={{0,24},{8,0},{16,8},{24,16},{1,25},{9,1},{17,9},{25,17},{2,26},{10... | collective-permute-start | bytes 589832 | tf_op jit(solution)/shard_map/ppermute | solution.py:168
  79.1 13.9 %collective-permute-done.2 = bf16[64,1536]{1,0:T(8,128)(2,1)S(1)} collective-permute-done((bf16[64,1536]{1,0:T(8,128)(2,1)S(1)}, bf16[64,1536]{1,0:T(8,128)(2,1)S(1)}, u32[]{:S(2)}, u32[]{:S(2)}) %collective-permute-start.2) | collective-permute-done | bytes 196640 | tf_op jit(solution)/shard_map/ppermute | solution.py:168
  93.0 11.7 %collective-permute-done.6.refs_6_ = bf16[256,1536]{1,0:T(8,128)(2,1)S(1)} collective-permute-done((bf16[256,1536]{1,0:T(8,128)(2,1)S(1)}, bf16[256,1536]{1,0:T(8,128)(2,1)S(1)}, u32[]{:S(2)}, u32[]{:S(2)}) %collective-permute-start.6) | collective-permute-done | bytes 786464 | tf_op jit(solution)/shard_map/ppermute | solution.py:168
  104.8 2.1 %collective-permute-start.7 = (bf16[128,1536]{1,0:T(8,128)(2,1)S(1)}, bf16[128,1536]{1,0:T(8,128)(2,1)S(1)}, u32[]{:S(2)}, u32[]{:S(2)}) collective-permute-start(bf16[128,1536]{1,0:T(8,128)(2,1)S(1)} %constant_dynamic-update-slice_fusion.refs_1_), channel_id=1, source_target_pairs={{0,96},{32,0},{64,32},{96,64},{1,97},{33,1},{65,33},{97,65},{2,98}... | collective-permute-start | bytes 1179656 | tf_op jit(solution)/shard_map/ppermute | solution.py:168
  106.9 2.4 %collective-permute-start.8 = (bf16[128,1536]{1,0:T(8,128)(2,1)S(1)}, bf16[128,1536]{1,0:T(8,128)(2,1)S(1)}, u32[]{:S(2)}, u32[]{:S(2)}) collective-permute-start(bf16[128,1536]{1,0:T(8,128)(2,1)S(1)} %constant_dynamic-update-slice_fusion.refs_1_), channel_id=1, source_target_pairs={{0,64},{32,96},{64,0},{96,32},{1,65},{33,97},{65,1},{97,33},{2,66}... | collective-permute-start | bytes 1179656 | tf_op jit(solution)/shard_map/ppermute | solution.py:168
  109.3 2.9 %collective-permute-start.9 = (bf16[128,1536]{1,0:T(8,128)(2,1)S(1)}, bf16[128,1536]{1,0:T(8,128)(2,1)}, u32[]{:S(2)}, u32[]{:S(2)}) collective-permute-start(bf16[128,1536]{1,0:T(8,128)(2,1)S(1)} %constant_dynamic-update-slice_fusion.refs_1_), channel_id=1, source_target_pairs={{0,32},{32,64},{64,96},{96,0},{1,33},{33,65},{65,97},{97,1},{2,34}... | collective-permute-start | bytes 1179656 | tf_op jit(solution)/shard_map/ppermute | solution.py:168
  112.2 5.1 %collective-permute-done.7.refs_3_ = bf16[128,1536]{1,0:T(8,128)(2,1)S(1)} collective-permute-done((bf16[128,1536]{1,0:T(8,128)(2,1)S(1)}, bf16[128,1536]{1,0:T(8,128)(2,1)S(1)}, u32[]{:S(2)}, u32[]{:S(2)}) %collective-permute-start.7) | collective-permute-done | bytes 393248 | tf_op jit(solution)/shard_map/ppermute | solution.py:168
  117.3 2.7 %collective-permute-done.8.refs_5_ = bf16[128,1536]{1,0:T(8,128)(2,1)S(1)} collective-permute-done((bf16[128,1536]{1,0:T(8,128)(2,1)S(1)}, bf16[128,1536]{1,0:T(8,128)(2,1)S(1)}, u32[]{:S(2)}, u32[]{:S(2)}) %collective-permute-start.8) | collective-permute-done | bytes 393248 | tf_op jit(solution)/shard_map/ppermute | solution.py:168
  120.0 0.7 copy-done.9
  120.7 9.1 %collective-permute-done.9.refs_7_ = bf16[128,1536]{1,0:T(8,128)(2,1)} collective-permute-done((bf16[128,1536]{1,0:T(8,128)(2,1)S(1)}, bf16[128,1536]{1,0:T(8,128)(2,1)}, u32[]{:S(2)}, u32[]{:S(2)}) %collective-permute-start.9) | collective-permute-done | bytes 393248 | tf_op jit(solution)/shard_map/ppermute | solution.py:168
  129.9 6.2 %stage.1.grads_ref = bf16[2048,1536]{1,0:T(8,128)(2,1)} custom-call(s32[5]{0:T(128)} %copy-done.1, bf16[4,128,1536]{2,1,0:T(8,128)(2,1)} %all-gather.4.cloned.1.call-done.own_ref, bf16[256,1536]{1,0:T(8,128)(2,1)} %copy-done.3, bf16[128,1536]{1,0:T(8,128)(2,1)} %copy-done.4, bf16[256,1536]{1,0:T(8,128)(2,1)} %copy-done.5, bf16[128,1536]{1,0:T(8,128)(2,1)} %copy-done.8, ...), custom_call_target="tpu_custom_call" | custom-call | bytes 12582912 | tf_op jit(solution)/shard_map/stage/pallas_call | solution.py:70
  136.1 8.1 %all-gather.6.cloned.1.call-done = bf16[3072,512]{1,0:T(8,128)(2,1)} async-done(((bf16[768,512]{1,0:T(8,128)(2,1)}), bf16[3072,512]{1,0:T(8,128)(2,1)}) %all-gather.6.cloned.1.call-update) | async-done | bytes 3145744 | tf_op jit(solution)/shard_map/all_gather | solution.py:184
  144.2 7.6 %product.1 = (bf16[4,96,1536]{2,1,0:T(8,128)(2,1)S(1)}, bf16[4,96,1536]{2,1,0:T(8,128)(2,1)S(1)}) custom-call(s32[5]{0:T(128)S(1)} %copy-done.2, bf16[4,768,512]{2,1,0:T(8,128)(2,1)} %bitcast.11, bf16[2048,1536]{1,0:T(8,128)(2,1)} %stage.1.grads_ref), custom_call_target="tpu_custom_call" | custom-call | flops 4831838208 | bytes 12582912 | tf_op jit(solution)/shard_map/product/pallas_call | solution.py:113
  151.8 2.4 %collective-permute-start.10 = (bf16[4,96,1536]{2,1,0:T(8,128)(2,1)S(1)}, bf16[4,96,1536]{2,1,0:T(8,128)(2,1)S(1)}, u32[]{:S(2)}, u32[]{:S(2)}) collective-permute-start(bf16[4,96,1536]{2,1,0:T(8,128)(2,1)S(1)} %get-tuple-element.30), channel_id=1, source_target_pairs={{0,1},{1,0},{2,3},{3,2},{4,5},{5,4},{6,7},{7,6},{8,9},{9,8},{10,11... | collective-permute-start | bytes 3538952 | tf_op jit(solution)/shard_map/ppermute | solution.py:196
  154.2 2.5 %collective-permute-done.10.got_ref = bf16[4,96,1536]{2,1,0:T(8,128)(2,1)S(1)} collective-permute-done((bf16[4,96,1536]{2,1,0:T(8,128)(2,1)S(1)}, bf16[4,96,1536]{2,1,0:T(8,128)(2,1)S(1)}, u32[]{:S(2)}, u32[]{:S(2)}) %collective-permute-start.10) | collective-permute-done | bytes 1179680 | tf_op jit(solution)/shard_map/ppermute | solution.py:196
  156.6 0.8 add_cores.1
  157.5 4.8 %collective-permute-start.11 = (bf16[96,1536]{1,0:T(8,128)(2,1)S(1)}, bf16[96,1536]{1,0:T(8,128)(2,1)S(1)}, u32[]{:S(2)}, u32[]{:S(2)}) collective-permute-start(bf16[96,1536]{1,0:T(8,128)(2,1)S(1)} %get-tuple-element.32), channel_id=1, source_target_pairs={{0,4},{2,6},{4,0},{6,2},{1,5},{3,7},{5,1},{7,3},{8,12},{10,14},{12... | collective-permute-start | bytes 884744 | tf_op jit(solution)/shard_map/ppermute | solution.py:168
  162.3 2.3 %collective-permute-start.12 = (bf16[96,1536]{1,0:T(8,128)(2,1)S(1)}, bf16[96,1536]{1,0:T(8,128)(2,1)S(1)}, u32[]{:S(2)}, u32[]{:S(2)}) collective-permute-start(bf16[96,1536]{1,0:T(8,128)(2,1)S(1)} %get-tuple-element.33), channel_id=1, source_target_pairs={{0,2},{2,4},{4,6},{6,0},{1,3},{3,5},{5,7},{7,1},{8,10},{10,12},{12... | collective-permute-start | bytes 884744 | tf_op jit(solution)/shard_map/ppermute | solution.py:168
  164.6 4.2 %collective-permute-start.13 = (bf16[96,1536]{1,0:T(8,128)(2,1)S(1)}, bf16[96,1536]{1,0:T(8,128)(2,1)S(1)}, u32[]{:S(2)}, u32[]{:S(2)}) collective-permute-start(bf16[96,1536]{1,0:T(8,128)(2,1)S(1)} %get-tuple-element.34), channel_id=1, source_target_pairs={{0,6},{2,0},{4,2},{6,4},{1,7},{3,1},{5,3},{7,5},{8,14},{10,8},{12,... | collective-permute-start | bytes 884744 | tf_op jit(solution)/shard_map/ppermute | solution.py:168
  169.1 7.0 %collective-permute-done.12.refs_1_ = bf16[96,1536]{1,0:T(8,128)(2,1)S(1)} collective-permute-done((bf16[96,1536]{1,0:T(8,128)(2,1)S(1)}, bf16[96,1536]{1,0:T(8,128)(2,1)S(1)}, u32[]{:S(2)}, u32[]{:S(2)}) %collective-permute-start.12) | collective-permute-done | bytes 294944 | tf_op jit(solution)/shard_map/ppermute | solution.py:168
  176.1 0.8 add_chips.1
  (33 shorter events, 0.6 us)
Async XLA Ops:
  6.5 123.3 %all-gather.4.cloned.1.call-start = ((), (), s32[]{:S(2)}) async-start(), calls=%async_computation | async-start | bytes 1966080 | tf_op jit(solution)/shard_map/all_gather | solution.py:178
  7.3 136.9 %all-gather.6.cloned.1.call-start = ((), (), s32[]{:S(2)}) async-start(), calls=%async_computation.1 | async-start | bytes 3932160 | tf_op jit(solution)/shard_map/all_gather | solution.py:184
  7.3 26.6 %collective-permute-start.1 = (bf16[128,1536]{1,0:T(8,128)(2,1)}, bf16[128,1536]{1,0:T(8,128)(2,1)S(1)}, u32[]{:S(2)}, u32[]{:S(2)}) collective-permute-start(bf16[128,1536]{1,0:T(8,128)(2,1)} %bitcast.9), channel_id=1, source_target_pairs={{0,8},{8,16},{16,24},{24,0},{1,9},{9,17},{17,25},{25,1},{2,10},{10... | collective-permute-start | bytes 1179656 | tf_op jit(solution)/shard_map/ppermute | solution.py:168
  17.0 43.5 %collective-permute-start = (bf16[128,1536]{1,0:T(8,128)(2,1)}, bf16[128,1536]{1,0:T(8,128)(2,1)S(1)}, u32[]{:S(2)}, u32[]{:S(2)}) collective-permute-start(bf16[128,1536]{1,0:T(8,128)(2,1)} %bitcast.10), channel_id=1, source_target_pairs={{0,24},{8,0},{16,8},{24,16},{1,25},{9,1},{17,9},{25,17},{2,26},{10... | collective-permute-start | bytes 1179656 | tf_op jit(solution)/shard_map/ppermute | solution.py:168
  22.6 37.9 %copy-start.1 = (s32[5]{0:T(128)}, s32[5]{0:T(128)S(1)}, u32[]{:S(2)}) copy-start(s32[5]{0:T(128)S(1)} %stack.23.where) | copy-start | bytes 64
  22.6 1.1 copy-start
  60.5 69.3 %copy-start.3 = (bf16[256,1536]{1,0:T(8,128)(2,1)}, bf16[256,1536]{1,0:T(8,128)(2,1)S(1)}, u32[]{:S(2)}) copy-start(bf16[256,1536]{1,0:T(8,128)(2,1)S(1)} %pad_maximum_fusion.refs_0_) | copy-start | bytes 2359300
  60.6 32.4 %collective-permute-start.4 = (bf16[256,1536]{1,0:T(8,128)(2,1)S(1)}, bf16[256,1536]{1,0:T(8,128)(2,1)S(1)}, u32[]{:S(2)}, u32[]{:S(2)}) collective-permute-start(bf16[256,1536]{1,0:T(8,128)(2,1)S(1)} %pad_maximum_fusion.refs_0_), channel_id=1, source_target_pairs={{0,96},{32,0},{64,32},{96,64},{1,97},{33,1},{65,33},{97,65},{2,98}... | collective-permute-start | bytes 2359304 | tf_op jit(solution)/shard_map/ppermute | solution.py:168
  65.0 28.1 %collective-permute-start.5 = (bf16[256,1536]{1,0:T(8,128)(2,1)S(1)}, bf16[256,1536]{1,0:T(8,128)(2,1)S(1)}, u32[]{:S(2)}, u32[]{:S(2)}) collective-permute-start(bf16[256,1536]{1,0:T(8,128)(2,1)S(1)} %pad_maximum_fusion.refs_0_), channel_id=1, source_target_pairs={{0,64},{32,96},{64,0},{96,32},{1,65},{33,97},{65,1},{97,33},{2,66}... | collective-permute-start | bytes 2359304 | tf_op jit(solution)/shard_map/ppermute | solution.py:168
  67.4 37.4 %collective-permute-start.6 = (bf16[256,1536]{1,0:T(8,128)(2,1)S(1)}, bf16[256,1536]{1,0:T(8,128)(2,1)S(1)}, u32[]{:S(2)}, u32[]{:S(2)}) collective-permute-start(bf16[256,1536]{1,0:T(8,128)(2,1)S(1)} %pad_maximum_fusion.refs_0_), channel_id=1, source_target_pairs={{0,32},{32,64},{64,96},{96,0},{1,33},{33,65},{65,97},{97,1},{2,34}... | collective-permute-start | bytes 2359304 | tf_op jit(solution)/shard_map/ppermute | solution.py:168
  69.9 23.1 %collective-permute-start.2 = (bf16[64,1536]{1,0:T(8,128)(2,1)S(1)}, bf16[64,1536]{1,0:T(8,128)(2,1)S(1)}, u32[]{:S(2)}, u32[]{:S(2)}) collective-permute-start(bf16[64,1536]{1,0:T(8,128)(2,1)S(1)} %slice.8), channel_id=1, source_target_pairs={{0,8},{8,16},{16,24},{24,0},{1,9},{9,17},{17,25},{25,1},{2,10},{10... | collective-permute-start | bytes 589832 | tf_op jit(solution)/shard_map/ppermute | solution.py:168
  76.8 16.2 %collective-permute-start.3 = (bf16[64,1536]{1,0:T(8,128)(2,1)S(1)}, bf16[64,1536]{1,0:T(8,128)(2,1)S(1)}, u32[]{:S(2)}, u32[]{:S(2)}) collective-permute-start(bf16[64,1536]{1,0:T(8,128)(2,1)S(1)} %slice.9), channel_id=1, source_target_pairs={{0,24},{8,0},{16,8},{24,16},{1,25},{9,1},{17,9},{25,17},{2,26},{10... | collective-permute-start | bytes 589832 | tf_op jit(solution)/shard_map/ppermute | solution.py:168
  93.0 36.9 %copy-start.5 = (bf16[256,1536]{1,0:T(8,128)(2,1)}, bf16[256,1536]{1,0:T(8,128)(2,1)S(1)}, u32[]{:S(2)}) copy-start(bf16[256,1536]{1,0:T(8,128)(2,1)S(1)} %collective-permute-done.4.refs_2_) | copy-start | bytes 2359300
  93.0 36.9 %copy-start.6 = (bf16[256,1536]{1,0:T(8,128)(2,1)}, bf16[256,1536]{1,0:T(8,128)(2,1)S(1)}, u32[]{:S(2)}) copy-start(bf16[256,1536]{1,0:T(8,128)(2,1)S(1)} %collective-permute-done.5.refs_4_) | copy-start | bytes 2359300
  104.8 25.1 %copy-start.7 = (bf16[256,1536]{1,0:T(8,128)(2,1)}, bf16[256,1536]{1,0:T(8,128)(2,1)S(1)}, u32[]{:S(2)}) copy-start(bf16[256,1536]{1,0:T(8,128)(2,1)S(1)} %collective-permute-done.6.refs_6_) | copy-start | bytes 2359300
  104.8 25.1 %copy-start.4 = (bf16[128,1536]{1,0:T(8,128)(2,1)}, bf16[128,1536]{1,0:T(8,128)(2,1)S(1)}, u32[]{:S(2)}) copy-start(bf16[128,1536]{1,0:T(8,128)(2,1)S(1)} %constant_dynamic-update-slice_fusion.refs_1_) | copy-start | bytes 1179652
  104.8 39.3 %copy-start.2 = (s32[5]{0:T(128)S(1)}, s32[5]{0:T(128)}, u32[]{:S(2)}) copy-start(s32[5]{0:T(128)} %copy-done.1) | copy-start | bytes 64
  104.8 12.4 %collective-permute-start.7 = (bf16[128,1536]{1,0:T(8,128)(2,1)S(1)}, bf16[128,1536]{1,0:T(8,128)(2,1)S(1)}, u32[]{:S(2)}, u32[]{:S(2)}) collective-permute-start(bf16[128,1536]{1,0:T(8,128)(2,1)S(1)} %constant_dynamic-update-slice_fusion.refs_1_), channel_id=1, source_target_pairs={{0,96},{32,0},{64,32},{96,64},{1,97},{33,1},{65,33},{97,65},{2,98}... | collective-permute-start | bytes 1179656 | tf_op jit(solution)/shard_map/ppermute | solution.py:168
  106.9 13.1 %collective-permute-start.8 = (bf16[128,1536]{1,0:T(8,128)(2,1)S(1)}, bf16[128,1536]{1,0:T(8,128)(2,1)S(1)}, u32[]{:S(2)}, u32[]{:S(2)}) collective-permute-start(bf16[128,1536]{1,0:T(8,128)(2,1)S(1)} %constant_dynamic-update-slice_fusion.refs_1_), channel_id=1, source_target_pairs={{0,64},{32,96},{64,0},{96,32},{1,65},{33,97},{65,1},{97,33},{2,66}... | collective-permute-start | bytes 1179656 | tf_op jit(solution)/shard_map/ppermute | solution.py:168
  109.3 20.5 %collective-permute-start.9 = (bf16[128,1536]{1,0:T(8,128)(2,1)S(1)}, bf16[128,1536]{1,0:T(8,128)(2,1)}, u32[]{:S(2)}, u32[]{:S(2)}) collective-permute-start(bf16[128,1536]{1,0:T(8,128)(2,1)S(1)} %constant_dynamic-update-slice_fusion.refs_1_), channel_id=1, source_target_pairs={{0,32},{32,64},{64,96},{96,0},{1,33},{33,65},{65,97},{97,1},{2,34}... | collective-permute-start | bytes 1179656 | tf_op jit(solution)/shard_map/ppermute | solution.py:168
  117.3 2.7 %copy-start.8 = (bf16[128,1536]{1,0:T(8,128)(2,1)}, bf16[128,1536]{1,0:T(8,128)(2,1)S(1)}, u32[]{:S(2)}) copy-start(bf16[128,1536]{1,0:T(8,128)(2,1)S(1)} %collective-permute-done.7.refs_3_) | copy-start | bytes 1179652
  120.0 0.7 copy-start.9
  151.8 4.8 %collective-permute-start.10 = (bf16[4,96,1536]{2,1,0:T(8,128)(2,1)S(1)}, bf16[4,96,1536]{2,1,0:T(8,128)(2,1)S(1)}, u32[]{:S(2)}, u32[]{:S(2)}) collective-permute-start(bf16[4,96,1536]{2,1,0:T(8,128)(2,1)S(1)} %get-tuple-element.30), channel_id=1, source_target_pairs={{0,1},{1,0},{2,3},{3,2},{4,5},{5,4},{6,7},{7,6},{8,9},{9,8},{10,11... | collective-permute-start | bytes 3538952 | tf_op jit(solution)/shard_map/ppermute | solution.py:196
  157.5 11.6 %collective-permute-start.11 = (bf16[96,1536]{1,0:T(8,128)(2,1)S(1)}, bf16[96,1536]{1,0:T(8,128)(2,1)S(1)}, u32[]{:S(2)}, u32[]{:S(2)}) collective-permute-start(bf16[96,1536]{1,0:T(8,128)(2,1)S(1)} %get-tuple-element.32), channel_id=1, source_target_pairs={{0,4},{2,6},{4,0},{6,2},{1,5},{3,7},{5,1},{7,3},{8,12},{10,14},{12... | collective-permute-start | bytes 884744 | tf_op jit(solution)/shard_map/ppermute | solution.py:168
  162.3 13.8 %collective-permute-start.12 = (bf16[96,1536]{1,0:T(8,128)(2,1)S(1)}, bf16[96,1536]{1,0:T(8,128)(2,1)S(1)}, u32[]{:S(2)}, u32[]{:S(2)}) collective-permute-start(bf16[96,1536]{1,0:T(8,128)(2,1)S(1)} %get-tuple-element.33), channel_id=1, source_target_pairs={{0,2},{2,4},{4,6},{6,0},{1,3},{3,5},{5,7},{7,1},{8,10},{10,12},{12... | collective-permute-start | bytes 884744 | tf_op jit(solution)/shard_map/ppermute | solution.py:168
  164.6 11.5 %collective-permute-start.13 = (bf16[96,1536]{1,0:T(8,128)(2,1)S(1)}, bf16[96,1536]{1,0:T(8,128)(2,1)S(1)}, u32[]{:S(2)}, u32[]{:S(2)}) collective-permute-start(bf16[96,1536]{1,0:T(8,128)(2,1)S(1)} %get-tuple-element.34), channel_id=1, source_target_pairs={{0,6},{2,0},{4,2},{6,4},{1,7},{3,1},{5,3},{7,5},{8,14},{10,8},{12,... | collective-permute-start | bytes 884744 | tf_op jit(solution)/shard_map/ppermute | solution.py:168
Sparse Core Ops, SparseCore 0:
  9.5 39.4 all-gather.3
  60.7 83.4 all-gather.5

commit v7 on v5

--- a/solution.py
+++ b/solution.py
@@ -191,7 +191,7 @@
     other, mine = product(where, inputs, right)
     got = lax.ppermute(other, "core", [(0, 1), (1, 0)])
     kept, *sends = add_cores(where, mine, got)
-    return add_chips(kept, [ring(sends[k - 1], "y", k) for k in (2, 1, 3)])
+    return add_chips(kept, [ring(sends[k - 1], "y", k) for k in (2, 3, 1)])
 
 
 def solution(mesh):

time: 184 us -> 184 us (level)
  no operation moved by 1% of the time
where the time goes in v7:
time: 184 us; the launch traced here: 183 us
  waiting for transfers between devices  87.6 us (48%)
  starting transfers between devices  62.7 us (34%)
  Pallas kernels  16.5 us (9%)
  between operations  13.7 us (7%)
  local copies, waits for them, and re-layouts  2.05 us (1%)
    ppermute x16, waiting for transfers between devices, ring(): return lax.ppermute(value, axis, [(i, (i + step) % 4) for i in range(4)])  77.1 us
    ppermute x16, starting transfers between devices, ring(): return lax.ppermute(value, axis, [(i, (i + step) % 4) for i in range(4)])  60.3 us
    all_gather x1, waiting for transfers between devices, shards(): inputs = lax.all_gather(turned, 'row', axis=0)  8.11 us
    pallas_call x1, Pallas kernels, product(): pl.pallas_call(product_kernel, out_shape=[jax.ShapeDtypeStruct((4, rows /...  7.64 us
    pallas_call x1, Pallas kernels, stage(): pl.pallas_call(stage_kernel, out_shape=jax.ShapeDtypeStruct((tokens, piec...  5.5 us
  transfers between devices with their start and end apart: 18, of which 10 were waited for; matrix products, arithmetic and copies ran while one was open for 0% of the time, Pallas kernels for 4%

profile of v7, /device:TPU:1, one launch (start us, length us, event | category | flops | bytes accessed | tf_op | source)
XLA Modules:
  0.0 182.7 jit_solution(16300118296010234164)
XLA Ops:
  6.5 9.6 %collective-permute-start.1 = (bf16[128,1536]{1,0:T(8,128)(2,1)}, bf16[128,1536]{1,0:T(8,128)(2,1)S(1)}, u32[]{:S(2)}, u32[]{:S(2)}) collective-permute-start(bf16[128,1536]{1,0:T(8,128)(2,1)} %bitcast.9), channel_id=1, source_target_pairs={{0,8},{8,16},{16,24},{24,0},{1,9},{9,17},{17,25},{25,1},{2,10},{10... | collective-permute-start | bytes 1179656 | tf_op jit(solution)/shard_map/ppermute | solution.py:165
  16.2 5.6 %collective-permute-start = (bf16[128,1536]{1,0:T(8,128)(2,1)}, bf16[128,1536]{1,0:T(8,128)(2,1)S(1)}, u32[]{:S(2)}, u32[]{:S(2)}) collective-permute-start(bf16[128,1536]{1,0:T(8,128)(2,1)} %bitcast.10), channel_id=1, source_target_pairs={{0,24},{8,0},{16,8},{24,16},{1,25},{9,1},{17,9},{25,17},{2,26},{10... | collective-permute-start | bytes 1179656 | tf_op jit(solution)/shard_map/ppermute | solution.py:165
  21.8 4.4 %collective-permute-start.2 = (bf16[128,1536]{1,0:T(8,128)(2,1)}, bf16[128,1536]{1,0:T(8,128)(2,1)S(1)}, u32[]{:S(2)}, u32[]{:S(2)}) collective-permute-start(bf16[128,1536]{1,0:T(8,128)(2,1)} %bitcast.11), channel_id=1, source_target_pairs={{0,96},{32,0},{64,32},{96,64},{1,97},{33,1},{65,33},{97,65},{2,98}... | collective-permute-start | bytes 1179656 | tf_op jit(solution)/shard_map/ppermute | solution.py:165
  26.1 2.4 %collective-permute-start.3 = (bf16[128,1536]{1,0:T(8,128)(2,1)}, bf16[128,1536]{1,0:T(8,128)(2,1)S(1)}, u32[]{:S(2)}, u32[]{:S(2)}) collective-permute-start(bf16[128,1536]{1,0:T(8,128)(2,1)} %bitcast.12), channel_id=1, source_target_pairs={{0,64},{32,96},{64,0},{96,32},{1,65},{33,97},{65,1},{97,33},{2,66}... | collective-permute-start | bytes 1179656 | tf_op jit(solution)/shard_map/ppermute | solution.py:165
  28.6 2.5 %collective-permute-start.4 = (bf16[128,1536]{1,0:T(8,128)(2,1)}, bf16[128,1536]{1,0:T(8,128)(2,1)S(1)}, u32[]{:S(2)}, u32[]{:S(2)}) collective-permute-start(bf16[128,1536]{1,0:T(8,128)(2,1)} %bitcast.13), channel_id=1, source_target_pairs={{0,32},{32,64},{64,96},{96,0},{1,33},{33,65},{65,97},{97,1},{2,34}... | collective-permute-start | bytes 1179656 | tf_op jit(solution)/shard_map/ppermute | solution.py:165
  31.2 1.1 copy-done
  32.3 1.8 turn.1
  34.1 25.6 %collective-permute-done = bf16[128,1536]{1,0:T(8,128)(2,1)S(1)} collective-permute-done((bf16[128,1536]{1,0:T(8,128)(2,1)}, bf16[128,1536]{1,0:T(8,128)(2,1)S(1)}, u32[]{:S(2)}, u32[]{:S(2)}) %collective-permute-start) | collective-permute-done | bytes 393248 | tf_op jit(solution)/shard_map/ppermute | solution.py:165
  59.8 4.4 %collective-permute-start.7 = (bf16[256,1536]{1,0:T(8,128)(2,1)S(1)}, bf16[256,1536]{1,0:T(8,128)(2,1)S(1)}, u32[]{:S(2)}, u32[]{:S(2)}) collective-permute-start(bf16[256,1536]{1,0:T(8,128)(2,1)S(1)} %pad_maximum_fusion.refs_1_), channel_id=1, source_target_pairs={{0,96},{32,0},{64,32},{96,64},{1,97},{33,1},{65,33},{97,65},{2,98}... | collective-permute-start | bytes 2359304 | tf_op jit(solution)/shard_map/ppermute | solution.py:165
  64.2 2.4 %collective-permute-start.8 = (bf16[256,1536]{1,0:T(8,128)(2,1)S(1)}, bf16[256,1536]{1,0:T(8,128)(2,1)S(1)}, u32[]{:S(2)}, u32[]{:S(2)}) collective-permute-start(bf16[256,1536]{1,0:T(8,128)(2,1)S(1)} %pad_maximum_fusion.refs_1_), channel_id=1, source_target_pairs={{0,64},{32,96},{64,0},{96,32},{1,65},{33,97},{65,1},{97,33},{2,66}... | collective-permute-start | bytes 2359304 | tf_op jit(solution)/shard_map/ppermute | solution.py:165
  66.7 2.5 %collective-permute-start.9 = (bf16[256,1536]{1,0:T(8,128)(2,1)S(1)}, bf16[256,1536]{1,0:T(8,128)(2,1)S(1)}, u32[]{:S(2)}, u32[]{:S(2)}) collective-permute-start(bf16[256,1536]{1,0:T(8,128)(2,1)S(1)} %pad_maximum_fusion.refs_1_), channel_id=1, source_target_pairs={{0,32},{32,64},{64,96},{96,0},{1,33},{33,65},{65,97},{97,1},{2,34}... | collective-permute-start | bytes 2359304 | tf_op jit(solution)/shard_map/ppermute | solution.py:165
  69.2 6.9 %collective-permute-start.5 = (bf16[64,1536]{1,0:T(8,128)(2,1)S(1)}, bf16[64,1536]{1,0:T(8,128)(2,1)S(1)}, u32[]{:S(2)}, u32[]{:S(2)}) collective-permute-start(bf16[64,1536]{1,0:T(8,128)(2,1)S(1)} %slice.8), channel_id=1, source_target_pairs={{0,8},{8,16},{16,24},{24,0},{1,9},{9,17},{17,25},{25,1},{2,10},{10... | collective-permute-start | bytes 589832 | tf_op jit(solution)/shard_map/ppermute | solution.py:165
  76.1 2.3 %collective-permute-start.6 = (bf16[64,1536]{1,0:T(8,128)(2,1)S(1)}, bf16[64,1536]{1,0:T(8,128)(2,1)S(1)}, u32[]{:S(2)}, u32[]{:S(2)}) collective-permute-start(bf16[64,1536]{1,0:T(8,128)(2,1)S(1)} %slice.9), channel_id=1, source_target_pairs={{0,24},{8,0},{16,8},{24,16},{1,25},{9,1},{17,9},{25,17},{2,26},{10... | collective-permute-start | bytes 589832 | tf_op jit(solution)/shard_map/ppermute | solution.py:165
  78.4 13.9 %collective-permute-done.5 = bf16[64,1536]{1,0:T(8,128)(2,1)S(1)} collective-permute-done((bf16[64,1536]{1,0:T(8,128)(2,1)S(1)}, bf16[64,1536]{1,0:T(8,128)(2,1)S(1)}, u32[]{:S(2)}, u32[]{:S(2)}) %collective-permute-start.5) | collective-permute-done | bytes 196640 | tf_op jit(solution)/shard_map/ppermute | solution.py:165
  92.3 11.7 %collective-permute-done.9.refs_10_ = bf16[256,1536]{1,0:T(8,128)(2,1)S(1)} collective-permute-done((bf16[256,1536]{1,0:T(8,128)(2,1)S(1)}, bf16[256,1536]{1,0:T(8,128)(2,1)S(1)}, u32[]{:S(2)}, u32[]{:S(2)}) %collective-permute-start.9) | collective-permute-done | bytes 786464 | tf_op jit(solution)/shard_map/ppermute | solution.py:165
  104.1 1.9 %collective-permute-start.10 = (bf16[128,1536]{1,0:T(8,128)(2,1)S(1)}, bf16[128,1536]{1,0:T(8,128)(2,1)S(1)}, u32[]{:S(2)}, u32[]{:S(2)}) collective-permute-start(bf16[128,1536]{1,0:T(8,128)(2,1)S(1)} %constant_dynamic-update-slice_fusion.refs_2_), channel_id=1, source_target_pairs={{0,96},{32,0},{64,32},{96,64},{1,97},{33,1},{65,33},{97,65},{2,98}... | collective-permute-start | bytes 1179656 | tf_op jit(solution)/shard_map/ppermute | solution.py:165
  106.0 2.4 %collective-permute-start.11 = (bf16[128,1536]{1,0:T(8,128)(2,1)S(1)}, bf16[128,1536]{1,0:T(8,128)(2,1)S(1)}, u32[]{:S(2)}, u32[]{:S(2)}) collective-permute-start(bf16[128,1536]{1,0:T(8,128)(2,1)S(1)} %constant_dynamic-update-slice_fusion.refs_2_), channel_id=1, source_target_pairs={{0,64},{32,96},{64,0},{96,32},{1,65},{33,97},{65,1},{97,33},{2,66}... | collective-permute-start | bytes 1179656 | tf_op jit(solution)/shard_map/ppermute | solution.py:165
  108.5 2.9 %collective-permute-start.12 = (bf16[128,1536]{1,0:T(8,128)(2,1)S(1)}, bf16[128,1536]{1,0:T(8,128)(2,1)S(1)}, u32[]{:S(2)}, u32[]{:S(2)}) collective-permute-start(bf16[128,1536]{1,0:T(8,128)(2,1)S(1)} %constant_dynamic-update-slice_fusion.refs_2_), channel_id=1, source_target_pairs={{0,32},{32,64},{64,96},{96,0},{1,33},{33,65},{65,97},{97,1},{2,34}... | collective-permute-start | bytes 1179656 | tf_op jit(solution)/shard_map/ppermute | solution.py:165
  111.3 5.1 %collective-permute-done.10.refs_5_ = bf16[128,1536]{1,0:T(8,128)(2,1)S(1)} collective-permute-done((bf16[128,1536]{1,0:T(8,128)(2,1)S(1)}, bf16[128,1536]{1,0:T(8,128)(2,1)S(1)}, u32[]{:S(2)}, u32[]{:S(2)}) %collective-permute-start.10) | collective-permute-done | bytes 393248 | tf_op jit(solution)/shard_map/ppermute | solution.py:165
  116.4 2.7 %collective-permute-done.11.refs_8_ = bf16[128,1536]{1,0:T(8,128)(2,1)S(1)} collective-permute-done((bf16[128,1536]{1,0:T(8,128)(2,1)S(1)}, bf16[128,1536]{1,0:T(8,128)(2,1)S(1)}, u32[]{:S(2)}, u32[]{:S(2)}) %collective-permute-start.11) | collective-permute-done | bytes 393248 | tf_op jit(solution)/shard_map/ppermute | solution.py:165
  119.1 9.9 %collective-permute-done.12.refs_11_ = bf16[128,1536]{1,0:T(8,128)(2,1)S(1)} collective-permute-done((bf16[128,1536]{1,0:T(8,128)(2,1)S(1)}, bf16[128,1536]{1,0:T(8,128)(2,1)S(1)}, u32[]{:S(2)}, u32[]{:S(2)}) %collective-permute-start.12) | collective-permute-done | bytes 393248 | tf_op jit(solution)/shard_map/ppermute | solution.py:165
  129.8 5.5 %stage.1.grads_ref = bf16[2048,1536]{1,0:T(8,128)(2,1)} custom-call(bf16[128,1536]{1,0:T(8,128)(2,1)} %bitcast.14, bf16[256,1536]{1,0:T(8,128)(2,1)} %copy-done.1, bf16[128,1536]{1,0:T(8,128)(2,1)} %copy-done.2, bf16[128,1536]{1,0:T(8,128)(2,1)} %copy-done.6, bf16[256,1536]{1,0:T(8,128)(2,1)} %copy-done.3, bf16[128,1536]{1,0:T(8,128)(2,1)} %copy-done.9, ...), custom_call_target="tpu_custom_call" | custom-call | bytes 12582912 | tf_op jit(solution)/shard_map/stage/pallas_call | solution.py:67
  135.3 8.1 %all-gather.3.cloned.1.call-done = bf16[3072,512]{1,0:T(8,128)(2,1)} async-done(((bf16[768,512]{1,0:T(8,128)(2,1)}), bf16[3072,512]{1,0:T(8,128)(2,1)}) %all-gather.3.cloned.1.call-update) | async-done | bytes 3145744 | tf_op jit(solution)/shard_map/all_gather | solution.py:180
  143.4 7.6 %product.1 = (bf16[4,96,1536]{2,1,0:T(8,128)(2,1)S(1)}, bf16[4,96,1536]{2,1,0:T(8,128)(2,1)S(1)}) custom-call(s32[5]{0:T(128)S(1)} %stack.23.where, bf16[4,768,512]{2,1,0:T(8,128)(2,1)} %bitcast.15, bf16[2048,1536]{1,0:T(8,128)(2,1)} %stage.1.grads_ref), custom_call_target="tpu_custom_call" | custom-call | flops 4831838208 | bytes 12582912 | tf_op jit(solution)/shard_map/product/pallas_call | solution.py:110
  151.1 2.4 %collective-permute-start.13 = (bf16[4,96,1536]{2,1,0:T(8,128)(2,1)S(1)}, bf16[4,96,1536]{2,1,0:T(8,128)(2,1)S(1)}, u32[]{:S(2)}, u32[]{:S(2)}) collective-permute-start(bf16[4,96,1536]{2,1,0:T(8,128)(2,1)S(1)} %get-tuple-element.36), channel_id=1, source_target_pairs={{0,1},{1,0},{2,3},{3,2},{4,5},{5,4},{6,7},{7,6},{8,9},{9,8},{10,11... | collective-permute-start | bytes 3538952 | tf_op jit(solution)/shard_map/ppermute | solution.py:192
  153.5 2.5 %collective-permute-done.13.got_ref = bf16[4,96,1536]{2,1,0:T(8,128)(2,1)S(1)} collective-permute-done((bf16[4,96,1536]{2,1,0:T(8,128)(2,1)S(1)}, bf16[4,96,1536]{2,1,0:T(8,128)(2,1)S(1)}, u32[]{:S(2)}, u32[]{:S(2)}) %collective-permute-start.13) | collective-permute-done | bytes 1179680 | tf_op jit(solution)/shard_map/ppermute | solution.py:192
  156.7 4.8 %collective-permute-start.14 = (bf16[96,1536]{1,0:T(8,128)(2,1)S(1)}, bf16[96,1536]{1,0:T(8,128)(2,1)S(1)}, u32[]{:S(2)}, u32[]{:S(2)}) collective-permute-start(bf16[96,1536]{1,0:T(8,128)(2,1)S(1)} %get-tuple-element.38), channel_id=1, source_target_pairs={{0,4},{2,6},{4,0},{6,2},{1,5},{3,7},{5,1},{7,3},{8,12},{10,14},{12... | collective-permute-start | bytes 884744 | tf_op jit(solution)/shard_map/ppermute | solution.py:165
  161.6 2.7 %collective-permute-start.15 = (bf16[96,1536]{1,0:T(8,128)(2,1)S(1)}, bf16[96,1536]{1,0:T(8,128)(2,1)S(1)}, u32[]{:S(2)}, u32[]{:S(2)}) collective-permute-start(bf16[96,1536]{1,0:T(8,128)(2,1)S(1)} %get-tuple-element.39), channel_id=1, source_target_pairs={{0,6},{2,0},{4,2},{6,4},{1,7},{3,1},{5,3},{7,5},{8,14},{10,8},{12,... | collective-permute-start | bytes 884744 | tf_op jit(solution)/shard_map/ppermute | solution.py:165
  164.3 2.6 %collective-permute-start.16 = (bf16[96,1536]{1,0:T(8,128)(2,1)S(1)}, bf16[96,1536]{1,0:T(8,128)(2,1)S(1)}, u32[]{:S(2)}, u32[]{:S(2)}) collective-permute-start(bf16[96,1536]{1,0:T(8,128)(2,1)S(1)} %get-tuple-element.40), channel_id=1, source_target_pairs={{0,2},{2,4},{4,6},{6,0},{1,3},{3,5},{5,7},{7,1},{8,10},{10,12},{12... | collective-permute-start | bytes 884744 | tf_op jit(solution)/shard_map/ppermute | solution.py:165
  166.9 1.5 collective-permute-done.14.refs_0_
  168.4 6.7 %collective-permute-done.15.refs_1_ = bf16[96,1536]{1,0:T(8,128)(2,1)S(1)} collective-permute-done((bf16[96,1536]{1,0:T(8,128)(2,1)S(1)}, bf16[96,1536]{1,0:T(8,128)(2,1)S(1)}, u32[]{:S(2)}, u32[]{:S(2)}) %collective-permute-start.15) | collective-permute-done | bytes 294944 | tf_op jit(solution)/shard_map/ppermute | solution.py:165
  175.1 0.8 add_chips.1
  (40 shorter events, 1.8 us)
Async XLA Ops:
  6.5 136.9 %all-gather.3.cloned.1.call-start = ((), (), s32[]{:S(2)}) async-start(), calls=%async_computation | async-start | bytes 3932160 | tf_op jit(solution)/shard_map/all_gather | solution.py:180
  6.5 27.6 %collective-permute-start.1 = (bf16[128,1536]{1,0:T(8,128)(2,1)}, bf16[128,1536]{1,0:T(8,128)(2,1)S(1)}, u32[]{:S(2)}, u32[]{:S(2)}) collective-permute-start(bf16[128,1536]{1,0:T(8,128)(2,1)} %bitcast.9), channel_id=1, source_target_pairs={{0,8},{8,16},{16,24},{24,0},{1,9},{9,17},{17,25},{25,1},{2,10},{10... | collective-permute-start | bytes 1179656 | tf_op jit(solution)/shard_map/ppermute | solution.py:165
  16.2 43.5 %collective-permute-start = (bf16[128,1536]{1,0:T(8,128)(2,1)}, bf16[128,1536]{1,0:T(8,128)(2,1)S(1)}, u32[]{:S(2)}, u32[]{:S(2)}) collective-permute-start(bf16[128,1536]{1,0:T(8,128)(2,1)} %bitcast.10), channel_id=1, source_target_pairs={{0,24},{8,0},{16,8},{24,16},{1,25},{9,1},{17,9},{25,17},{2,26},{10... | collective-permute-start | bytes 1179656 | tf_op jit(solution)/shard_map/ppermute | solution.py:165
  21.8 38.0 %collective-permute-start.2 = (bf16[128,1536]{1,0:T(8,128)(2,1)}, bf16[128,1536]{1,0:T(8,128)(2,1)S(1)}, u32[]{:S(2)}, u32[]{:S(2)}) collective-permute-start(bf16[128,1536]{1,0:T(8,128)(2,1)} %bitcast.11), channel_id=1, source_target_pairs={{0,96},{32,0},{64,32},{96,64},{1,97},{33,1},{65,33},{97,65},{2,98}... | collective-permute-start | bytes 1179656 | tf_op jit(solution)/shard_map/ppermute | solution.py:165
  26.1 33.6 %collective-permute-start.3 = (bf16[128,1536]{1,0:T(8,128)(2,1)}, bf16[128,1536]{1,0:T(8,128)(2,1)S(1)}, u32[]{:S(2)}, u32[]{:S(2)}) collective-permute-start(bf16[128,1536]{1,0:T(8,128)(2,1)} %bitcast.12), channel_id=1, source_target_pairs={{0,64},{32,96},{64,0},{96,32},{1,65},{33,97},{65,1},{97,33},{2,66}... | collective-permute-start | bytes 1179656 | tf_op jit(solution)/shard_map/ppermute | solution.py:165
  28.6 31.2 %collective-permute-start.4 = (bf16[128,1536]{1,0:T(8,128)(2,1)}, bf16[128,1536]{1,0:T(8,128)(2,1)S(1)}, u32[]{:S(2)}, u32[]{:S(2)}) collective-permute-start(bf16[128,1536]{1,0:T(8,128)(2,1)} %bitcast.13), channel_id=1, source_target_pairs={{0,32},{32,64},{64,96},{96,0},{1,33},{33,65},{65,97},{97,1},{2,34}... | collective-permute-start | bytes 1179656 | tf_op jit(solution)/shard_map/ppermute | solution.py:165
  31.2 1.1 copy-start
  59.8 69.3 %copy-start.1 = (bf16[256,1536]{1,0:T(8,128)(2,1)}, bf16[256,1536]{1,0:T(8,128)(2,1)S(1)}, u32[]{:S(2)}) copy-start(bf16[256,1536]{1,0:T(8,128)(2,1)S(1)} %pad_maximum_fusion.refs_1_) | copy-start | bytes 2359300
  59.8 69.2 %copy-start.6 = (bf16[128,1536]{1,0:T(8,128)(2,1)}, bf16[128,1536]{1,0:T(8,128)(2,1)S(1)}, u32[]{:S(2)}) copy-start(bf16[128,1536]{1,0:T(8,128)(2,1)S(1)} %collective-permute-done.2.refs_3_) | copy-start | bytes 1179652
  59.8 69.2 %copy-start.7 = (bf16[128,1536]{1,0:T(8,128)(2,1)}, bf16[128,1536]{1,0:T(8,128)(2,1)S(1)}, u32[]{:S(2)}) copy-start(bf16[128,1536]{1,0:T(8,128)(2,1)S(1)} %collective-permute-done.3.refs_6_) | copy-start | bytes 1179652
  59.8 69.2 %copy-start.8 = (bf16[128,1536]{1,0:T(8,128)(2,1)}, bf16[128,1536]{1,0:T(8,128)(2,1)S(1)}, u32[]{:S(2)}) copy-start(bf16[128,1536]{1,0:T(8,128)(2,1)S(1)} %collective-permute-done.4.refs_9_) | copy-start | bytes 1179652
  59.8 32.5 %collective-permute-start.7 = (bf16[256,1536]{1,0:T(8,128)(2,1)S(1)}, bf16[256,1536]{1,0:T(8,128)(2,1)S(1)}, u32[]{:S(2)}, u32[]{:S(2)}) collective-permute-start(bf16[256,1536]{1,0:T(8,128)(2,1)S(1)} %pad_maximum_fusion.refs_1_), channel_id=1, source_target_pairs={{0,96},{32,0},{64,32},{96,64},{1,97},{33,1},{65,33},{97,65},{2,98}... | collective-permute-start | bytes 2359304 | tf_op jit(solution)/shard_map/ppermute | solution.py:165
  64.2 28.1 %collective-permute-start.8 = (bf16[256,1536]{1,0:T(8,128)(2,1)S(1)}, bf16[256,1536]{1,0:T(8,128)(2,1)S(1)}, u32[]{:S(2)}, u32[]{:S(2)}) collective-permute-start(bf16[256,1536]{1,0:T(8,128)(2,1)S(1)} %pad_maximum_fusion.refs_1_), channel_id=1, source_target_pairs={{0,64},{32,96},{64,0},{96,32},{1,65},{33,97},{65,1},{97,33},{2,66}... | collective-permute-start | bytes 2359304 | tf_op jit(solution)/shard_map/ppermute | solution.py:165
  66.7 37.4 %collective-permute-start.9 = (bf16[256,1536]{1,0:T(8,128)(2,1)S(1)}, bf16[256,1536]{1,0:T(8,128)(2,1)S(1)}, u32[]{:S(2)}, u32[]{:S(2)}) collective-permute-start(bf16[256,1536]{1,0:T(8,128)(2,1)S(1)} %pad_maximum_fusion.refs_1_), channel_id=1, source_target_pairs={{0,32},{32,64},{64,96},{96,0},{1,33},{33,65},{65,97},{97,1},{2,34}... | collective-permute-start | bytes 2359304 | tf_op jit(solution)/shard_map/ppermute | solution.py:165
  69.2 23.1 %collective-permute-start.5 = (bf16[64,1536]{1,0:T(8,128)(2,1)S(1)}, bf16[64,1536]{1,0:T(8,128)(2,1)S(1)}, u32[]{:S(2)}, u32[]{:S(2)}) collective-permute-start(bf16[64,1536]{1,0:T(8,128)(2,1)S(1)} %slice.8), channel_id=1, source_target_pairs={{0,8},{8,16},{16,24},{24,0},{1,9},{9,17},{17,25},{25,1},{2,10},{10... | collective-permute-start | bytes 589832 | tf_op jit(solution)/shard_map/ppermute | solution.py:165
  76.1 16.2 %collective-permute-start.6 = (bf16[64,1536]{1,0:T(8,128)(2,1)S(1)}, bf16[64,1536]{1,0:T(8,128)(2,1)S(1)}, u32[]{:S(2)}, u32[]{:S(2)}) collective-permute-start(bf16[64,1536]{1,0:T(8,128)(2,1)S(1)} %slice.9), channel_id=1, source_target_pairs={{0,24},{8,0},{16,8},{24,16},{1,25},{9,1},{17,9},{25,17},{2,26},{10... | collective-permute-start | bytes 589832 | tf_op jit(solution)/shard_map/ppermute | solution.py:165
  92.3 36.7 %copy-start.3 = (bf16[256,1536]{1,0:T(8,128)(2,1)}, bf16[256,1536]{1,0:T(8,128)(2,1)S(1)}, u32[]{:S(2)}) copy-start(bf16[256,1536]{1,0:T(8,128)(2,1)S(1)} %collective-permute-done.7.refs_4_) | copy-start | bytes 2359300
  92.3 36.7 %copy-start.4 = (bf16[256,1536]{1,0:T(8,128)(2,1)}, bf16[256,1536]{1,0:T(8,128)(2,1)S(1)}, u32[]{:S(2)}) copy-start(bf16[256,1536]{1,0:T(8,128)(2,1)S(1)} %collective-permute-done.8.refs_7_) | copy-start | bytes 2359300
  104.1 25.0 %copy-start.5 = (bf16[256,1536]{1,0:T(8,128)(2,1)}, bf16[256,1536]{1,0:T(8,128)(2,1)S(1)}, u32[]{:S(2)}) copy-start(bf16[256,1536]{1,0:T(8,128)(2,1)S(1)} %collective-permute-done.9.refs_10_) | copy-start | bytes 2359300
  104.1 25.0 %copy-start.2 = (bf16[128,1536]{1,0:T(8,128)(2,1)}, bf16[128,1536]{1,0:T(8,128)(2,1)S(1)}, u32[]{:S(2)}) copy-start(bf16[128,1536]{1,0:T(8,128)(2,1)S(1)} %constant_dynamic-update-slice_fusion.refs_2_) | copy-start | bytes 1179652
  104.1 12.3 %collective-permute-start.10 = (bf16[128,1536]{1,0:T(8,128)(2,1)S(1)}, bf16[128,1536]{1,0:T(8,128)(2,1)S(1)}, u32[]{:S(2)}, u32[]{:S(2)}) collective-permute-start(bf16[128,1536]{1,0:T(8,128)(2,1)S(1)} %constant_dynamic-update-slice_fusion.refs_2_), channel_id=1, source_target_pairs={{0,96},{32,0},{64,32},{96,64},{1,97},{33,1},{65,33},{97,65},{2,98}... | collective-permute-start | bytes 1179656 | tf_op jit(solution)/shard_map/ppermute | solution.py:165
  106.0 13.1 %collective-permute-start.11 = (bf16[128,1536]{1,0:T(8,128)(2,1)S(1)}, bf16[128,1536]{1,0:T(8,128)(2,1)S(1)}, u32[]{:S(2)}, u32[]{:S(2)}) collective-permute-start(bf16[128,1536]{1,0:T(8,128)(2,1)S(1)} %constant_dynamic-update-slice_fusion.refs_2_), channel_id=1, source_target_pairs={{0,64},{32,96},{64,0},{96,32},{1,65},{33,97},{65,1},{97,33},{2,66}... | collective-permute-start | bytes 1179656 | tf_op jit(solution)/shard_map/ppermute | solution.py:165
  108.5 20.5 %collective-permute-start.12 = (bf16[128,1536]{1,0:T(8,128)(2,1)S(1)}, bf16[128,1536]{1,0:T(8,128)(2,1)S(1)}, u32[]{:S(2)}, u32[]{:S(2)}) collective-permute-start(bf16[128,1536]{1,0:T(8,128)(2,1)S(1)} %constant_dynamic-update-slice_fusion.refs_2_), channel_id=1, source_target_pairs={{0,32},{32,64},{64,96},{96,0},{1,33},{33,65},{65,97},{97,1},{2,34}... | collective-permute-start | bytes 1179656 | tf_op jit(solution)/shard_map/ppermute | solution.py:165
  116.4 12.7 %copy-start.9 = (bf16[128,1536]{1,0:T(8,128)(2,1)}, bf16[128,1536]{1,0:T(8,128)(2,1)S(1)}, u32[]{:S(2)}) copy-start(bf16[128,1536]{1,0:T(8,128)(2,1)S(1)} %collective-permute-done.10.refs_5_) | copy-start | bytes 1179652
  119.1 10.0 %copy-start.10 = (bf16[128,1536]{1,0:T(8,128)(2,1)}, bf16[128,1536]{1,0:T(8,128)(2,1)S(1)}, u32[]{:S(2)}) copy-start(bf16[128,1536]{1,0:T(8,128)(2,1)S(1)} %collective-permute-done.11.refs_8_) | copy-start | bytes 1179652
  129.1 0.7 copy-start.11
  151.1 4.8 %collective-permute-start.13 = (bf16[4,96,1536]{2,1,0:T(8,128)(2,1)S(1)}, bf16[4,96,1536]{2,1,0:T(8,128)(2,1)S(1)}, u32[]{:S(2)}, u32[]{:S(2)}) collective-permute-start(bf16[4,96,1536]{2,1,0:T(8,128)(2,1)S(1)} %get-tuple-element.36), channel_id=1, source_target_pairs={{0,1},{1,0},{2,3},{3,2},{4,5},{5,4},{6,7},{7,6},{8,9},{9,8},{10,11... | collective-permute-start | bytes 3538952 | tf_op jit(solution)/shard_map/ppermute | solution.py:192
  156.7 11.6 %collective-permute-start.14 = (bf16[96,1536]{1,0:T(8,128)(2,1)S(1)}, bf16[96,1536]{1,0:T(8,128)(2,1)S(1)}, u32[]{:S(2)}, u32[]{:S(2)}) collective-permute-start(bf16[96,1536]{1,0:T(8,128)(2,1)S(1)} %get-tuple-element.38), channel_id=1, source_target_pairs={{0,4},{2,6},{4,0},{6,2},{1,5},{3,7},{5,1},{7,3},{8,12},{10,14},{12... | collective-permute-start | bytes 884744 | tf_op jit(solution)/shard_map/ppermute | solution.py:165
  161.6 13.5 %collective-permute-start.15 = (bf16[96,1536]{1,0:T(8,128)(2,1)S(1)}, bf16[96,1536]{1,0:T(8,128)(2,1)S(1)}, u32[]{:S(2)}, u32[]{:S(2)}) collective-permute-start(bf16[96,1536]{1,0:T(8,128)(2,1)S(1)} %get-tuple-element.39), channel_id=1, source_target_pairs={{0,6},{2,0},{4,2},{6,4},{1,7},{3,1},{5,3},{7,5},{8,14},{10,8},{12,... | collective-permute-start | bytes 884744 | tf_op jit(solution)/shard_map/ppermute | solution.py:165
  164.3 10.8 %collective-permute-start.16 = (bf16[96,1536]{1,0:T(8,128)(2,1)S(1)}, bf16[96,1536]{1,0:T(8,128)(2,1)S(1)}, u32[]{:S(2)}, u32[]{:S(2)}) collective-permute-start(bf16[96,1536]{1,0:T(8,128)(2,1)S(1)} %get-tuple-element.40), channel_id=1, source_target_pairs={{0,2},{2,4},{4,6},{6,0},{1,3},{3,5},{5,7},{7,1},{8,10},{10,12},{12... | collective-permute-start | bytes 884744 | tf_op jit(solution)/shard_map/ppermute | solution.py:165
Sparse Core Ops, SparseCore 0:
  60.0 83.4 all-gather.2
